TPU v7x, 32 devices: a whole 2x2x4 slice. The times are simulated.
32 devices in a mesh: dp: 16 (over z, y, core), section: 2 (over x).
Axes of the slice: x: 2, y: 2, z: 4, core: 2. Of those that a mesh axis runs over, the one named last changes fastest.
Arguments:
- inputs: bfloat16 [32, 512, 1024], P('dp', None, 'section'), may hold values from -6 to 6
- cotangent: bfloat16 [32, 512, 1024], P('dp', None, 'section'), may hold values from -6 to 6
- memory: bfloat16 [2, 32, 512, 1024], P('section', 'dp'), may hold values from -6 to 6
- compressed: bfloat16 [2, 32, 512, 1024], P('section', 'dp'), may hold values from -6 to 6
- reset_flags: int32 [32], P('dp'), may hold values 0 or 1
- boundary: int32 [32], P('dp'), may hold values from 1 to 512
- gain_attn: bfloat16 [2, 1024], P('section'), may hold values from 0.5 to 1.5
- projection_weight: bfloat16 [2, 1024, 3072], P('section'), may hold values from -0.1875 to 0.1875
- w_output: bfloat16 [2, 1024, 1024], P('section'), may hold values from -1 to 1
- gain_ffn: bfloat16 [2, 1024], P('section'), may hold values from 0.5 to 1.5
- w_up: bfloat16 [2, 1024, 4096], P('section'), may hold values from -0.1875 to 0.1875
- b_up: bfloat16 [2, 4096], P('section'), may hold values from -3 to 3
- w_down: bfloat16 [2, 4096, 1024], P('section'), may hold values from -0.09375 to 0.09375
- b_down: bfloat16 [2, 1024], P('section'), may hold values from -2 to 2
- w_compress: bfloat16 [2, 2, 1024, 1024], P('section'), may hold values from -0.125 to 0.125
- b_compress: bfloat16 [2, 1024], P('section'), may hold values from -2 to 2
Outputs:
- outputs: bfloat16 [32, 512, 1024], P('dp', None, 'section')
- grad_inputs: bfloat16 [32, 512, 1024], P('dp', None, 'section')
- new_memory: bfloat16 [2, 32, 512, 1024], P('section', 'dp')
- new_compressed: bfloat16 [2, 32, 512, 1024], P('section', 'dp')
- grad_gain_attn: float32 [2, 1024], P('section', 'dp')
- grad_w_project: float32 [2, 1024, 3072], P('section', 'dp')
- grad_w_output: float32 [2, 1024, 1024], P('section', 'dp')
- grad_gain_ffn: float32 [2, 1024], P('section', 'dp')
- grad_w_up: float32 [2, 1024, 4096], P('section', 'dp')
- grad_b_up: float32 [2, 4096], P('section', 'dp')
- grad_w_down: float32 [2, 4096, 1024], P('section', 'dp')
- grad_b_down: float32 [2, 1024], P('section', 'dp')
All inputs are finite; a program needn't handle non-finite values. No bound on the sum of `reset_flags` on one device may be relied on, other than what follows from the above.
Results may differ from a plain program's by a relative error of at most 0.024.
Values may be sent and summed in bfloat16 or wider, within the bound.
No kernel may reach another device: no remote copies, remote signals or barrier semaphores. Data moves between devices by JAX's collectives and lax.ppermute only.
A program may use at most 448 MiB of HBM per device.

v0:
```python
import jax
import jax.numpy as jnp
from jax import lax
from jax.sharding import PartitionSpec as P

MODEL_WIDTH = 1024
HEADS = 8
HEAD = 128
SEG = 512
MEM = 512
CMEM = 512
RATE = 2
MB = 2
COMP = 256


EPS = 1e-05
NEG = -1e30
ROOT_TWO_PI = 0.7978845608028654


def from_partner(block, axis, bit):
    count = lax.axis_size(axis)
    route = []
    for low in range(count):
        high = low | 1 << bit
        if high != low and high < count:
            route += [(low, high), (high, low)]
    return lax.ppermute(block, axis, route)


def passed_along(value, axis, by):
    size = lax.axis_size(axis)
    pairs = [(i, i + by) for i in range(size) if 0 <= i + by < size]
    return lax.ppermute(value, axis, pairs)


def layer_norm(values, scale_gain):
    centred = values - jnp.mean(values, axis=-1, keepdims=True)
    spread = jnp.mean(centred * centred, axis=-1, keepdims=True)
    return centred * lax.rsqrt(spread + EPS) * scale_gain


def gaussian_unit(values):
    return (
        0.5
        * values
        * (1.0 + jnp.tanh(ROOT_TWO_PI * (values + 0.044715 * values * values * values)))
    )


def visible_mask(reset_rows, bounds):
    query_pos = lax.broadcasted_iota(jnp.int32, (1, SEG, 1), 1)
    key_pos = lax.broadcasted_iota(jnp.int32, (1, 1, SEG), 2)
    limit = bounds[:, None, None]
    after_bound = query_pos >= limit
    segment_keys = (key_pos <= query_pos) & ((key_pos >= limit) == after_bound)
    memory_keys = (reset_rows[:, None, None] == 0) & (query_pos < limit)
    memory_keys = jnp.broadcast_to(memory_keys, (reset_rows.shape[0], SEG, CMEM + MEM))
    return jnp.concatenate([memory_keys, segment_keys], axis=2)


def batch_portions(batch_index, count, memory_rows, condensed_rows, reset_flags, boundary):
    start = batch_index * count
    return tuple(
        (
            lax.dynamic_slice_in_dim(member, start, count, 0)
            for member in (memory_rows, condensed_rows, reset_flags, boundary)
        )
    )


def forward_layer(inputs, memory_rows, condensed_rows, reset_rows, bounds, params):
    gain_attn, projection_weight, w_output, gain_ffn, w_up, b_up, w_down, b_down = params
    keep_rows = (1 - reset_rows).astype(jnp.bfloat16)[:, None, None]
    context = jnp.concatenate([condensed_rows * keep_rows, memory_rows * keep_rows, inputs], axis=1)
    batch_size = inputs.shape[0]
    key_span = context.shape[1]
    normalized_rows = layer_norm(context.astype(jnp.float32), gain_attn.astype(jnp.float32)).astype(
        jnp.bfloat16
    )
    queries = jnp.einsum(
        "bsd,de->bse",
        normalized_rows[:, key_span - SEG :],
        projection_weight[:, :MODEL_WIDTH],
        preferred_element_type=jnp.float32,
    ).astype(jnp.bfloat16)
    keyvals = jnp.einsum(
        "aim,mo->aio",
        normalized_rows,
        projection_weight[:, MODEL_WIDTH:],
        preferred_element_type=jnp.float32,
    ).astype(jnp.bfloat16)
    head_queries = queries.reshape(batch_size, SEG, HEADS, HEAD)
    key_rows = keyvals[:, :, :MODEL_WIDTH].reshape(batch_size, key_span, HEADS, HEAD)
    value_rows = keyvals[:, :, MODEL_WIDTH:].reshape(batch_size, key_span, HEADS, HEAD)
    allowed = visible_mask(reset_rows, bounds)[:, None]
    attention_logits = jnp.einsum(
        "bqhd,bkhd->bhqk", head_queries, key_rows, preferred_element_type=jnp.float32
    ) * HEAD ** (-0.5)
    attention_logits = jnp.where(allowed, attention_logits, NEG)
    row_max = jnp.max(attention_logits, axis=-1, keepdims=True)
    exponent = jnp.exp(attention_logits - row_max)
    denominator = jnp.sum(exponent, axis=-1, keepdims=True)
    attention = (exponent / denominator).astype(jnp.bfloat16)
    log_total = row_max + jnp.log(denominator)
    attended = jnp.einsum(
        "bhqk,bkhd->bqhd", attention, value_rows, preferred_element_type=jnp.float32
    )
    attended = attended.reshape(batch_size, SEG, MODEL_WIDTH).astype(jnp.bfloat16)
    residual = inputs.astype(jnp.float32) + jnp.einsum(
        "bsd,de->bse", attended, w_output, preferred_element_type=jnp.float32
    )
    ffn_in = layer_norm(residual, gain_ffn.astype(jnp.float32)).astype(jnp.bfloat16)
    hidden_in = jnp.einsum(
        "bsd,df->bsf", ffn_in, w_up, preferred_element_type=jnp.float32
    ) + b_up.astype(jnp.float32)
    hidden = gaussian_unit(hidden_in).astype(jnp.bfloat16)
    output = residual + (
        jnp.einsum("bsf,fd->bsd", hidden, w_down, preferred_element_type=jnp.float32)
        + b_down.astype(jnp.float32)
    )
    saved_rows = (
        context,
        normalized_rows,
        head_queries,
        key_rows,
        value_rows,
        log_total,
        attended,
        residual,
        ffn_in,
        hidden_in,
        hidden,
        allowed,
    )
    return (output, saved_rows)


def backward_ffn(grad_low, saved_rows, params):
    gain_attn, projection_weight, w_output, gain_ffn, w_up, b_up, w_down, b_down = params
    residual, ffn_in, hidden_in, hidden = (
        saved_rows[7],
        saved_rows[8],
        saved_rows[9],
        saved_rows[10],
    )
    grad_y = grad_low.astype(jnp.float32)
    d_b_down = jnp.sum(grad_y, axis=(0, 1))
    d_w_down = jnp.einsum("bsf,bsd->fd", hidden, grad_low, preferred_element_type=jnp.float32)
    d_hidden = jnp.einsum("bsd,fd->bsf", grad_low, w_down, preferred_element_type=jnp.float32)
    unused, gate_back = jax.vjp(gaussian_unit, hidden_in)
    d_hidden_in = gate_back(d_hidden)[0].astype(jnp.bfloat16)
    d_b_up = jnp.sum(d_hidden_in.astype(jnp.float32), axis=(0, 1))
    d_w_up = jnp.einsum("bsd,bsf->df", ffn_in, d_hidden_in, preferred_element_type=jnp.float32)
    d_ffn_in = jnp.einsum("bsf,df->bsd", d_hidden_in, w_up, preferred_element_type=jnp.float32)
    unused_norm, norm_back = jax.vjp(layer_norm, residual, gain_ffn.astype(jnp.float32))
    d_through, d_gain_ffn = norm_back(d_ffn_in)
    return (grad_y + d_through, (d_gain_ffn, d_w_up, d_b_up, d_w_down, d_b_down))


def backward_attention(d_residual, saved_rows, params):
    gain_attn, projection_weight, w_output, gain_ffn, w_up, b_up, w_down, b_down = params
    context, normalized_rows, head_queries, key_rows, value_rows, log_total, attended = saved_rows[
        :7
    ]
    allowed = saved_rows[11]
    batch_size = context.shape[0]
    key_span = context.shape[1]
    grad_attn = d_residual.astype(jnp.bfloat16)
    d_w_output = jnp.einsum("bsd,bse->de", attended, grad_attn, preferred_element_type=jnp.float32)
    d_attended = jnp.einsum("bse,de->bsd", grad_attn, w_output, preferred_element_type=jnp.float32)
    d_attended = d_attended.astype(jnp.bfloat16).reshape(batch_size, SEG, HEADS, HEAD)
    attention_logits = jnp.einsum(
        "bqhd,bkhd->bhqk", head_queries, key_rows, preferred_element_type=jnp.float32
    ) * HEAD ** (-0.5)
    attention_logits = jnp.where(allowed, attention_logits, NEG)
    attention = jnp.exp(attention_logits - log_total)
    d_values = jnp.einsum(
        "bhqk,bqhd->bkhd",
        attention.astype(jnp.bfloat16),
        d_attended,
        preferred_element_type=jnp.float32,
    ).astype(jnp.bfloat16)
    d_attention = jnp.einsum(
        "bqhd,bkhd->bhqk", d_attended, value_rows, preferred_element_type=jnp.float32
    )
    inner_sum = jnp.sum(attention * d_attention, axis=-1, keepdims=True)
    d_scores = (attention * (d_attention - inner_sum)).astype(jnp.bfloat16)
    d_queries = jnp.einsum(
        "bhqk,bkhd->bqhd", d_scores, key_rows, preferred_element_type=jnp.float32
    ) * HEAD ** (-0.5)
    d_queries = d_queries.astype(jnp.bfloat16).reshape(batch_size, SEG, MODEL_WIDTH)
    d_keys = jnp.einsum(
        "bhqk,bqhd->bkhd", d_scores, head_queries, preferred_element_type=jnp.float32
    ) * HEAD ** (-0.5)
    d_keys = d_keys.astype(jnp.bfloat16).reshape(batch_size, key_span, MODEL_WIDTH)
    grad_key_value_rows = jnp.concatenate(
        [d_keys, d_values.reshape(batch_size, key_span, MODEL_WIDTH)], axis=2
    )
    query_rows = normalized_rows[:, key_span - SEG :]
    d_w_project = jnp.concatenate(
        [
            jnp.einsum("bsd,bse->de", query_rows, d_queries, preferred_element_type=jnp.float32),
            jnp.einsum(
                "iuc,iun->cn",
                normalized_rows,
                grad_key_value_rows,
                preferred_element_type=jnp.float32,
            ),
        ],
        axis=1,
    )
    d_normed = jnp.einsum(
        "mlg,jg->mlj",
        grad_key_value_rows,
        projection_weight[:, MODEL_WIDTH:],
        preferred_element_type=jnp.float32,
    )
    d_from_queries = jnp.einsum(
        "bse,de->bsd",
        d_queries,
        projection_weight[:, :MODEL_WIDTH],
        preferred_element_type=jnp.float32,
    )
    d_normed = jnp.concatenate(
        [d_normed[:, : key_span - SEG], d_normed[:, key_span - SEG :] + d_from_queries], axis=1
    )
    unused, context_back = jax.vjp(
        layer_norm, context.astype(jnp.float32), gain_attn.astype(jnp.float32)
    )
    d_context, d_gain_attn = context_back(d_normed)
    return (d_residual + d_context[:, key_span - SEG :], (d_gain_attn, d_w_project, d_w_output))


def body(
    inputs,
    cotangent,
    memory,
    compressed,
    reset_flags,
    boundary,
    gain_attn,
    projection_weight,
    w_output,
    gain_ffn,
    w_up,
    b_up,
    w_down,
    b_down,
    w_compress,
    b_compress,
):
    section_index = lax.axis_index("section")
    is_first = section_index == 0
    params = tuple(
        (
            member[0]
            for member in (
                gain_attn,
                projection_weight,
                w_output,
                gain_ffn,
                w_up,
                b_up,
                w_down,
                b_down,
            )
        )
    )
    memory_rows = memory[0]
    condensed_rows = compressed[0]
    streams_each = inputs.shape[0] // MB
    half_width = inputs.shape[2]
    incoming = from_partner(jnp.where(is_first, cotangent, inputs), "section", 0)
    first_inputs = jnp.concatenate([inputs, incoming], axis=2)
    last_cotangent = jnp.concatenate([incoming, cotangent], axis=2)
    arrived = jnp.zeros((streams_each, SEG, MODEL_WIDTH), jnp.bfloat16)
    layer_inputs = []
    layer_outputs = []
    saved_list = []
    for moment in range(MB + 1):
        if moment < MB:
            fresh_rows = first_inputs[moment * streams_each : (moment + 1) * streams_each]
        else:
            fresh_rows = jnp.zeros_like(arrived)
        current = jnp.where(is_first, fresh_rows, arrived)
        batch_index = jnp.clip(moment - section_index, 0, MB - 1)
        pieces = batch_portions(
            batch_index, streams_each, memory_rows, condensed_rows, reset_flags, boundary
        )
        output, saved_rows = forward_layer(
            current, pieces[0], pieces[1], pieces[2], pieces[3], params
        )
        sent_rows = output.astype(jnp.bfloat16)
        if moment < MB:
            arrived = passed_along(sent_rows, "section", 1)
        layer_inputs.append(current)
        layer_outputs.append(sent_rows)
        saved_list.append(saved_rows)
    grad_arrived = jnp.zeros((streams_each, SEG, MODEL_WIDTH), jnp.bfloat16)
    input_grads = []
    ffn_total = None
    attn_total = None
    for reverse_step in range(MB + 1):
        moment = MB - reverse_step
        if reverse_step < MB:
            from_cotangent = last_cotangent[
                (MB - 1 - reverse_step) * streams_each : (MB - reverse_step) * streams_each
            ]
        else:
            from_cotangent = jnp.zeros_like(grad_arrived)
        grad_now = jnp.where(is_first, grad_arrived, from_cotangent)
        offset = moment - section_index
        is_valid = (offset >= 0) & (offset < MB)
        batch_index = jnp.clip(offset, 0, MB - 1)
        saved_rows = saved_list[moment]
        d_residual, ffn_grads = backward_ffn(grad_now, saved_rows, params)
        ffn_grads = tuple((jnp.where(is_valid, member, 0.0) for member in ffn_grads))
        if ffn_total is None:
            ffn_total = ffn_grads
        else:
            ffn_total = tuple((earlier + latest for earlier, latest in zip(ffn_total, ffn_grads)))
        d_inputs, attn_grads = backward_attention(d_residual, saved_rows, params)
        attn_grads = tuple((jnp.where(is_valid, member, 0.0) for member in attn_grads))
        if attn_total is None:
            attn_total = attn_grads
        else:
            attn_total = tuple(
                (earlier + latest for earlier, latest in zip(attn_total, attn_grads))
            )
        grad_low = d_inputs.astype(jnp.bfloat16)
        if reverse_step < MB:
            grad_arrived = passed_along(grad_low, "section", -1)
        input_grads.append(grad_low)
    gradients = (
        lax.psum_scatter(attn_total[0], "dp", scatter_dimension=0, tiled=True),
        lax.psum_scatter(attn_total[1], "dp", scatter_dimension=0, tiled=True),
        lax.psum_scatter(attn_total[2], "dp", scatter_dimension=0, tiled=True),
        lax.psum_scatter(ffn_total[0], "dp", scatter_dimension=0, tiled=True),
        lax.psum_scatter(ffn_total[1], "dp", scatter_dimension=0, tiled=True),
        lax.psum_scatter(ffn_total[2], "dp", scatter_dimension=0, tiled=True),
        lax.psum_scatter(ffn_total[3], "dp", scatter_dimension=0, tiled=True),
        lax.psum_scatter(ffn_total[4], "dp", scatter_dimension=0, tiled=True),
    )
    final_rows = jnp.concatenate(layer_outputs[1:], axis=0)
    input_rows = jnp.concatenate(
        [input_grads[MB - batch_number] for batch_number in range(MB)], axis=0
    )
    new_memory = jnp.where(
        is_first,
        jnp.concatenate(layer_inputs[:MB], axis=0),
        jnp.concatenate(layer_inputs[1:], axis=0),
    )
    keep_all = (1 - reset_flags).astype(jnp.bfloat16)[:, None, None]
    evicted = memory_rows * keep_all
    grouped = evicted.reshape(evicted.shape[0], COMP, RATE * MODEL_WIDTH)
    squeezed = jnp.einsum(
        "bcr,rd->bcd",
        grouped,
        w_compress[0].reshape(RATE * MODEL_WIDTH, MODEL_WIDTH),
        preferred_element_type=jnp.float32,
    ) + b_compress[0].astype(jnp.float32)
    joined = jnp.concatenate([condensed_rows * keep_all, squeezed.astype(jnp.bfloat16)], axis=1)
    new_compressed = joined[:, COMP:]
    leaving = jnp.where(is_first, input_rows[:, :, half_width:], final_rows[:, :, :half_width])
    returned = from_partner(leaving, "section", 0)
    out_rows = jnp.where(is_first, returned, final_rows[:, :, half_width:])
    out_grads = jnp.where(is_first, input_rows[:, :, :half_width], returned)
    return (
        out_rows,
        out_grads,
        new_memory[None],
        new_compressed[None],
        gradients[0][None],
        gradients[1][None],
        gradients[2][None],
        gradients[3][None],
        gradients[4][None],
        gradients[5][None],
        gradients[6][None],
        gradients[7][None],
    )


def solution(mesh):
    return jax.shard_map(
        body,
        mesh=mesh,
        in_specs=(
            P("dp", None, "section"),
            P("dp", None, "section"),
            P("section", "dp", None, None),
            P("section", "dp", None, None),
            P("dp"),
            P("dp"),
            P("section", None),
            P("section", None, None),
            P("section", None, None),
            P("section", None),
            P("section", None, None),
            P("section", None),
            P("section", None, None),
            P("section", None),
            P("section", None, None, None),
            P("section", None),
        ),
        out_specs=(
            P("dp", None, "section"),
            P("dp", None, "section"),
            P("section", "dp", None, None),
            P("section", "dp", None, None),
            P("section", "dp"),
            P("section", "dp", None),
            P("section", "dp", None),
            P("section", "dp"),
            P("section", "dp", None),
            P("section", "dp"),
            P("section", "dp", None),
            P("section", "dp"),
        ),
        check_vma=False,
    )
```

profile of v0, /device:TPU:26, one launch (start us, length us, event | category | flops | bytes accessed | tf_op | source)
XLA Modules:
  0.0 1344.9 jit_solution(13828346065833481297)
XLA Ops:
  96.7 13.0 fusion.162
  112.8 18.1 %fusion.60 = f32[512,4096]{1,0:T(8,128)S(1)} fusion(bf16[1,1024,4096]{2,1,0:T(8,128)(2,1)} %param.26, f32[1,512,1024]{2,1,0:T(8,128)S(1)} %get-tuple-element.47, f32[1024]{0:T(1024)S(1)} %bitcast.496, f32[512]{0:T(512)S(1)} %fusion.240, f32[512]{0:T(512)S(1)} %broadcast_multiply_fusion.6), kind=kOutput, calls=%fused_computation.95 | convolution fusion | flops 4297064448 | bytes 18882560 | tf_op jit(solution)/shard_map/bsd,df->bsf/dot_general | solution.py:115
  141.9 20.8 %collective-permute-done.1 = bf16[1,512,1024]{2,1,0:T(8,128)(2,1)} collective-permute-done((bf16[1,512,1024]{2,1,0:T(8,128)(2,1)S(1)}, bf16[1,512,1024]{2,1,0:T(8,128)(2,1)}, u32[]{:S(2)}, u32[]{:S(2)}) %collective-permute-start.1) | collective-permute-done | bytes 1048608 | tf_op jit(solution)/shard_map/ppermute | solution.py:35
  204.0 11.5 fusion.273
  226.8 13.0 fusion.159
  260.7 20.9 %collective-permute-done.2 = bf16[1,512,1024]{2,1,0:T(8,128)(2,1)S(1)} collective-permute-done((bf16[1,512,1024]{2,1,0:T(8,128)(2,1)S(1)}, bf16[1,512,1024]{2,1,0:T(8,128)(2,1)S(1)}, u32[]{:S(2)}, u32[]{:S(2)}) %collective-permute-start.2) | collective-permute-done | bytes 1048608 | tf_op jit(solution)/shard_map/ppermute | solution.py:35
  314.9 15.5 %fusion.274 = (f32[8,512]{1,0:T(8,128)S(1)}, f32[8,512,1536]{2,1,0:T(8,128)}) fusion(bf16[512,8,128]{0,2,1:T(8,128)(2,1)} %bitcast.442, bf16[1536,8,128]{0,2,1:T(8,128)(2,1)} %bitcast.430, pred[512,1536]{1,0:T(8,128)(4,1)} %add_bitcast_fusion.2), kind=kOutput, calls=%fused_computation.416 | convolution fusion | flops 1629483008 | bytes 30162944 | tf_op jit(solution)/shard_map/bqhd,bkhd->bhqk/dot_general | solution.py:98
  344.3 13.0 fusion.156
  371.2 16.6 %convert_reduce_fusion.2 = (f32[4096]{0:T(1024)}, bf16[512,4096]{1,0:T(8,128)(2,1)}) fusion(bf16[1,4096,1024]{2,1,0:T(8,128)(2,1)} %param.28, bf16[2,512,1024]{2,1,0:T(8,128)(2,1)S(1)} %copy-done.57, pred[]{:T(512)S(6)} %eq.78, f32[512,4096]{1,0:T(8,128)} %fusion.56, f32[4096]{0:T(1024)S(1)} %bitcast.510), kind=kOutput, calls=%fused_computation.99 | convolution fusion | flops 4352110592 | bytes 22052864 | tf_op jit(solution)/shard_map/bsd,fd->bsf/dot_general | solution.py:151
  403.7 24.9 %multiply_reduce_fusion.2 = (f32[8,512]{1,0:T(8,128)S(1)}, f32[8,512,1536]{2,1,0:T(8,128)}) fusion(f32[8,512,1536]{2,1,0:T(8,128)} %get-tuple-element.87, f32[8,512]{1,0:T(8,128)S(1)} %log_add_fusion.2, bf16[512,8,128]{0,2,1:T(8,128)(2,1)} %bitcast.450, bf16[1536,8,128]{2,1,0:T(8,128)(2,1)} %bitcast.437), kind=kOutput, calls=%fused_computation.7 | convolution fusion | flops 1629483008 | bytes 54558720 | tf_op jit(solution)/shard_map/bqhd,bkhd->bhqk/dot_general | solution.py:185
  428.6 12.2 fusion.86
  440.8 16.6 %multiply_convert_fusion.2 = bf16[8,512,1536]{2,1,0:T(8,128)(2,1)S(1)} fusion(f32[8,512,1536]{2,1,0:T(8,128)} %get-tuple-element.90, f32[8,512,1536]{2,1,0:T(8,128)} %get-tuple-element.87, f32[8,512]{1,0:T(8,128)S(1)} %get-tuple-element.89, f32[8,512]{1,0:T(8,128)S(1)} %log_add_fusion.2), kind=kLoop, calls=%fused_computation.6 | loop fusion | flops 25165824 | bytes 62947328 | tf_op jit(solution)/shard_map/convert_element_type | solution.py:189
  514.6 11.9 fusion.85
  535.5 15.7 %convert_reduce_fusion.1 = (f32[4096]{0:T(1024)}, bf16[512,4096]{1,0:T(8,128)(2,1)S(1)}) fusion(bf16[1,4096,1024]{2,1,0:T(8,128)(2,1)} %param.28, bf16[1,512,1024]{2,1,0:T(8,128)(2,1)S(1)} %get-tuple-element.29, f32[512,4096]{1,0:T(8,128)} %copy-done.163, f32[4096]{0:T(1024)S(1)} %bitcast.511), kind=kOutput, calls=%fused_computation.98 | convolution fusion | flops 4351586304 | bytes 22052864 | tf_op jit(solution)/shard_map/bsd,fd->bsf/dot_general | solution.py:151
  567.9 19.3 %multiply_reduce_fusion.1 = (f32[8,512]{1,0:T(8,128)S(1)}, f32[8,512,1536]{2,1,0:T(8,128)}) fusion(f32[8,512,1536]{2,1,0:T(8,128)} %get-tuple-element.85, f32[8,512]{1,0:T(8,128)S(1)} %copy-done.100, bf16[512,8,128]{0,2,1:T(8,128)(2,1)S(1)} %bitcast.452, bf16[1536,8,128]{2,1,0:T(8,128)(2,1)} %bitcast.435), kind=kOutput, calls=%fused_computation.4 | convolution fusion | flops 1629483008 | bytes 54558720 | tf_op jit(solution)/shard_map/bqhd,bkhd->bhqk/dot_general | solution.py:185
  587.3 12.7 fusion.89
  599.9 16.6 %multiply_convert_fusion.1 = bf16[8,512,1536]{2,1,0:T(8,128)(2,1)S(1)} fusion(f32[8,512,1536]{2,1,0:T(8,128)} %get-tuple-element.93, f32[8,512,1536]{2,1,0:T(8,128)} %get-tuple-element.85, f32[8,512]{1,0:T(8,128)S(1)} %get-tuple-element.92, f32[8,512]{1,0:T(8,128)S(1)} %copy-done.100), kind=kLoop, calls=%fused_computation.3 | loop fusion | flops 25165824 | bytes 62947328 | tf_op jit(solution)/shard_map/convert_element_type | solution.py:189
  674.3 13.1 fusion.84
  693.1 15.4 %convert_reduce_fusion = (f32[4096]{0:T(1024)}, bf16[512,4096]{1,0:T(8,128)(2,1)S(1)}) fusion(bf16[1,4096,1024]{2,1,0:T(8,128)(2,1)} %param.28, bf16[1,512,1024]{2,1,0:T(8,128)(2,1)S(1)} %collective-permute-done.4, pred[]{:T(512)S(6)} %eq.78, f32[512,4096]{1,0:T(8,128)} %copy-done.162, f32[4096]{0:T(1024)S(1)} %bitcast.512), kind=kOutput, calls=%fused_computation.97 | convolution fusion | flops 4352110592 | bytes 22052864 | tf_op jit(solution)/shard_map/bsd,fd->bsf/dot_general | solution.py:151
  729.5 19.8 %multiply_reduce_fusion = (f32[8,512]{1,0:T(8,128)S(1)}, f32[8,512,1536]{2,1,0:T(8,128)}) fusion(f32[8,512,1536]{2,1,0:T(8,128)} %get-tuple-element.83, f32[8,512]{1,0:T(8,128)S(1)} %copy-done.99, bf16[512,8,128]{0,2,1:T(8,128)(2,1)S(1)} %bitcast.448, bf16[1536,8,128]{2,1,0:T(8,128)(2,1)} %bitcast.433), kind=kOutput, calls=%fused_computation.1 | convolution fusion | flops 1629483008 | bytes 54558720 | tf_op jit(solution)/shard_map/bqhd,bkhd->bhqk/dot_general | solution.py:185
  749.3 22.6 %multiply_convert_fusion = bf16[8,512,1536]{2,1,0:T(8,128)(2,1)} fusion(f32[8,512,1536]{2,1,0:T(8,128)} %get-tuple-element.96, f32[8,512,1536]{2,1,0:T(8,128)} %get-tuple-element.83, f32[8,512]{1,0:T(8,128)S(1)} %get-tuple-element.95, f32[8,512]{1,0:T(8,128)S(1)} %copy-done.99), kind=kLoop, calls=%fused_computation | loop fusion | flops 25165824 | bytes 62947328 | tf_op jit(solution)/shard_map/convert_element_type | solution.py:189
  795.1 12.5 fusion.92
  807.7 14.3 %fusion.83 = f32[1024,2048]{1,0:T(8,128)} fusion(bf16[1,1536,1024]{1,2,0:T(8,128)(2,1)} %bitcast.468, bf16[1,1536,1024]{1,2,0:T(8,128)(2,1)} %bitcast.454, bf16[512,1024]{1,0:T(8,128)(2,1)} %copy-done.94, bf16[512,1024]{1,0:T(8,128)(2,1)} %copy-done.87, bf16[512,1024]{1,0:T(8,128)(2,1)S(1)} %copy-done.86, f32[1024]{0:T(1024)S(1)} %bitcast.489, ...), kind=kOutput, calls=%fused_computation.152 | convolution fusion | flops 6470762496 | bytes 17842176 | tf_op jit(solution)/shard_map/iuc,iun->cn/dot_general | solution.py:205
  821.9 16.3 %fusion.13 = f32[1024,3072]{1,0:T(8,128)} fusion(f32[1024,2048]{1,0:T(8,128)} %fusion.85, f32[1024,1024]{1,0:T(8,128)S(1)} %copy-done.25, f32[1024,2048]{1,0:T(8,128)} %fusion.84, f32[1024,1024]{1,0:T(8,128)S(1)} %copy-done.26, f32[1024,2048]{1,0:T(8,128)} %fusion.83, f32[1024,1024]{1,0:T(8,128)} %fusion.231, pred[]{:T(512)S(6)} %and.102, pred[]{:T(512)S(6)} %and.101, ...), kind=kLoop, calls=%fused_computation.31 | loop fusion | flops 25165824 | bytes 50331652 | tf_op jit(solution)/shard_map/add | solution.py:330
  838.6 18.4 %fusion.187 = f32[4096,1024]{1,0:T(8,128)} fusion(bf16[2,512,1024]{2,1,0:T(8,128)(2,1)} %copy-done.56, pred[]{:T(512)S(6)} %eq.78, f32[512,4096]{1,0:T(8,128)} %fusion.56, f32[4096]{0:T(1024)S(1)} %bitcast.513), kind=kOutput, calls=%fused_computation.297 | convolution fusion | flops 4316463104 | bytes 26230784 | tf_op jit(solution)/shard_map/bsf,bsd->fd/dot_general | solution.py:150
  857.0 16.9 %fusion.184 = f32[4096,1024]{1,0:T(8,128)} fusion(bf16[1,512,1024]{2,1,0:T(8,128)(2,1)S(1)} %copy-done.52, f32[512,4096]{1,0:T(8,128)} %copy-done.163, f32[4096]{0:T(1024)S(1)} %bitcast.514), kind=kOutput, calls=%fused_computation.294 | convolution fusion | flops 4315938816 | bytes 26230784 | tf_op jit(solution)/shard_map/bsf,bsd->fd/dot_general | solution.py:150
  873.9 25.7 %select_add_fusion = f32[4096,1024]{1,0:T(8,128)} fusion(f32[4096,1024]{1,0:T(8,128)} %fusion.184, f32[4096,1024]{1,0:T(8,128)} %fusion.187, pred[]{:T(512)S(6)} %and.102, pred[]{:T(512)S(6)} %and.101, pred[]{:T(512)S(6)} %and.100, bf16[1,512,1024]{2,1,0:T(8,128)(2,1)S(1)} %copy-done.73, pred[]{:T(512)S(6)} %eq.78, f32[512,4096]{1,0:T(8,128)} %copy-done.162, ...), kind=kOutput, calls=%fused_computation.24 | convolution fusion | flops 4337434624 | bytes 59785220 | tf_op jit(solution)/shard_map/bsf,bsd->fd/dot_general | solution.py:150
  900.3 13.6 %fusion.253 = f32[1024,4096]{1,0:T(8,128)} fusion(bf16[512,4096]{1,0:T(8,128)(2,1)} %get-tuple-element.102, f32[1,512,1024]{2,1,0:T(8,128)} %copy-done.30, f32[512]{0:T(512)S(1)} %copy-done.151, f32[512]{0:T(512)S(1)} %copy-done.135, f32[1024]{0:T(1024)S(1)} %bitcast.505), kind=kOutput, calls=%fused_computation.401 | convolution fusion | flops 4297064448 | bytes 23076864 | tf_op jit(solution)/shard_map/bsd,bsf->df/dot_general | solution.py:155
  922.7 25.0 %select_add_fusion.1 = f32[1024,4096]{1,0:T(8,128)} fusion(f32[1024,4096]{1,0:T(8,128)} %fusion.256, f32[1024,4096]{1,0:T(8,128)} %fusion.253, pred[]{:T(512)S(6)} %and.102, pred[]{:T(512)S(6)} %and.101, pred[]{:T(512)S(6)} %and.100, bf16[512,4096]{1,0:T(8,128)(2,1)} %copy-done.66, f32[1,512,1024]{2,1,0:T(8,128)} %copy-done.13, f32[1024]{0:T(1024)S(1)} %bitcast.507, ...), kind=kOutput, calls=%fused_computation.25 | convolution fusion | flops 4318035968 | bytes 56631300 | tf_op jit(solution)/shard_map/bsd,bsf->df/dot_general | solution.py:155
  1009.5 51.4 %all-reduce.4 = (f32[1024]{0:T(1024)S(1)}, f32[1024]{0:T(1024)S(1)}, f32[4096]{0:T(1024)S(1)}, f32[1024]{0:T(1024)S(1)}) all-reduce(f32[1024]{0:T(1024)S(1)} %select_add_fusion.6, f32[1024]{0:T(1024)S(1)} %select_add_fusion.5, f32[4096]{0:T(1024)S(1)} %select_add_fusion.3, ...), channel_id=2, replica_groups=mesh['dp'=16,'section'=2] {'dp'}, use_global_device_ids=true, to_apply=%region_36.37.clone | all-reduce | flops 7168 | bytes 57344
  1066.9 88.3 %reduce-scatter.11.cloned.1.call-done = f32[256,1024]{1,0:T(8,128)} async-done(((f32[4096,1024]{1,0:T(8,128)}), f32[256,1024]{1,0:T(8,128)}) %reduce-scatter.11.cloned.1.call-update) | async-done | bytes 1048592 | tf_op jit(solution)/shard_map/reduce_scatter | solution.py:343
  1155.2 182.7 %reduce-scatter.9.cloned.1.call-done = f32[64,4096]{1,0:T(8,128)} async-done(((f32[1024,4096]{1,0:T(8,128)}), f32[64,4096]{1,0:T(8,128)}) %reduce-scatter.9.cloned.1.call-update) | async-done | bytes 1048592 | tf_op jit(solution)/shard_map/reduce_scatter | solution.py:341
  (560 shorter events, 514.4 us)
Async XLA Ops:
  7.2 102.5 %copy-start = (bf16[1,1024,1024]{2,1,0:T(8,128)(2,1)S(1)}, bf16[1,1024,1024]{2,1,0:T(8,128)(2,1)}, u32[]{:S(2)}) copy-start(bf16[1,1024,1024]{2,1,0:T(8,128)(2,1)} %param.24) | copy-start | bytes 6291460
  7.2 1059.7 %reduce-scatter.7.cloned.1.call-start = ((), (), s32[]{:S(2)}) async-start(), calls=%async_computation.5 | async-start | bytes 4456448 | tf_op jit(solution)/shard_map/reduce_scatter | solution.py:339
  10.3 25.1 %collective-permute-start = (bf16[2,512,512]{2,1,0:T(8,128)(2,1)}, bf16[2,512,512]{2,1,0:T(8,128)(2,1)S(1)}, u32[]{:S(2)}, u32[]{:S(2)}) collective-permute-start(bf16[2,512,512]{2,1,0:T(8,128)(2,1)} %get-tuple-element.74), channel_id=1, source_target_pairs={{0,1},{1,0},{2,3},{3,2},{4,5},{5,4},{6,7},{7,6},{8,9},{9,8},{10,11... | collective-permute-start | bytes 3145736 | tf_op jit(solution)/shard_map/ppermute | solution.py:29
  15.1 292.6 %copy-start.82 = (f32[1,1024]{1,0:T(1,128)}, f32[1,1024]{1,0:T(1,128)S(1)}, u32[]{:S(2)}) copy-start(f32[1,1024]{1,0:T(1,128)S(1)} %convert_element_type.664) | copy-start | bytes 12292
  16.5 701.5 %copy-start.101 = (f32[1,1024]{1,0:T(1,128)}, f32[1,1024]{1,0:T(1,128)S(1)}, u32[]{:S(2)}) copy-start(f32[1,1024]{1,0:T(1,128)S(1)} %convert_element_type.665) | copy-start | bytes 12292
  17.9 232.7 %copy-start.154 = (f32[1,1024]{1,0:T(1,128)}, f32[1,1024]{1,0:T(1,128)S(1)}, u32[]{:S(2)}) copy-start(f32[1,1024]{1,0:T(1,128)S(1)} %convert_element_type.667) | copy-start | bytes 12292
  36.6 73.1 %copy-start.6 = (bf16[1,512,1024]{2,1,0:T(8,128)(2,1)}, bf16[1,512,1024]{2,1,0:T(8,128)(2,1)S(1)}, u32[]{:S(2)}) copy-start(bf16[1,512,1024]{2,1,0:T(8,128)(2,1)S(1)} %slice_select_fusion.1) | copy-start | bytes 3145732
  109.7 21.4 %slice-start.6 = ((s8[8388608]{0:T(1024)(128)(4,1)}), s8[4194304]{0:T(1024)(128)(4,1)S(1)}, s32[]{:S(2)}) async-start(s8[8388608]{0:T(1024)(128)(4,1)} %bitcast.524), calls=%async_computation.14 | async-start | bytes 8388608
  136.6 26.0 %collective-permute-start.1 = (bf16[1,512,1024]{2,1,0:T(8,128)(2,1)S(1)}, bf16[1,512,1024]{2,1,0:T(8,128)(2,1)}, u32[]{:S(2)}, u32[]{:S(2)}) collective-permute-start(bf16[1,512,1024]{2,1,0:T(8,128)(2,1)S(1)} %fusion.122), channel_id=1, source_target_pairs={{0,1},{2,3},{4,5},{6,7},{8,9},{10,11},{12,13},{14,15},{16,17},{18,... | collective-permute-start | bytes 3145736 | tf_op jit(solution)/shard_map/ppermute | solution.py:35
  164.3 75.5 %copy-start.3 = (bf16[1,512,1024]{2,1,0:T(8,128)(2,1)}, bf16[1,512,1024]{2,1,0:T(8,128)(2,1)S(1)}, u32[]{:S(2)}) copy-start(bf16[1,512,1024]{2,1,0:T(8,128)(2,1)S(1)} %slice_select_fusion.2) | copy-start | bytes 3145732
  256.3 29.0 %copy-start.75 = (bf16[1,512,1024]{2,1,0:T(8,128)(2,1)}, bf16[1,512,1024]{2,1,0:T(8,128)(2,1)S(1)}, u32[]{:S(2)}) copy-start(bf16[1,512,1024]{2,1,0:T(8,128)(2,1)S(1)} %fusion.121) | copy-start | bytes 3145732
  256.3 25.4 %copy-start.21 = (bf16[1,512,1024]{2,1,0:T(8,128)(2,1)S(1)}, bf16[1,512,1024]{2,1,0:T(8,128)(2,1)}, u32[]{:S(2)}) copy-start(bf16[1,512,1024]{2,1,0:T(8,128)(2,1)} %get-tuple-element.57) | copy-start | bytes 3145732
  256.3 25.4 %copy-start.23 = (bf16[1,512,1024]{2,1,0:T(8,128)(2,1)S(1)}, bf16[1,512,1024]{2,1,0:T(8,128)(2,1)}, u32[]{:S(2)}) copy-start(bf16[1,512,1024]{2,1,0:T(8,128)(2,1)} %get-tuple-element.107) | copy-start | bytes 3145732
  256.3 25.3 %collective-permute-start.2 = (bf16[1,512,1024]{2,1,0:T(8,128)(2,1)S(1)}, bf16[1,512,1024]{2,1,0:T(8,128)(2,1)S(1)}, u32[]{:S(2)}, u32[]{:S(2)}) collective-permute-start(bf16[1,512,1024]{2,1,0:T(8,128)(2,1)S(1)} %fusion.121), channel_id=1, source_target_pairs={{0,1},{2,3},{4,5},{6,7},{8,9},{10,11},{12,13},{14,15},{16,17},{18,... | collective-permute-start | bytes 3145736 | tf_op jit(solution)/shard_map/ppermute | solution.py:35
  259.4 30.4 %copy-start.56 = (bf16[2,512,1024]{2,1,0:T(8,128)(2,1)}, bf16[2,512,1024]{2,1,0:T(8,128)(2,1)S(1)}, u32[]{:S(2)}) copy-start(bf16[2,512,1024]{2,1,0:T(8,128)(2,1)S(1)} %constant_dynamic-update-slice_fusion) | copy-start | bytes 6291460
  359.9 35.6 %copy-start.30 = (f32[1,512,1024]{2,1,0:T(8,128)}, f32[1,512,1024]{2,1,0:T(8,128)S(1)}, u32[]{:S(2)}) copy-start(f32[1,512,1024]{2,1,0:T(8,128)S(1)} %get-tuple-element.43) | copy-start | bytes 6291460
  359.9 35.6 %copy-start.134 = (f32[512]{0:T(512)}, f32[512]{0:T(512)S(1)}, u32[]{:S(2)}) copy-start(f32[512]{0:T(512)S(1)} %broadcast_multiply_fusion.4) | copy-start | bytes 6148
  360.3 35.2 %copy-start.150 = (f32[512]{0:T(512)}, f32[512]{0:T(512)S(1)}, u32[]{:S(2)}) copy-start(f32[512]{0:T(512)S(1)} %fusion.242) | copy-start | bytes 6148
  360.3 27.5 %slice-start.4 = ((s8[8388608]{0:T(1024)(128)(4,1)}), s8[4194304]{0:T(1024)(128)(4,1)S(1)}, s32[]{:S(2)}) async-start(s8[8388608]{0:T(1024)(128)(4,1)} %bitcast.522), calls=%async_computation.12 | async-start | bytes 8388608
  403.7 24.9 %copy-start.46 = (bf16[512,1024]{0,1:T(8,128)(2,1)S(1)}, bf16[512,1024]{0,1:T(8,128)(2,1)}, u32[]{:S(2)}) copy-start(bf16[512,1024]{0,1:T(8,128)(2,1)} %copy.91) | copy-start | bytes 3145732
  440.8 21.2 %copy-start.42 = (bf16[512,1024]{0,1:T(8,128)(2,1)S(1)}, bf16[512,1024]{0,1:T(8,128)(2,1)}, u32[]{:S(2)}) copy-start(bf16[512,1024]{0,1:T(8,128)(2,1)} %copy.89) | copy-start | bytes 3145732
  512.9 21.6 %collective-permute-start.3 = (bf16[1,512,1024]{2,1,0:T(8,128)(2,1)}, bf16[1,512,1024]{2,1,0:T(8,128)(2,1)S(1)}, u32[]{:S(2)}, u32[]{:S(2)}) collective-permute-start(bf16[1,512,1024]{2,1,0:T(8,128)(2,1)} %get-tuple-element.55), channel_id=1, source_target_pairs={{1,0},{3,2},{5,4},{7,6},{9,8},{11,10},{13,12},{15,14},{17,16},{19,... | collective-permute-start | bytes 3145736 | tf_op jit(solution)/shard_map/ppermute | solution.py:35
  535.5 26.0 %copy-start.50 = (bf16[1,512,1024]{2,1,0:T(8,128)(2,1)}, bf16[1,512,1024]{2,1,0:T(8,128)(2,1)S(1)}, u32[]{:S(2)}) copy-start(bf16[1,512,1024]{2,1,0:T(8,128)(2,1)S(1)} %get-tuple-element.29) | copy-start | bytes 3145732
  599.9 21.2 %copy-start.41 = (bf16[512,1024]{0,1:T(8,128)(2,1)S(1)}, bf16[512,1024]{0,1:T(8,128)(2,1)}, u32[]{:S(2)}) copy-start(bf16[512,1024]{0,1:T(8,128)(2,1)} %copy.87) | copy-start | bytes 3145732
  669.6 23.4 %collective-permute-start.4 = (bf16[1,512,1024]{2,1,0:T(8,128)(2,1)S(1)}, bf16[1,512,1024]{2,1,0:T(8,128)(2,1)S(1)}, u32[]{:S(2)}, u32[]{:S(2)}) collective-permute-start(bf16[1,512,1024]{2,1,0:T(8,128)(2,1)S(1)} %fusion.108), channel_id=1, source_target_pairs={{1,0},{3,2},{5,4},{7,6},{9,8},{11,10},{13,12},{15,14},{17,16},{19,... | collective-permute-start | bytes 3145736 | tf_op jit(solution)/shard_map/ppermute | solution.py:35
  693.1 25.6 %copy-start.72 = (bf16[1,512,1024]{2,1,0:T(8,128)(2,1)}, bf16[1,512,1024]{2,1,0:T(8,128)(2,1)S(1)}, u32[]{:S(2)}) copy-start(bf16[1,512,1024]{2,1,0:T(8,128)(2,1)S(1)} %collective-permute-done.4) | copy-start | bytes 3145732
  727.5 339.4 %reduce-scatter.5.cloned.1.call-start = ((), (), s32[]{:S(2)}) async-start(), calls=%async_computation.4 | async-start | bytes 13369344 | tf_op jit(solution)/shard_map/reduce_scatter | solution.py:338
  749.2 22.6 %copy-start.9 = (bf16[1,1536,1024]{1,2,0:T(8,128)(2,1)S(1)}, bf16[1,1536,1024]{1,2,0:T(8,128)(2,1)}, u32[]{:S(2)}) copy-start(bf16[1,1536,1024]{1,2,0:T(8,128)(2,1)} %copy.86) | copy-start | bytes 9437188
  838.3 316.9 %reduce-scatter.11.cloned.1.call-start = ((), (), s32[]{:S(2)}) async-start(), calls=%async_computation.7 | async-start | bytes 17825792 | tf_op jit(solution)/shard_map/reduce_scatter | solution.py:343
  899.6 438.3 %reduce-scatter.9.cloned.1.call-start = ((), (), s32[]{:S(2)}) async-start(), calls=%async_computation.6 | async-start | bytes 17825792 | tf_op jit(solution)/shard_map/reduce_scatter | solution.py:341
  978.0 29.3 %copy-start.77 = (bf16[1,512,1024]{2,1,0:T(8,128)(2,1)}, bf16[1,512,1024]{2,1,0:T(8,128)(2,1)S(1)}, u32[]{:S(2)}) copy-start(bf16[1,512,1024]{2,1,0:T(8,128)(2,1)S(1)} %fusion.117) | copy-start | bytes 3145732
  1009.4 54.0 %collective-permute-start.5 = (bf16[2,512,512]{2,1,0:T(8,128)(2,1)}, bf16[2,512,512]{2,1,0:T(8,128)(2,1)}, u32[]{:S(2)}, u32[]{:S(2)}) collective-permute-start(bf16[2,512,512]{2,1,0:T(8,128)(2,1)} %fusion.175), channel_id=1, source_target_pairs={{0,1},{1,0},{2,3},{3,2},{4,5},{5,4},{6,7},{7,6},{8,9},{9,8},{10,11... | collective-permute-start | bytes 3145736 | tf_op jit(solution)/shard_map/ppermute | solution.py:29
  (160 other events, 1187.5 us)
Sparse Core Ops, SparseCore 0:
  727.6 72.9 reduce-scatter.6
  838.4 134.2 reduce-scatter.4
  977.9 177.2 reduce-scatter.10
  1160.3 177.5 reduce-scatter.8
where the time goes:
time: 1360 us; the launch traced here: 1340 us
  matrix products  628 us (46%)
  waiting for transfers between devices  334 us (25%)
  other arithmetic  212 us (16%)
  local copies, waits for them, and re-layouts  86.1 us (6%)
  blocking collectives  51.4 us (4%)
  between operations  22 us (2%)
    reduce_scatter x1, waiting for transfers between devices, body(): lax.psum_scatter(ffn_total[1], 'dp', scatter_dimension=0, tiled=True)  183 us
    reduce_scatter x1, waiting for transfers between devices, body(): lax.psum_scatter(ffn_total[3], 'dp', scatter_dimension=0, tiled=True)  88.3 us
    dot_general x3, matrix products, backward_attention(): jnp.einsum('bqhd,bkhd->bhqk', d_attended, value_rows, preferred_element_t...  64 us
    dot_general x3, matrix products, backward_ffn(): jnp.einsum('bsf,bsd->fd', hidden, grad_low, preferred_element_type=jnp.fl...  61 us
    convert_element_type x3, other arithmetic, backward_attention(): d_scores = (attention * (d_attention - inner_sum)).astype(jnp.bfloat16)  55.9 us
    ppermute x4, waiting for transfers between devices, passed_along(): return lax.ppermute(value, axis, pairs)  55.3 us
    unnamed x1, blocking collectives  51.4 us
    unnamed x373, local copies, waits for them, and re-layouts  47.8 us
  transfers between devices with their start and end apart: 10, of which 7 were waited for; matrix products, arithmetic and copies ran while one was open for 24% of the time, Pallas kernels for 0%

commit v1 on v0

v1 whole, which is shorter than its diff:
```python
import math

import jax
import jax.numpy as jnp
from jax import lax
from jax.experimental import pallas as pl
from jax.experimental.pallas import tpu as pltpu
from jax.sharding import PartitionSpec as P

WIDTH = 1024
HEADS = 8
HEAD = 128
FF = 4096
SEG = 512
MEM = 512
CMEM = 512
RATE = 2
COMP = 256
CTX = MEM + CMEM
HALF = SEG // 2
HP = 4

EPS = 1e-05
NEG = -1e30
ROOT_TWO_PI = 0.7978845608028654
SCALE = HEAD**-0.5
LOG2E = math.log2(math.e)
LN2 = math.log(2.0)
BF = jnp.bfloat16
F32 = jnp.float32
PARAMS = pltpu.CompilerParams(vmem_limit_bytes=56 << 20)


def nn(a, b):
    return lax.dot_general(a, b, (((1,), (0,)), ((), ())), preferred_element_type=F32)


def nt(a, b):
    return lax.dot_general(a, b, (((1,), (1,)), ((), ())), preferred_element_type=F32)


def tn(a, b):
    return lax.dot_general(a, b, (((0,), (0,)), ((), ())), preferred_element_type=F32)


def shape(dims, dtype=BF):
    return jax.ShapeDtypeStruct(dims, dtype)


def whole(*dims):
    return pl.BlockSpec(dims, lambda *_: (0,) * len(dims))


def cost(flops, moved, trans=0):
    return pl.CostEstimate(flops=int(flops), bytes_accessed=int(moved), transcendentals=int(trans))


def normalise(values):
    centred = values - jnp.mean(values, axis=-1, keepdims=True)
    inverse = lax.rsqrt(jnp.mean(centred * centred, axis=-1, keepdims=True) + EPS)
    return centred * inverse, inverse


def norm_back(unit, inverse, gain, grad):
    scaled = grad * gain
    along = jnp.mean(scaled * unit, axis=-1, keepdims=True)
    return inverse * (scaled - jnp.mean(scaled, axis=-1, keepdims=True) - unit * along)


def memory_kernel(flags, comp, mem, gain, wk, wv, normed, kv):
    seq, source = pl.program_id(0), pl.program_id(1)
    keep = (1 - flags[seq]).astype(F32)
    rows = jnp.where(source == 0, comp[0].astype(F32), mem[0].astype(F32)) * keep
    unit, _ = normalise(rows)
    rounded = (unit * gain[...].astype(F32)).astype(BF)
    normed[0] = rounded
    kv[0, :, :WIDTH] = nn(rounded, wk[...]).astype(BF)
    kv[0, :, WIDTH:] = nn(rounded, wv[...]).astype(BF)


def memory_keyvals(flags, compressed, memory, gain, w_proj):
    seqs = memory.shape[0]
    rows = pl.BlockSpec((1, MEM, WIDTH), lambda s, j, *_: (s, 0, 0))
    return pl.pallas_call(
        memory_kernel,
        name="memory_keyvals",
        grid_spec=pltpu.PrefetchScalarGridSpec(
            num_scalar_prefetch=1,
            grid=(seqs, 2),
            in_specs=[
                rows,
                rows,
                whole(1, WIDTH),
                pl.BlockSpec((WIDTH, WIDTH), lambda *_: (0, 1)),
                pl.BlockSpec((WIDTH, WIDTH), lambda *_: (0, 2)),
            ],
            out_specs=[
                pl.BlockSpec((1, MEM, WIDTH), lambda s, j, *_: (s, j, 0)),
                pl.BlockSpec((1, MEM, 2 * WIDTH), lambda s, j, *_: (s, j, 0)),
            ],
        ),
        out_shape=[shape((seqs, CTX, WIDTH)), shape((seqs, CTX, 2 * WIDTH))],
        compiler_params=PARAMS,
        cost_estimate=cost(seqs * CTX * WIDTH * 2 * WIDTH * 2, 24 << 20),
    )(flags, compressed, memory, gain, w_proj, w_proj)


def project_kernel(x, gain, w, normed, qkv):
    tile = pl.program_id(0)

    @pl.when(tile == 0)
    def _():
        unit, _ = normalise(x[...].astype(F32))
        normed[...] = (unit * gain[...].astype(F32)).astype(BF)

    factor = jnp.where(tile == 0, SCALE * LOG2E, 1.0)
    qkv[...] = (nn(normed[...], w[...]) * factor).astype(BF)


def project(x, gain, w_proj):
    return pl.pallas_call(
        project_kernel,
        name="project",
        grid=(3,),
        in_specs=[whole(SEG, WIDTH), whole(1, WIDTH), pl.BlockSpec((WIDTH, WIDTH), lambda t: (0, t))],
        out_specs=[whole(SEG, WIDTH), pl.BlockSpec((SEG, WIDTH), lambda t: (0, t))],
        out_shape=[shape((SEG, WIDTH)), shape((SEG, 3 * WIDTH))],
        compiler_params=PARAMS,
        cost_estimate=cost(SEG * WIDTH * 3 * WIDTH * 2, 11 << 20),
    )(x, gain, w_proj)


def fill_masks(info, bias, unseen):
    key = lax.broadcasted_iota(jnp.int32, (SEG, SEG), 0)
    query = lax.broadcasted_iota(jnp.int32, (SEG, SEG), 1)
    least = jnp.where(query >= info[1], info[1], 0)
    bias[...] = jnp.where((key <= query) & (key >= least), 0.0, NEG)
    position = lax.broadcasted_iota(jnp.int32, (1, SEG), 1)
    limit = jnp.where(info[0] == 0, info[1], 0)
    unseen[...] = jnp.where(position < limit, 0.0, -NEG)


def attend_kernel(info, q, kx, vx, km, vm, attended, log_total, bias, unseen):
    @pl.when(pl.program_id(0) == 0)
    def _():
        fill_masks(info, bias, unseen)

    pieces = [
        (h, slice(h * HEAD, (h + 1) * HEAD), slice(part * HALF, (part + 1) * HALF), (part + 1) * HALF)
        for h in range(HP)
        for part in range(2)
    ]

    def scores(h, c, r, count):
        rows = q[r, c]
        return nt(km[:, c], rows), nt(kx[:count, c], rows) + bias[:count, r]

    def weights(h, c, r, count, on_memory, on_segment):
        hidden = unseen[:, r]
        top = jnp.maximum(
            jnp.max(on_memory, axis=0, keepdims=True) - hidden,
            jnp.max(on_segment, axis=0, keepdims=True),
        )
        p_memory = jnp.exp2(on_memory - (top + hidden))
        p_segment = jnp.exp2(on_segment - top)
        total = jnp.sum(p_memory, axis=0, keepdims=True) + jnp.sum(p_segment, axis=0, keepdims=True)
        log_total[h, :, r] = top + jnp.log2(total)
        return p_memory.astype(BF), p_segment.astype(BF), total

    def finish(h, c, r, count, p_memory, p_segment, total):
        turned = nn(vm[:, c].T, p_memory) + nn(vx[:count, c].T, p_segment)
        attended[r, c] = (turned * (1.0 / total)).T.astype(BF)

    held, ready = {}, {}
    for step in range(len(pieces) + 2):
        if step < len(pieces):
            held[step] = scores(*pieces[step])
        if 0 <= step - 1 < len(pieces):
            ready[step - 1] = weights(*pieces[step - 1], *held.pop(step - 1))
        if 0 <= step - 2 < len(pieces):
            finish(*pieces[step - 2], *ready.pop(step - 2))


def head_specs(seq):
    wide = HP * HEAD
    count = WIDTH // wide
    segment = [pl.BlockSpec((SEG, wide), lambda h, *_, o=o: (0, o * count + h)) for o in range(3)]
    memory = [
        pl.BlockSpec((None, CTX, wide), lambda h, *_, o=o: (seq, 0, o * count + h)) for o in range(2)
    ]
    stat = pl.BlockSpec((HP, 1, SEG), lambda h, *_: (h, 0, 0))
    scratch = [pltpu.VMEM((SEG, SEG), F32), pltpu.VMEM((1, SEG), F32)]
    return count, segment, memory, stat, scratch


def attend(info, qkv, kv_memory, seq):
    count, segment, memory, stat, scratch = head_specs(seq)
    return pl.pallas_call(
        attend_kernel,
        name="attend",
        grid_spec=pltpu.PrefetchScalarGridSpec(
            num_scalar_prefetch=1,
            grid=(count,),
            in_specs=segment + memory,
            out_specs=[segment[0], stat],
            scratch_shapes=scratch,
        ),
        out_shape=[shape((SEG, WIDTH)), shape((HEADS, 1, SEG), F32)],
        compiler_params=PARAMS,
        cost_estimate=cost(12e9, 10 << 20),
    )(info, qkv, qkv, qkv, kv_memory, kv_memory)


FT = 1024
FS = 512


def gelu_parts(v):
    square = v * v
    t = jnp.tanh(ROOT_TWO_PI * v * (1.0 + 0.044715 * square))
    half = 0.5 + 0.5 * t
    slope = ROOT_TWO_PI * (1.0 + 3 * 0.044715 * square)
    return v * half, half * (1.0 + v * (1.0 - t) * slope)


def feed_kernel(
    attended, x, w_out, gain, w_up, b_up, w_down, b_down, y, residual, ffn_in, hidden, gate, total
):
    step = pl.program_id(0)

    @pl.when(step == 0)
    def _():
        rows = x[...].astype(F32) + nn(attended[...], w_out[...])
        residual[...] = rows
        unit, _ = normalise(rows)
        ffn_in[...] = (unit * gain[...].astype(F32)).astype(BF)
        total[...] = rows + b_down[...].astype(F32)

    cuts = [slice(i * FS, (i + 1) * FS) for i in range(FT // FS)]
    ups = [nn(ffn_in[...], w_up[:, c]) + b_up[:, c].astype(F32) for c in cuts]
    added = None
    for c, up in zip(cuts, ups):
        value, slope = gelu_parts(up)
        value = value.astype(BF)
        hidden[:, c] = value
        gate[:, c] = slope.astype(BF)
        part = nn(value, w_down[c, :])
        added = part if added is None else added + part
    total[...] += added

    @pl.when(step == pl.num_programs(0) - 1)
    def _():
        y[...] = total[...].astype(BF)


def feed(attended, x, w_out, gain, w_up, b_up, w_down, b_down):
    steps = FF // FT
    wide = pl.BlockSpec((SEG, FT), lambda t: (0, t))
    return pl.pallas_call(
        feed_kernel,
        name="feed",
        grid=(steps,),
        in_specs=[
            whole(SEG, WIDTH),
            whole(SEG, WIDTH),
            whole(WIDTH, WIDTH),
            whole(1, WIDTH),
            pl.BlockSpec((WIDTH, FT), lambda t: (0, t)),
            pl.BlockSpec((1, FT), lambda t: (0, t)),
            pl.BlockSpec((FT, WIDTH), lambda t: (t, 0)),
            whole(1, WIDTH),
        ],
        out_specs=[whole(SEG, WIDTH), whole(SEG, WIDTH), whole(SEG, WIDTH), wide, wide],
        out_shape=[
            shape((SEG, WIDTH)),
            shape((SEG, WIDTH), F32),
            shape((SEG, WIDTH)),
            shape((SEG, FF)),
            shape((SEG, FF)),
        ],
        scratch_shapes=[pltpu.VMEM((SEG, WIDTH), F32)],
        compiler_params=PARAMS,
        cost_estimate=cost(SEG * WIDTH * (2 * FF + WIDTH) * 2, 32 << 20),
    )(attended, x, w_out, gain, w_up, b_up, w_down, b_down)


def feed_back_kernel(
    gy, w_down, gate, w_up, residual, gain, w_out, d_hidden, d_residual, low, d_attended, d_up, d_down, total
):
    step = pl.program_id(0)

    @pl.when(step == 0)
    def _():
        d_down[...] = jnp.sum(gy[...].astype(F32), axis=0, keepdims=True)

    cuts = [slice(i * FS, (i + 1) * FS) for i in range(FT // FS)]
    raws = [nt(gy[...], w_down[c, :]) for c in cuts]
    added = None
    for c, raw in zip(cuts, raws):
        value = (raw * gate[:, c].astype(F32)).astype(BF)
        d_hidden[:, c] = value
        d_up[:, c] = jnp.sum(value.astype(F32), axis=0, keepdims=True)
        part = nt(value, w_up[:, c])
        added = part if added is None else added + part

    @pl.when(step == 0)
    def _():
        total[...] = added

    @pl.when(step > 0)
    def _():
        total[...] += added

    @pl.when(step == pl.num_programs(0) - 1)
    def _():
        unit, inverse = normalise(residual[...])
        grad = gy[...].astype(F32) + norm_back(unit, inverse, gain[...].astype(F32), total[...])
        d_residual[...] = grad
        low[...] = grad.astype(BF)
        d_attended[...] = nt(low[...], w_out[...]).astype(BF)


def feed_back(gy, w_down, gate, w_up, residual, gain, w_out):
    steps = FF // FT
    wide = pl.BlockSpec((SEG, FT), lambda t: (0, t))
    return pl.pallas_call(
        feed_back_kernel,
        name="feed_back",
        grid=(steps,),
        in_specs=[
            whole(SEG, WIDTH),
            pl.BlockSpec((FT, WIDTH), lambda t: (t, 0)),
            wide,
            pl.BlockSpec((WIDTH, FT), lambda t: (0, t)),
            whole(SEG, WIDTH),
            whole(1, WIDTH),
            whole(WIDTH, WIDTH),
        ],
        out_specs=[
            wide,
            whole(SEG, WIDTH),
            whole(SEG, WIDTH),
            whole(SEG, WIDTH),
            pl.BlockSpec((1, FT), lambda t: (0, t)),
            whole(1, WIDTH),
        ],
        out_shape=[
            shape((SEG, FF)),
            shape((SEG, WIDTH), F32),
            shape((SEG, WIDTH)),
            shape((SEG, WIDTH)),
            shape((1, FF), F32),
            shape((1, WIDTH), F32),
        ],
        scratch_shapes=[pltpu.VMEM((SEG, WIDTH), F32)],
        compiler_params=PARAMS,
        cost_estimate=cost(SEG * WIDTH * (2 * FF + WIDTH) * 2, 32 << 20),
    )(gy, w_down, gate, w_up, residual, gain, w_out)


def attend_back_kernel(
    info, q, kx, vx, km, vm, d_out, out, log_total, dq, dkx, dvx, dkm, dvm, bias, unseen
):
    @pl.when(pl.program_id(0) == 0)
    def _():
        fill_masks(info, bias, unseen)

    every, low, high = slice(0, SEG), slice(0, HALF), slice(HALF, SEG)
    for h in range(d_out.shape[1] // HEAD):
        c = slice(h * HEAD, (h + 1) * HEAD)
        qh, gh = q[:, c], d_out[:, c]
        inner = jnp.sum((gh.astype(F32) * out[:, c].astype(F32)).T, axis=0, keepdims=True)
        level = log_total[h]

        def piece(k, v, r, mask):
            logits = nt(k, qh[r])
            if mask is None:
                p = jnp.exp2(logits - (level[:, r] + unseen[:, r]))
            else:
                p = jnp.exp2(logits + mask - level[:, r])
            ds = (p * (nt(v, gh[r]) - inner[:, r])).astype(BF)
            return p.astype(BF), ds

        p_memory, ds_memory = piece(km[:, c], vm[:, c], every, None)
        p_low, ds_low = piece(kx[low, c], vx[low, c], every, bias[low, :])
        p_high, ds_high = piece(kx[high, c], vx[high, c], high, bias[high, high])
        dvm[:, c] = nn(p_memory, gh).astype(BF)
        dkm[:, c] = (nn(ds_memory, qh) * LN2).astype(BF)
        dvx[low, c] = nn(p_low, gh).astype(BF)
        dkx[low, c] = (nn(ds_low, qh) * LN2).astype(BF)
        dvx[high, c] = nn(p_high, gh[high]).astype(BF)
        dkx[high, c] = (nn(ds_high, qh[high]) * LN2).astype(BF)
        turned = kx[:, c].T
        first = nn(km[:, c].T, ds_memory) + nn(turned[:, low], ds_low)
        dq[low, c] = (first[:, low] * SCALE).T.astype(BF)
        dq[high, c] = ((first[:, high] + nn(turned[:, high], ds_high)) * SCALE).T.astype(BF)


def attend_back(info, qkv, kv_memory, seq, d_out, out, log_total):
    count, segment, memory, stat, scratch = head_specs(seq)
    plain = segment[0]
    rows = pl.BlockSpec((CTX, HP * HEAD), lambda h, *_: (0, h))
    return pl.pallas_call(
        attend_back_kernel,
        name="attend_back",
        grid_spec=pltpu.PrefetchScalarGridSpec(
            num_scalar_prefetch=1,
            grid=(count,),
            in_specs=segment + memory + [plain, plain, stat],
            out_specs=[plain, plain, plain, rows, rows],
            scratch_shapes=scratch,
        ),
        out_shape=[shape((SEG, WIDTH))] * 3 + [shape((CTX, WIDTH))] * 2,
        compiler_params=PARAMS,
        cost_estimate=cost(18e9, 20 << 20),
    )(info, qkv, qkv, qkv, kv_memory, kv_memory, d_out, out, log_total)


def project_back_kernel(dq, dk, dv, w, x, gain, d_residual, dx, total):
    step = pl.program_id(0)

    @pl.when(step == 0)
    def _():
        total[...] = nt(dq[...], w[...])

    @pl.when(step == 1)
    def _():
        total[...] += nt(dk[...], w[...])

    @pl.when(step == 2)
    def _():
        grad = total[...] + nt(dv[...], w[...])
        unit, inverse = normalise(x[...].astype(F32))
        dx[...] = (d_residual[...] + norm_back(unit, inverse, gain[...].astype(F32), grad)).astype(BF)


def project_back(dq, dk, dv, w_proj, x, gain, d_residual):
    full = whole(SEG, WIDTH)
    return pl.pallas_call(
        project_back_kernel,
        name="project_back",
        grid=(3,),
        in_specs=[
            full,
            full,
            full,
            pl.BlockSpec((WIDTH, WIDTH), lambda t: (0, t)),
            full,
            whole(1, WIDTH),
            full,
        ],
        out_specs=full,
        out_shape=shape((SEG, WIDTH)),
        scratch_shapes=[pltpu.VMEM((SEG, WIDTH), F32)],
        compiler_params=PARAMS,
        cost_estimate=cost(SEG * WIDTH * 3 * WIDTH * 2, 14 << 20),
    )(dq, dk, dv, w_proj, x, gain, d_residual)


def compress_kernel(flags, grouped, w, bias, out):
    keep = (1 - flags[pl.program_id(0)]).astype(BF)
    out[0] = (nn(grouped[0] * keep, w[...]) + bias[...].astype(F32)).astype(BF)


def compress(flags, memory, w_compress, b_compress):
    seqs = memory.shape[0]
    wide = RATE * WIDTH
    grouped = memory.reshape(seqs, COMP, wide)
    return pl.pallas_call(
        compress_kernel,
        name="compress",
        grid_spec=pltpu.PrefetchScalarGridSpec(
            num_scalar_prefetch=1,
            grid=(seqs,),
            in_specs=[
                pl.BlockSpec((1, COMP, wide), lambda s, *_: (s, 0, 0)),
                whole(wide, WIDTH),
                whole(1, WIDTH),
            ],
            out_specs=pl.BlockSpec((1, COMP, WIDTH), lambda s, *_: (s, 0, 0)),
        ),
        out_shape=shape((seqs, COMP, WIDTH)),
        compiler_params=PARAMS,
        cost_estimate=cost(seqs * COMP * wide * WIDTH * 2, 8 << 20),
    )(flags, grouped, w_compress.reshape(wide, WIDTH), b_compress)


def turned_index(value, bits):
    return sum(((value >> b) & 1) << (bits - 1 - b) for b in range(bits))


def weight_kernel(count, rows, extra, mine, *refs):
    parts = (len(refs) - 2 - (1 if extra else 0)) // 2
    lefts, rights = refs[:parts], refs[parts : 2 * parts]
    send, keep = refs[-2:]
    value = None
    for left, right in zip(lefts, rights):
        term = tn(left[...], right[...])
        value = term if value is None else value + term
    value = value.astype(BF)
    even = mine[0] == 0
    bits = (count - 1).bit_length()
    for pair in range(count // 2):
        place = turned_index(pair, bits - 1)
        one = value[(2 * pair) * rows : (2 * pair + 1) * rows]
        two = value[(2 * pair + 1) * rows : (2 * pair + 2) * rows]
        send[place, 0, :rows] = jnp.where(even, two, one)
        keep[place, 0, :rows] = jnp.where(even, one, two)
    if extra:
        small = refs[2 * parts]
        for pair in range(count // 2):
            place = turned_index(pair, bits - 1)
            send[place, 0, rows:] = jnp.where(even, small[2 * pair + 1], small[2 * pair])
            keep[place, 0, rows:] = jnp.where(even, small[2 * pair], small[2 * pair + 1])


def weight_grad(mine, size, lefts, rights, columns, tile, small=None):
    height = lefts[0][0].shape[-1]
    tall = min(height, 1024)
    blocks = height // tall
    count = size // blocks
    rows = tall // count
    order = (blocks - 1).bit_length()

    def spec(array, lead, width, first, along):
        def place(i, j, *_):
            col = first + (i if along == 0 else j)
            return (0, col) if lead is None else (lead, 0, col)

        depth = array.shape[-2]
        return pl.BlockSpec((depth, width) if lead is None else (None, depth, width), place)

    def out_place(i, j, *_):
        return (0, sum(((i // (1 << b)) % 2) * (1 << (order - 1 - b)) for b in range(order)), 0, j)

    total = rows + (0 if small is None else small.shape[1])
    block = pl.BlockSpec((count // 2, 1, total, tile), out_place)
    out = shape((count // 2, blocks, total, columns))
    specs = [spec(a, lead, tall, 0, 0) for a, lead in lefts]
    specs += [spec(a, lead, tile, first, 1) for a, lead, first in rights]
    args = [a for a, _ in lefts] + [a for a, _, _ in rights]
    if small is not None:
        specs.append(pl.BlockSpec(small.shape[:2] + (tile,), lambda i, j, *_: (0, 0, j)))
        args.append(small)
    depth = sum(a.shape[-2] for a, _ in lefts)
    send, keep = pl.pallas_call(
        lambda *refs: weight_kernel(count, rows, small is not None, *refs),
        name="weight_grad",
        grid_spec=pltpu.PrefetchScalarGridSpec(
            num_scalar_prefetch=1,
            grid=(blocks, columns // tile),
            in_specs=specs,
            out_specs=[block, block],
        ),
        out_shape=[out, out],
        compiler_params=PARAMS,
        cost_estimate=cost(2 * depth * height * columns, 2 * (depth * (height + columns) + height * columns)),
    )(mine, *args)
    flat = (size // 2, total, columns)
    return send.reshape(flat), keep.reshape(flat)


def halve_kernel(bit, kept_a, got_a, kept_b, got_b, send, keep):
    send[...] = (kept_a[...].astype(F32) + got_a[...].astype(F32)).astype(BF)
    keep[...] = (kept_b[...].astype(F32) + got_b[...].astype(F32)).astype(BF)


def halve(bit, kept, got):
    count, rows, columns = kept.shape
    half = count // 2
    steps = 2 if columns % 256 == 0 and kept.size >= 1 << 19 else 1
    block = (half, rows, columns // steps)
    other = pl.BlockSpec(block, lambda j, b: (1 - b[0], 0, j))
    own = pl.BlockSpec(block, lambda j, b: (b[0], 0, j))
    plain = pl.BlockSpec(block, lambda j, b: (0, 0, j))
    out = shape((half, rows, columns))
    return pl.pallas_call(
        halve_kernel,
        name="halve",
        grid_spec=pltpu.PrefetchScalarGridSpec(
            num_scalar_prefetch=1,
            grid=(steps,),
            in_specs=[other, other, own, own],
            out_specs=[plain, plain],
        ),
        out_shape=[out, out],
        compiler_params=PARAMS,
        cost_estimate=cost(kept.size, kept.size * 6),
    )(bit, kept, got, kept, got)


def swap_bit(value, size, bit):
    return lax.ppermute(value, "dp", [(i, i ^ (1 << bit)) for i in range(size)])


def reduce_parts(send, keep, size, bits):
    for level in range(len(bits)):
        got = swap_bit(send, size, level)
        if level + 1 < len(bits):
            send, keep = halve(bits[level + 1], keep, got)
    return keep[0].astype(F32) + got[0].astype(F32)


def one_way(value, first, second):
    return lax.ppermute(value, "section", [(first, second)])


def nothing(shapes):
    def kernel(*refs):
        pass

    anywhere = pl.BlockSpec(memory_space=pl.ANY)
    return pl.pallas_call(
        kernel, name="nothing", out_shape=shapes, out_specs=[anywhere] * len(shapes), compiler_params=PARAMS
    )()


def branches(chosen, first, second):
    shapes = jax.eval_shape(first if first is not None else second)
    leaves, tree = jax.tree.flatten(shapes)
    empty = lambda: jax.tree.unflatten(tree, nothing([shape(leaf.shape, leaf.dtype) for leaf in leaves]))
    return lax.cond(chosen, first or empty, second or empty)


def after(value, *others):
    return lax.optimization_barrier((value,) + others)[0]


def body(
    inputs,
    cotangent,
    memory,
    compressed,
    reset_flags,
    boundary,
    gain_attn,
    projection_weight,
    w_output,
    gain_ffn,
    w_up,
    b_up,
    w_down,
    b_down,
    w_compress,
    b_compress,
):
    section = lax.axis_index("section")
    is_first = section == 0
    size = lax.axis_size("dp")
    mine = lax.axis_index("dp")
    levels = (size - 1).bit_length()
    bits = [((mine >> b) & 1).astype(jnp.int32).reshape(1) for b in range(levels)]
    seqs, _, width = inputs.shape
    memory, compressed = memory[0], compressed[0]
    w_proj, w_out, w_up, w_down = projection_weight[0], w_output[0], w_up[0], w_down[0]
    info = [jnp.stack([reset_flags[s], boundary[s]]).astype(jnp.int32) for s in range(seqs)]

    leaving = jnp.where(is_first, cotangent, inputs)
    arriving = [lax.ppermute(leaving[s], "section", [(0, 1), (1, 0)]) for s in range(seqs)]
    first_x = [jnp.concatenate([inputs[s], arriving[s]], axis=1) for s in range(seqs)]
    last_gy = [jnp.concatenate([arriving[s], cotangent[s]], axis=1) for s in range(seqs)]
    normed_memory, kv_memory = memory_keyvals(reset_flags, compressed, memory, gain_attn, w_proj)

    def forward(s, x):
        normed, qkv = project(x, gain_attn, w_proj)
        attended, log_total = attend(info[s], qkv, kv_memory, s)
        y, residual, ffn_in, hidden, gate = feed(
            attended, x, w_out, gain_ffn, w_up, b_up, w_down, b_down
        )
        return dict(
            y=y,
            normed=normed,
            qkv=qkv,
            attended=attended,
            log_total=log_total,
            residual=residual,
            ffn_in=ffn_in,
            hidden=hidden,
            gate=gate,
        )

    def back_ffn(saved, gy):
        names = ("d_hidden", "d_residual", "low", "d_attended", "d_up", "d_down")
        values = feed_back(gy, w_down, saved["gate"], w_up, saved["residual"], gain_ffn, w_out)
        return dict(zip(names, values))

    def back_attend(s, saved, part):
        names = ("dq", "dkx", "dvx", "dkm", "dvm")
        values = attend_back(
            info[s], saved["qkv"], kv_memory, s, part["d_attended"], saved["attended"], saved["log_total"]
        )
        return dict(zip(names, values))

    def back_project(x, part, grads):
        return project_back(
            grads["dq"], grads["dkx"], grads["dvx"], w_proj, x, gain_attn, part["d_residual"]
        )

    def backward(s, x, saved, gy):
        part = back_ffn(saved, gy)
        grads = back_attend(s, saved, part)
        return part, grads, back_project(x, part, grads)

    def squeeze():
        return compress(reset_flags, memory, w_compress[0], b_compress)

    run0 = is_first
    saved_a0, squeezed_second = lax.cond(
        run0,
        lambda: (forward(0, first_x[0]), nothing([shape((seqs, COMP, WIDTH))])[0]),
        lambda: (
            dict(zip(sorted(FORWARD), nothing([FORWARD[k] for k in sorted(FORWARD)]))),
            squeeze(),
        ),
    )
    hop_a = one_way(saved_a0["y"], 0, 1)
    run1 = after(is_first, saved_a0["log_total"])
    saved_b0 = branches(run1, lambda: forward(1, first_x[1]), None)
    hop_b = one_way(saved_b0["y"], 0, 1)
    run2 = after(is_first, saved_b0["log_total"])
    squeezed_first, saved_a1 = lax.cond(
        run2,
        lambda: (
            squeeze(),
            dict(zip(sorted(FORWARD), nothing([FORWARD[k] for k in sorted(FORWARD)]))),
        ),
        lambda: (nothing([shape((seqs, COMP, WIDTH))])[0], forward(0, hop_a)),
    )
    run3 = after(is_first, saved_a1["log_total"])
    saved_b1 = branches(run3, None, lambda: forward(1, hop_b))

    run4 = after(is_first, saved_b1["log_total"])
    part_a1, grads_a1, dx_a1 = branches(run4, None, lambda: backward(0, hop_a, saved_a1, last_gy[0]))
    back_a = one_way(dx_a1, 1, 0)
    run5 = after(is_first, part_a1["d_down"], dx_a1)
    part_b1, grads_b1, dx_b1 = branches(run5, None, lambda: backward(1, hop_b, saved_b1, last_gy[1]))
    back_b = one_way(dx_b1, 1, 0)
    run6 = after(is_first, part_b1["d_down"], dx_b1)
    part_a0, grads_a0, dx_a0 = branches(run6, lambda: backward(0, first_x[0], saved_a0, back_a), None)

    out_a = one_way(saved_a1["y"][:, :width], 1, 0)
    out_b = one_way(saved_b1["y"][:, :width], 1, 0)

    def chunk(token, make):
        pick = after(is_first, token)
        first = lambda: make(saved_a0, saved_b0, part_a0, part_b0, grads_a0, grads_b0, back_a, back_b)
        second = lambda: make(
            saved_a1, saved_b1, part_a1, part_b1, grads_a1, grads_b1, last_gy[0], last_gy[1]
        )
        return lax.cond(pick, first, second)

    part_b0 = grads_b0 = None
    sums = {}
    token = dx_a0
    halfw = WIDTH // 2
    for i in range(2):
        send, keep = chunk(
            token,
            lambda sa, sb, pa, pb, ga, gb, ya, yb, i=i: weight_grad(
                bits[0],
                size,
                [(sa["hidden"], None), (sb["hidden"], None)],
                [(ya, None, i), (yb, None, i)],
                halfw,
                halfw,
            ),
        )
        sums["down", i] = (send, keep)
        token = keep
    run7 = after(is_first, token)
    part_b0 = branches(run7, lambda: back_ffn(saved_b0, back_b), None)
    token = part_b0["d_down"]
    for i in range(2):
        send, keep = chunk(
            token,
            lambda sa, sb, pa, pb, ga, gb, ya, yb, i=i: weight_grad(
                bits[0],
                size,
                [(sa["ffn_in"], None), (sb["ffn_in"], None)],
                [(pa["d_hidden"], None, 2 * i), (pb["d_hidden"], None, 2 * i)],
                FF // 2,
                1024,
            ),
        )
        sums["up", i] = (send, keep)
        token = keep

    def biases(pa, pb):
        up = (pa["d_up"] + pb["d_up"]).reshape(size, FF // size)
        down = (pa["d_down"] + pb["d_down"]).reshape(size, WIDTH // size)
        row = jnp.concatenate([up, down], axis=1).astype(BF)
        return jnp.pad(row[:, None, :], ((0, 0), (0, 15), (0, WIDTH - row.shape[1])))

    send, keep = chunk(
        token,
        lambda sa, sb, pa, pb, ga, gb, ya, yb: weight_grad(
            bits[0],
            size,
            [(sa["attended"], None), (sb["attended"], None)],
            [(pa["low"], None, 0), (pb["low"], None, 0)],
            WIDTH,
            1024,
            biases(pa, pb),
        ),
    )
    sums["out"] = (send, keep)
    run8 = after(is_first, keep)
    grads_b0 = branches(run8, lambda: back_attend(1, saved_b0, part_b0), None)
    token = grads_b0["dq"]
    for name, key, mem_key in (("key", "dkx", "dkm"), ("value", "dvx", "dvm"), ("query", "dq", None)):

        def make(sa, sb, pa, pb, ga, gb, ya, yb, key=key, mem_key=mem_key):
            lefts = [(sa["normed"], None), (sb["normed"], None)]
            rights = [(ga[key], None, 0), (gb[key], None, 0)]
            if mem_key is not None:
                lefts += [(normed_memory, 0), (normed_memory, 1)]
                rights += [(ga[mem_key], None, 0), (gb[mem_key], None, 0)]
            return weight_grad(bits[0], size, lefts, rights, WIDTH, 512)

        sums[name] = chunk(token, make)
        token = sums[name][1]
    run9 = after(is_first, token)
    dx_b0 = branches(run9, lambda: back_project(first_x[1], part_b0, grads_b0), None)
    grad_a = one_way(dx_a0[:, width:], 0, 1)
    grad_b = one_way(dx_b0[:, width:], 0, 1)

    done = {name: reduce_parts(send, keep, size, bits) for name, (send, keep) in sums.items()}
    rows = WIDTH // size
    g_down = jnp.concatenate([done["down", 0], done["down", 1]], axis=1)
    g_up = jnp.concatenate([done["up", 0], done["up", 1]], axis=1)
    g_out = done["out"][:rows]
    g_b_up = done["out"][rows, : FF // size]
    g_b_down = done["out"][rows, FF // size : FF // size + WIDTH // size]
    g_proj = jnp.concatenate([done["query"], done["key"], done["value"]], axis=1)

    def gain_grad(grad, weight, gain):
        own = lax.dynamic_slice_in_dim(weight, mine * rows, rows, 0).astype(F32)
        scale = lax.dynamic_slice_in_dim(gain, mine * rows, rows, 0).astype(F32)
        return jnp.sum(grad * own, axis=1) / scale

    g_gain_attn = gain_grad(g_proj, w_proj, gain_attn[0])
    g_gain_ffn = gain_grad(g_up, w_up, gain_ffn[0])

    outputs = jnp.stack(
        [
            jnp.where(is_first, got, saved["y"][:, width:])
            for got, saved in ((out_a, saved_a1), (out_b, saved_b1))
        ]
    )
    grad_inputs = jnp.stack(
        [jnp.where(is_first, dx[:, :width], got) for got, dx in ((grad_a, dx_a0), (grad_b, dx_b0))]
    )
    new_memory = jnp.stack(
        [jnp.where(is_first, x, hop) for x, hop in ((first_x[0], hop_a), (first_x[1], hop_b))]
    )
    keep_all = (1 - reset_flags).astype(BF)[:, None, None]
    squeezed = jnp.where(is_first, squeezed_first, squeezed_second)
    new_compressed = jnp.concatenate([compressed[:, COMP:] * keep_all, squeezed], axis=1)
    return (
        outputs,
        grad_inputs,
        new_memory[None],
        new_compressed[None],
        g_gain_attn[None],
        g_proj[None],
        g_out[None],
        g_gain_ffn[None],
        g_up[None],
        g_b_up[None],
        g_down[None],
        g_b_down[None],
    )


FORWARD = dict(
    y=shape((SEG, WIDTH)),
    normed=shape((SEG, WIDTH)),
    qkv=shape((SEG, 3 * WIDTH)),
    attended=shape((SEG, WIDTH)),
    log_total=shape((HEADS, 1, SEG), F32),
    residual=shape((SEG, WIDTH), F32),
    ffn_in=shape((SEG, WIDTH)),
    hidden=shape((SEG, FF)),
    gate=shape((SEG, FF)),
)


def solution(mesh):
    return jax.shard_map(
        body,
        mesh=mesh,
        in_specs=(
            P("dp", None, "section"),
            P("dp", None, "section"),
            P("section", "dp", None, None),
            P("section", "dp", None, None),
            P("dp"),
            P("dp"),
            P("section", None),
            P("section", None, None),
            P("section", None, None),
            P("section", None),
            P("section", None, None),
            P("section", None),
            P("section", None, None),
            P("section", None),
            P("section", None, None, None),
            P("section", None),
        ),
        out_specs=(
            P("dp", None, "section"),
            P("dp", None, "section"),
            P("section", "dp", None, None),
            P("section", "dp", None, None),
            P("section", "dp"),
            P("section", "dp", None),
            P("section", "dp", None),
            P("section", "dp"),
            P("section", "dp", None),
            P("section", "dp"),
            P("section", "dp", None),
            P("section", "dp"),
        ),
        check_vma=False,
    )
```

time: 1360 us -> 669 us (0.49)
  matrix products: 628 us -> 0 us
  Pallas kernels: 0 us -> 324 us
  other arithmetic: 212 us -> 30.6 us
  waiting for transfers between devices: 334 us -> 225 us
  local copies, waits for them, and re-layouts: 86.1 us -> 23.8 us
  blocking collectives: 51.4 us -> 0 us
  starting transfers between devices: 10.3 us -> 40.4 us
  between operations: 22 us -> 1.55 us
  loops' own time: 0 us -> 16.6 us
    dot_general x64 -> x0, matrix products: 628 us -> none  [the longest x3 64 us: backward_attention(): jnp.einsum('bqhd,bkhd->bhqk', d_attended, value_rows, preferred_element_t...]
    pallas_call x0 -> x53, Pallas kernels: none -> 324 us  [the longest x8 69.3 us: weight_grad(): pl.pallas_call(lambda *refs: weight_kernel(count, rows, small is not None...]
    reduce_scatter x4 -> x0, waiting for transfers between devices: 271 us -> none  [the longest x1 183 us: body(): lax.psum_scatter(ffn_total[1], 'dp', scatter_dimension=0, tiled=True)]
    ppermute x6 -> x42, waiting for transfers between devices: 63.4 us -> 225 us  [the longest x8 119 us: one_way(): return lax.ppermute(value, 'section', [(first, second)])]
    reduce_sum x24 -> x0, other arithmetic: 90.7 us -> none  [the longest x3 34 us: forward_layer(): denominator = jnp.sum(exponent, axis=-1, keepdims=True)]
    convert_element_type x10 -> x1, other arithmetic: 59.2 us -> 0.01 us  [body(): keep_all = (1 - reset_flags).astype(BF)[:, None, None]]
    unnamed x1 -> x0, blocking collectives: 51.4 us -> none
    unnamed x373 -> x132, local copies, waits for them, and re-layouts: 47.8 us -> 9.79 us
  transfers between devices with their start and end apart: 10 -> 42, of which waited for: 7 -> 21; matrix products, arithmetic and copies ran while one was open for 24% -> 5% of each run, Pallas kernels for 0% -> 35%
where the time goes in v1:
time: 669 us; the launch traced here: 662 us
  Pallas kernels  324 us (48%)
  waiting for transfers between devices  225 us (34%)
  starting transfers between devices  40.4 us (6%)
  other arithmetic  30.6 us (5%)
  local copies, waits for them, and re-layouts  23.8 us (4%)
  loops' own time  16.6 us (2%)
    ppermute x8, waiting for transfers between devices, one_way(): return lax.ppermute(value, 'section', [(first, second)])  119 us
    ppermute x32, waiting for transfers between devices, swap_bit(): return lax.ppermute(value, 'dp', [(i, i ^ 1 << bit) for i in range(size)])  104 us
    pallas_call x8, Pallas kernels, weight_grad(): pl.pallas_call(lambda *refs: weight_kernel(count, rows, small is not None...  69.3 us
    pallas_call x24, Pallas kernels, halve(): pl.pallas_call(halve_kernel, name='halve', grid_spec=pltpu.PrefetchScalar...  57.2 us
    pallas_call x2, Pallas kernels, feed_back(): pl.pallas_call(feed_back_kernel, name='feed_back', grid=(steps,), in_spec...  40.7 us
    pallas_call x2, Pallas kernels, feed(): pl.pallas_call(feed_kernel, name='feed', grid=(steps,), in_specs=[whole(S...  38.6 us
    pallas_call x2, Pallas kernels, attend_back(): pl.pallas_call(attend_back_kernel, name='attend_back', grid_spec=pltpu.Pr...  38.1 us
    ppermute x32, starting transfers between devices, swap_bit(): return lax.ppermute(value, 'dp', [(i, i ^ 1 << bit) for i in range(size)])  24.3 us
  transfers between devices with their start and end apart: 42, of which 21 were waited for; matrix products, arithmetic and copies ran while one was open for 5% of the time, Pallas kernels for 35%

profile of v1, /device:TPU:26, one launch (start us, length us, event | category | flops | bytes accessed | tf_op | source)
XLA Modules:
  0.0 662.2 jit_solution(15611597827298869475)
XLA Ops:
  5.3 16.5 %memory_keyvals.1 = (bf16[2,1024,1024]{2,1,0:T(8,128)(2,1)}, bf16[2,1024,2048]{2,1,0:T(8,128)(2,1)}) custom-call(s32[2]{0:T(128)S(1)} %copy-done.52, bf16[2,512,1024]{2,1,0:T(8,128)(2,1)} %bitcast.121, bf16[2,512,1024]{2,1,0:T(8,128)(2,1)S(1)} %bitcast.118, bf16[1,1024]{1,0:T(2,128)(2,1)S(1)} %copy-done.50, bf16[1024,3072]{1,0:T(8,128)(2,1)} %bitcast.102, ...), custom_call_target="tpu_custom_call" | custom-call | flops 8589934592 | bytes 25165824 | tf_op jit(solution)/shard_map/memory_keyvals/pallas_call | solution.py:84
  31.3 8.7 %conditional.18 = (bf16[512,1024]{1,0:T(8,128)(2,1)}, bf16[512,1024]{1,0:T(8,128)(2,1)}, bf16[512,4096]{1,0:T(8,128)(2,1)}, bf16[512,4096]{1,0:T(8,128)(2,1)}, f...) conditional(s32[]{:T(128)} %convert_element_type.162, ...), branch_computations={%region_0.1_spmd, %region_1.2_spmd} | conditional | flops 24884901888 | bytes 68157576 | solution.py:708
  50.9 44.8 %collective-permute-done.2 = bf16[512,1024]{1,0:T(8,128)(2,1)} collective-permute-done((bf16[512,1024]{1,0:T(8,128)(2,1)}, bf16[512,1024]{1,0:T(8,128)(2,1)}, u32[]{:S(2)}, u32[]{:S(2)}) %collective-permute-start.2) | collective-permute-done | bytes 1048608 | tf_op jit(solution)/shard_map/ppermute | solution.py:605
  95.6 39.3 %conditional.20 = (bf16[2,256,1024]{2,1,0:T(8,128)(2,1)}, bf16[512,1024]{1,0:T(8,128)(2,1)}, bf16[512,1024]{1,0:T(8,128)(2,1)}, bf16[512,4096]{1,0:T(8,128)(2,1)...) conditional(s32[]{:T(128)} %convert_element_type.164, ...), branch_computations={%region_4.5_spmd, %region_5.6_spmd} | conditional | flops 24884901888 | bytes 63963244 | solution.py:721
  104.1 11.8 %attend.6 = (bf16[512,1024]{1,0:T(8,128)(2,1)}, f32[8,1,512]{2,1,0:T(1,128)S(1)}) custom-call(s32[2]{0:T(128)S(1)} %get-tuple-element.530.info, bf16[512,3072]{1,0:T(8,128)(2,1)} %get-tuple-element.1267.q.kx.vx, bf16[512,3072]{1,0:T(8,128)(2,1)} %get-tuple-element.1267.q.kx.vx, bf16[512,3072]{1,0:T(8,128)(2,1)} %get-tuple-element.1267.q.kx.vx, ...), custom_call_target="tpu_custom_call" | custom-call | flops 12000000000 | bytes 10485760 | tf_op jit(solution)/shard_map/cond/branch_0_fun/attend/pallas_call | solution.py:198
  116.0 18.9 %feed.6 = (bf16[512,1024]{1,0:T(8,128)(2,1)}, f32[512,1024]{1,0:T(8,128)}, bf16[512,1024]{1,0:T(8,128)(2,1)}, bf16[512,4096]{1,0:T(8,128)(2,1)}, bf16[512,4096]{1,0:T(8,128)(2,1)}) custom-call(bf16[512,1024]{1,0:T(8,128)(2,1)} %get-tuple-element.1261.attended, bf16[512,1024]{1,0:T(8,128)(2,1)} %get-tuple-element.531.x, bf16[1024,1024]{1,0:T(8,128)(2,1)S(1)} %copy-done.58, ...), custom_call_target="tpu_custom_call" | custom-call | flops 9663676416 | bytes 33554432 | tf_op jit(solution)/shard_map/cond/branch_0_fun/feed/pallas_call | solution.py:259
  136.8 39.1 %conditional.21 = ((bf16[512,1024]{1,0:T(8,128)(2,1)}, bf16[512,1024]{1,0:T(8,128)(2,1)}, bf16[512,4096]{1,0:T(8,128)(2,1)}, bf16[512,4096]{1,0:T(8,128)(2,1)}, ...) conditional(s32[]{:T(128)} %convert_element_type.165, ...), branch_computations={%region_6.7_spmd, %region_7.8_spmd} | conditional | flops 24884901888 | bytes 68157576 | solution.py:622
  145.0 11.1 %attend.7 = (bf16[512,1024]{1,0:T(8,128)(2,1)S(1)}, f32[8,1,512]{2,1,0:T(1,128)S(1)}) custom-call(s32[2]{0:T(128)S(1)} %get-tuple-element.563.info, bf16[512,3072]{1,0:T(8,128)(2,1)} %get-tuple-element.1286.q.kx.vx, bf16[512,3072]{1,0:T(8,128)(2,1)} %get-tuple-element.1286.q.kx.vx, bf16[512,3072]{1,0:T(8,128)(2,1)} %get-tuple-element.1286.q.kx.vx, ...), custom_call_target="tpu_custom_call" | custom-call | flops 12000000000 | bytes 10485760 | tf_op jit(solution)/shard_map/cond/branch_0_fun/attend/pallas_call | solution.py:198
  156.2 19.7 %feed.7 = (bf16[512,1024]{1,0:T(8,128)(2,1)}, f32[512,1024]{1,0:T(8,128)}, bf16[512,1024]{1,0:T(8,128)(2,1)}, bf16[512,4096]{1,0:T(8,128)(2,1)}, bf16[512,4096]{1,0:T(8,128)(2,1)}) custom-call(bf16[512,1024]{1,0:T(8,128)(2,1)S(1)} %get-tuple-element.1280.attended, bf16[512,1024]{1,0:T(8,128)(2,1)} %get-tuple-element.564.x, ...), custom_call_target="tpu_custom_call" | custom-call | flops 9663676416 | bytes 33554432 | tf_op jit(solution)/shard_map/cond/branch_0_fun/feed/pallas_call | solution.py:259
  179.3 49.1 %conditional.22 = (f32[1,1024]{1,0:T(1,128)S(1)}, bf16[512,4096]{1,0:T(8,128)(2,1)}, f32[1,4096]{1,0:T(1,128)S(1)}, bf16[512,1024]{1,0:T(8,128)(2,1)}, bf16[1024...) conditional(s32[]{:T(128)} %convert_element_type.166, ...), branch_computations={%region_8.9_spmd, %region_9.10_spmd} | conditional | flops 30884900864 | bytes 88080512 | solution.py:622
  179.5 20.4 %feed_back.4 = (bf16[512,4096]{1,0:T(8,128)(2,1)}, f32[512,1024]{1,0:T(8,128)}, bf16[512,1024]{1,0:T(8,128)(2,1)}, bf16[512,1024]{1,0:T(8,128)(2,1)}, f32[1,4096]{1,0:T(1,128)S(1)}, /*index=5*/f32[1,1024]{1,0:T(1,128)S(1)}) custom-call(bf16[512,1024]{1,0:T(8,128)(2,1)} %get-tuple-element.583.gy, bf16[4096,1024]{1,0:T(8,128)(2,1)} %get-tuple-element.584.w_down, ...), custom_call_target="tpu_custom_call" | custom-call | flops 9663676416 | bytes 33554432 | tf_op jit(solution)/shard_map/cond/branch_0_fun/feed_back/pallas_call | solution.py:326
  199.9 19.1 %attend_back.4 = (bf16[512,1024]{1,0:T(8,128)(2,1)}, bf16[512,1024]{1,0:T(8,128)(2,1)}, bf16[512,1024]{1,0:T(8,128)(2,1)}, bf16[1024,1024]{1,0:T(8,128)(2,1)}, bf16[1024,1024]{1,0:T(8,128)(2,1)}) custom-call(s32[2]{0:T(128)S(1)} %get-tuple-element.594.info, bf16[512,3072]{1,0:T(8,128)(2,1)} %get-tuple-element.595.q.kx.vx, ...), custom_call_target="tpu_custom_call" | custom-call | flops 17999998976 | bytes 20971520 | tf_op jit(solution)/shard_map/cond/branch_0_fun/attend_back/pallas_call | solution.py:403
  219.0 9.2 %project_back.4 = bf16[512,1024]{1,0:T(8,128)(2,1)} custom-call(bf16[512,1024]{1,0:T(8,128)(2,1)} %get-tuple-element.1304.dq, bf16[512,1024]{1,0:T(8,128)(2,1)} %get-tuple-element.1303.dk, bf16[512,1024]{1,0:T(8,128)(2,1)} %get-tuple-element.1306.dv, bf16[1024,3072]{1,0:T(8,128)(2,1)S(1)} %bitcast.113, bf16[512,1024]{1,0:T(8,128)(2,1)} %get-tuple-element.606.x, ...), custom_call_target="tpu_custom_call" | custom-call | flops 3221225472 | bytes 14680064 | tf_op jit(solution)/shard_map/cond/branch_0_fun/project_back/pallas_call | solution.py:439
  234.1 48.5 %conditional.23 = (f32[1,1024]{1,0:T(1,128)S(1)}, bf16[512,4096]{1,0:T(8,128)(2,1)}, f32[1,4096]{1,0:T(1,128)S(1)}, bf16[512,1024]{1,0:T(8,128)(2,1)}, bf16[1024...) conditional(s32[]{:T(128)} %convert_element_type.167, ...), branch_computations={%region_10.11_spmd, %region_11.12_spmd} | conditional | flops 30884900864 | bytes 92274848 | solution.py:622
  234.1 20.3 %feed_back.5 = (bf16[512,4096]{1,0:T(8,128)(2,1)}, f32[512,1024]{1,0:T(8,128)}, bf16[512,1024]{1,0:T(8,128)(2,1)}, bf16[512,1024]{1,0:T(8,128)(2,1)}, f32[1,4096]{1,0:T(1,128)S(1)}, /*index=5*/f32[1,1024]{1,0:T(1,128)S(1)}) custom-call(bf16[512,1024]{1,0:T(8,128)(2,1)} %get-tuple-element.619.gy, bf16[4096,1024]{1,0:T(8,128)(2,1)} %get-tuple-element.620.w_down, ...), custom_call_target="tpu_custom_call" | custom-call | flops 9663676416 | bytes 33554432 | tf_op jit(solution)/shard_map/cond/branch_0_fun/feed_back/pallas_call | solution.py:326
  254.4 19.0 %attend_back.5 = (bf16[512,1024]{1,0:T(8,128)(2,1)}, bf16[512,1024]{1,0:T(8,128)(2,1)}, bf16[512,1024]{1,0:T(8,128)(2,1)}, bf16[1024,1024]{1,0:T(8,128)(2,1)}, bf16[1024,1024]{1,0:T(8,128)(2,1)}) custom-call(s32[2]{0:T(128)S(1)} %get-tuple-element.630.info, bf16[512,3072]{1,0:T(8,128)(2,1)} %get-tuple-element.631.q.kx.vx, ...), custom_call_target="tpu_custom_call" | custom-call | flops 17999998976 | bytes 20971520 | tf_op jit(solution)/shard_map/cond/branch_0_fun/attend_back/pallas_call | solution.py:403
  273.5 8.8 %project_back.5 = bf16[512,1024]{1,0:T(8,128)(2,1)} custom-call(bf16[512,1024]{1,0:T(8,128)(2,1)} %get-tuple-element.1324.dq, bf16[512,1024]{1,0:T(8,128)(2,1)} %get-tuple-element.1323.dk, bf16[512,1024]{1,0:T(8,128)(2,1)} %get-tuple-element.1326.dv, bf16[1024,3072]{1,0:T(8,128)(2,1)S(1)} %bitcast.115, bf16[512,1024]{1,0:T(8,128)(2,1)} %get-tuple-element.642.x, ...), custom_call_target="tpu_custom_call" | custom-call | flops 3221225472 | bytes 14680064 | tf_op jit(solution)/shard_map/cond/branch_0_fun/project_back/pallas_call | solution.py:439
  307.9 8.9 %conditional.25 = (bf16[2,4,256,512]{3,2,1,0:T(8,128)(2,1)}, bf16[8,256,512]{2,1,0:T(8,128)(2,1)}) conditional(s32[]{:T(128)} %convert_element_type.169, (s32[1]{0:T(128)}, bf16[512,4096]{1,0:T(8,128)(2,1)}, bf16[512,4096]{1,0:T(8,128)(2,1)}, bf16[512,1024]{1,0:T(8,128)(2,1)}, bf16[512,1024]{1,0:T(8,128)(2,1)}) %tuple.223, (s32[1]{0:T(128)}, ...), branch_computations={%region_14.15_spmd, %region_15.16_spmd} | conditional | flops 4294967296 | bytes 13631504 | solution.py:750
  307.9 8.9 %weight_grad.32 = (bf16[2,4,256,512]{3,2,1,0:T(8,128)(2,1)}, bf16[2,4,256,512]{3,2,1,0:T(8,128)(2,1)}) custom-call(s32[1]{0:T(128)} %get-tuple-element.691.refs_0_, bf16[512,4096]{1,0:T(8,128)(2,1)} %get-tuple-element.692.refs_1_, bf16[512,4096]{1,0:T(8,128)(2,1)} %get-tuple-element.693.refs_2_, bf16[512,1024]{1,0:T(8,128)(2,1)} %get-tuple-element.694.refs_3_, ...), custom_call_target="tpu_custom_call" | custom-call | flops 4294967296 | bytes 13631488 | tf_op jit(solution)/shard_map/cond/branch_0_fun/weight_grad/pallas_call | solution.py:546
  316.8 9.0 %conditional.26 = (bf16[2,4,256,512]{3,2,1,0:T(8,128)(2,1)}, bf16[8,256,512]{2,1,0:T(8,128)(2,1)}) conditional(s32[]{:T(128)} %convert_element_type.170, (s32[1]{0:T(128)}, bf16[512,4096]{1,0:T(8,128)(2,1)}, bf16[512,4096]{1,0:T(8,128)(2,1)}, bf16[512,1024]{1,0:T(8,128)(2,1)}, bf16[512,1024]{1,0:T(8,128)(2,1)}) %tuple.223, (s32[1]{0:T(128)}, ...), branch_computations={%region_16.17_spmd, %region_17.18_spmd} | conditional | flops 4294967296 | bytes 13631504 | solution.py:750
  316.8 9.0 %weight_grad.34 = (bf16[2,4,256,512]{3,2,1,0:T(8,128)(2,1)}, bf16[2,4,256,512]{3,2,1,0:T(8,128)(2,1)}) custom-call(s32[1]{0:T(128)} %get-tuple-element.701.refs_0_, bf16[512,4096]{1,0:T(8,128)(2,1)} %get-tuple-element.702.refs_1_, bf16[512,4096]{1,0:T(8,128)(2,1)} %get-tuple-element.703.refs_2_, bf16[512,1024]{1,0:T(8,128)(2,1)} %get-tuple-element.704.refs_3_, ...), custom_call_target="tpu_custom_call" | custom-call | flops 4294967296 | bytes 13631488 | tf_op jit(solution)/shard_map/cond/branch_0_fun/weight_grad/pallas_call | solution.py:546
  334.4 8.6 %conditional.29 = (bf16[8,1,64,2048]{3,2,1,0:T(8,128)(2,1)}, bf16[8,64,2048]{2,1,0:T(8,128)(2,1)}) conditional(s32[]{:T(128)} %convert_element_type.173, (s32[1]{0:T(128)}, bf16[512,1024]{1,0:T(8,128)(2,1)}, bf16[512,1024]{1,0:T(8,128)(2,1)}, bf16[512,4096]{1,0:T(8,128)(2,1)}, bf16[512,4096]{1,0:T(8,128)(2,1)}) %tuple.230, (s32[1]{0:T(128)}, ...), branch_computations={%region_22.23_spmd, %region_23.24_spmd} | conditional | flops 4294967296 | bytes 10485776 | solution.py:750
  334.4 8.6 %weight_grad.38 = (bf16[8,1,64,2048]{3,2,1,0:T(8,128)(2,1)}, bf16[8,1,64,2048]{3,2,1,0:T(8,128)(2,1)}) custom-call(s32[1]{0:T(128)} %get-tuple-element.734.refs_0_, bf16[512,1024]{1,0:T(8,128)(2,1)} %get-tuple-element.735.refs_1_, bf16[512,1024]{1,0:T(8,128)(2,1)} %get-tuple-element.736.refs_2_, bf16[512,4096]{1,0:T(8,128)(2,1)} %get-tuple-element.737.refs_3_, ...), custom_call_target="tpu_custom_call" | custom-call | flops 4294967296 | bytes 10485760 | tf_op jit(solution)/shard_map/cond/branch_0_fun/weight_grad/pallas_call | solution.py:546
  351.1 11.9 %conditional.32 = (bf16[8,1,64,1024]{3,2,1,0:T(8,128)(2,1)}, bf16[8,64,1024]{2,1,0:T(8,128)(2,1)}) conditional(s32[]{:T(128)} %convert_element_type.176, (s32[1]{0:T(128)}, bf16[512,1024]{1,0:T(8,128)(2,1)}, bf16[512,1024]{1,0:T(8,128)(2,1)}, bf16[2,1024,1024]{2,1,0:T(8,128)(2,1)}, bf16[512,1024]{1,0:T(8,128)(2,1)S(1)}, ...), branch_computations={%region_28.29_spmd, %region_29.30_spmd} | conditional | flops 6442450944 | bytes 14680080 | solution.py:750
  351.1 11.7 %weight_grad.42 = (bf16[8,1,64,1024]{3,2,1,0:T(8,128)(2,1)}, bf16[8,1,64,1024]{3,2,1,0:T(8,128)(2,1)}) custom-call(s32[1]{0:T(128)} %get-tuple-element.773.refs_0_, bf16[512,1024]{1,0:T(8,128)(2,1)} %get-tuple-element.774.refs_1_, bf16[512,1024]{1,0:T(8,128)(2,1)} %get-tuple-element.775.refs_2_, bf16[2,1024,1024]{2,1,0:T(8,128)(2,1)} %get-tuple-element.776.refs_3_.refs_4_, ...), custom_call_target="tpu_custom_call" | custom-call | flops 6442450944 | bytes 14680064 | tf_op jit(solution)/shard_map/cond/branch_0_fun/weight_grad/pallas_call | solution.py:546
  363.0 11.7 %conditional.33 = (bf16[8,1,64,1024]{3,2,1,0:T(8,128)(2,1)}, bf16[8,64,1024]{2,1,0:T(8,128)(2,1)}) conditional(s32[]{:T(128)} %convert_element_type.177, (s32[1]{0:T(128)}, bf16[512,1024]{1,0:T(8,128)(2,1)}, bf16[512,1024]{1,0:T(8,128)(2,1)}, bf16[2,1024,1024]{2,1,0:T(8,128)(2,1)}, bf16[512,1024]{1,0:T(8,128)(2,1)S(1)}, ...), branch_computations={%region_30.31_spmd, %region_31.32_spmd} | conditional | flops 6442450944 | bytes 14680080 | solution.py:750
  363.0 11.7 %weight_grad.44 = (bf16[8,1,64,1024]{3,2,1,0:T(8,128)(2,1)}, bf16[8,1,64,1024]{3,2,1,0:T(8,128)(2,1)}) custom-call(s32[1]{0:T(128)} %get-tuple-element.789.refs_0_, bf16[512,1024]{1,0:T(8,128)(2,1)} %get-tuple-element.790.refs_1_, bf16[512,1024]{1,0:T(8,128)(2,1)} %get-tuple-element.791.refs_2_, bf16[2,1024,1024]{2,1,0:T(8,128)(2,1)} %get-tuple-element.792.refs_3_.refs_4_, ...), custom_call_target="tpu_custom_call" | custom-call | flops 6442450944 | bytes 14680064 | tf_op jit(solution)/shard_map/cond/branch_0_fun/weight_grad/pallas_call | solution.py:546
  384.8 59.7 %collective-permute-done.9 = bf16[512,512]{1,0:T(8,128)(2,1)S(1)} collective-permute-done((bf16[512,512]{1,0:T(8,128)(2,1)S(1)}, bf16[512,512]{1,0:T(8,128)(2,1)S(1)}, u32[]{:S(2)}, u32[]{:S(2)}) %collective-permute-start.9) | collective-permute-done | bytes 524320 | tf_op jit(solution)/shard_map/ppermute | solution.py:605
  460.4 8.6 %collective-permute-done.19.got_a.got_b = bf16[4,64,1024]{2,1,0:T(8,128)(2,1)S(1)} collective-permute-done((bf16[4,64,1024]{2,1,0:T(8,128)(2,1)}, bf16[4,64,1024]{2,1,0:T(8,128)(2,1)S(1)}, u32[]{:S(2)}, u32[]{:S(2)}) %collective-permute-start.19) | collective-permute-done | bytes 524320 | tf_op jit(solution)/shard_map/ppermute | solution.py:593
  558.1 18.7 %collective-permute-done.39.got_a.got_b = bf16[4,256,512]{2,1,0:T(8,128)(2,1)S(1)} collective-permute-done((bf16[4,256,512]{2,1,0:T(8,128)(2,1)}, bf16[4,256,512]{2,1,0:T(8,128)(2,1)S(1)}, u32[]{:S(2)}, u32[]{:S(2)}) %collective-permute-start.39) | collective-permute-done | bytes 1048608 | tf_op jit(solution)/shard_map/ppermute | solution.py:593
  580.6 16.9 %collective-permute-done.35.got_a.got_b = bf16[4,256,512]{2,1,0:T(8,128)(2,1)S(1)} collective-permute-done((bf16[4,256,512]{2,1,0:T(8,128)(2,1)}, bf16[4,256,512]{2,1,0:T(8,128)(2,1)S(1)}, u32[]{:S(2)}, u32[]{:S(2)}) %collective-permute-start.35) | collective-permute-done | bytes 1048608 | tf_op jit(solution)/shard_map/ppermute | solution.py:593
  612.4 16.1 %collective-permute-done.25 = bf16[1,80,1024]{2,1,0:T(8,128)(2,1)S(1)} collective-permute-done((bf16[1,80,1024]{2,1,0:T(8,128)(2,1)}, bf16[1,80,1024]{2,1,0:T(8,128)(2,1)S(1)}, u32[]{:S(2)}, u32[]{:S(2)}) %collective-permute-start.25) | collective-permute-done | bytes 163872 | tf_op jit(solution)/shard_map/ppermute | solution.py:593
  (319 shorter events, 289.9 us)
Async XLA Ops:
  3.2 23.1 %collective-permute-start = (bf16[512,512]{1,0:T(8,128)(2,1)}, bf16[512,512]{1,0:T(8,128)(2,1)}, u32[]{:S(2)}, u32[]{:S(2)}) collective-permute-start(bf16[512,512]{1,0:T(8,128)(2,1)} %get-tuple-element.1205), channel_id=1, source_target_pairs={{0,1},{1,0},{2,3},{3,2},{4,5},{5,4},{6,7},{7,6},{8,9},{9,8},{10,11... | collective-permute-start | bytes 1572872 | tf_op jit(solution)/shard_map/ppermute | solution.py:659
  3.7 24.7 %collective-permute-start.1 = (bf16[512,512]{1,0:T(8,128)(2,1)}, bf16[512,512]{1,0:T(8,128)(2,1)}, u32[]{:S(2)}, u32[]{:S(2)}) collective-permute-start(bf16[512,512]{1,0:T(8,128)(2,1)} %get-tuple-element.1204), channel_id=1, source_target_pairs={{0,1},{1,0},{2,3},{3,2},{4,5},{5,4},{6,7},{7,6},{8,9},{9,8},{10,11... | collective-permute-start | bytes 1572872 | tf_op jit(solution)/shard_map/ppermute | solution.py:659
  40.0 55.6 %collective-permute-start.2 = (bf16[512,1024]{1,0:T(8,128)(2,1)}, bf16[512,1024]{1,0:T(8,128)(2,1)}, u32[]{:S(2)}, u32[]{:S(2)}) collective-permute-start(bf16[512,1024]{1,0:T(8,128)(2,1)} %get-tuple-element.1001), channel_id=1, source_target_pairs={{0,1},{2,3},{4,5},{6,7},{8,9},{10,11},{12,13},{14,15},{16,17},{18,... | collective-permute-start | bytes 3145736 | tf_op jit(solution)/shard_map/ppermute | solution.py:605
  47.3 89.5 %collective-permute-start.4 = (bf16[512,1024]{1,0:T(8,128)(2,1)}, bf16[512,1024]{1,0:T(8,128)(2,1)}, u32[]{:S(2)}, u32[]{:S(2)}) collective-permute-start(bf16[512,1024]{1,0:T(8,128)(2,1)} %get-tuple-element.1005), channel_id=1, source_target_pairs={{0,1},{2,3},{4,5},{6,7},{8,9},{10,11},{12,13},{14,15},{16,17},{18,... | collective-permute-start | bytes 3145736 | tf_op jit(solution)/shard_map/ppermute | solution.py:605
  228.4 64.6 %collective-permute-start.6 = (bf16[512,1024]{1,0:T(8,128)(2,1)}, bf16[512,1024]{1,0:T(8,128)(2,1)}, u32[]{:S(2)}, u32[]{:S(2)}) collective-permute-start(bf16[512,1024]{1,0:T(8,128)(2,1)} %get-tuple-element.1014), channel_id=1, source_target_pairs={{1,0},{3,2},{5,4},{7,6},{9,8},{11,10},{13,12},{15,14},{17,16},{19,... | collective-permute-start | bytes 3145736 | tf_op jit(solution)/shard_map/ppermute | solution.py:605
  282.6 25.3 %collective-permute-start.8 = (bf16[512,1024]{1,0:T(8,128)(2,1)}, bf16[512,1024]{1,0:T(8,128)(2,1)}, u32[]{:S(2)}, u32[]{:S(2)}) collective-permute-start(bf16[512,1024]{1,0:T(8,128)(2,1)} %get-tuple-element.1021), channel_id=1, source_target_pairs={{1,0},{3,2},{5,4},{7,6},{9,8},{11,10},{13,12},{15,14},{17,16},{19,... | collective-permute-start | bytes 3145736 | tf_op jit(solution)/shard_map/ppermute | solution.py:605
  286.9 97.4 %collective-permute-start.5 = (bf16[512,512]{1,0:T(8,128)(2,1)}, bf16[512,512]{1,0:T(8,128)(2,1)}, u32[]{:S(2)}, u32[]{:S(2)}) collective-permute-start(bf16[512,512]{1,0:T(8,128)(2,1)} %slice.77), channel_id=1, source_target_pairs={{1,0},{3,2},{5,4},{7,6},{9,8},{11,10},{13,12},{15,14},{17,16},{19,... | collective-permute-start | bytes 1572872 | tf_op jit(solution)/shard_map/ppermute | solution.py:605
  290.8 93.9 %collective-permute-start.3 = (bf16[512,512]{1,0:T(8,128)(2,1)}, bf16[512,512]{1,0:T(8,128)(2,1)}, u32[]{:S(2)}, u32[]{:S(2)}) collective-permute-start(bf16[512,512]{1,0:T(8,128)(2,1)} %slice.75), channel_id=1, source_target_pairs={{1,0},{3,2},{5,4},{7,6},{9,8},{11,10},{13,12},{15,14},{17,16},{19,... | collective-permute-start | bytes 1572872 | tf_op jit(solution)/shard_map/ppermute | solution.py:605
  380.5 64.0 %collective-permute-start.9 = (bf16[512,512]{1,0:T(8,128)(2,1)S(1)}, bf16[512,512]{1,0:T(8,128)(2,1)S(1)}, u32[]{:S(2)}, u32[]{:S(2)}) collective-permute-start(bf16[512,512]{1,0:T(8,128)(2,1)S(1)} %slice.92), channel_id=1, source_target_pairs={{0,1},{2,3},{4,5},{6,7},{8,9},{10,11},{12,13},{14,15},{16,17},{18,... | collective-permute-start | bytes 1572872 | tf_op jit(solution)/shard_map/ppermute | solution.py:605
  382.9 67.4 %collective-permute-start.7 = (bf16[512,512]{1,0:T(8,128)(2,1)S(1)}, bf16[512,512]{1,0:T(8,128)(2,1)S(1)}, u32[]{:S(2)}, u32[]{:S(2)}) collective-permute-start(bf16[512,512]{1,0:T(8,128)(2,1)S(1)} %slice.82), channel_id=1, source_target_pairs={{0,1},{2,3},{4,5},{6,7},{8,9},{10,11},{12,13},{14,15},{16,17},{18,... | collective-permute-start | bytes 1572872 | tf_op jit(solution)/shard_map/ppermute | solution.py:605
  384.2 66.1 %collective-permute-start.18 = (bf16[8,64,1024]{2,1,0:T(8,128)(2,1)}, bf16[8,64,1024]{2,1,0:T(8,128)(2,1)S(1)}, u32[]{:S(2)}, u32[]{:S(2)}) collective-permute-start(bf16[8,64,1024]{2,1,0:T(8,128)(2,1)} %bitcast.48), channel_id=1, source_target_pairs={{0,2},{2,0},{4,6},{6,4},{8,10},{10,8},{12,14},{14,12},{16,18},{18,... | collective-permute-start | bytes 3145736 | tf_op jit(solution)/shard_map/ppermute | solution.py:593
  384.2 67.5 %collective-permute-start.14 = (bf16[8,64,1024]{2,1,0:T(8,128)(2,1)}, bf16[8,64,1024]{2,1,0:T(8,128)(2,1)}, u32[]{:S(2)}, u32[]{:S(2)}) collective-permute-start(bf16[8,64,1024]{2,1,0:T(8,128)(2,1)} %bitcast.46), channel_id=1, source_target_pairs={{0,2},{2,0},{4,6},{6,4},{8,10},{10,8},{12,14},{14,12},{16,18},{18,... | collective-permute-start | bytes 3145736 | tf_op jit(solution)/shard_map/ppermute | solution.py:593
  384.7 67.1 %collective-permute-start.10 = (bf16[8,64,1024]{2,1,0:T(8,128)(2,1)}, bf16[8,64,1024]{2,1,0:T(8,128)(2,1)}, u32[]{:S(2)}, u32[]{:S(2)}) collective-permute-start(bf16[8,64,1024]{2,1,0:T(8,128)(2,1)} %bitcast.44), channel_id=1, source_target_pairs={{0,2},{2,0},{4,6},{6,4},{8,10},{10,8},{12,14},{14,12},{16,18},{18,... | collective-permute-start | bytes 3145736 | tf_op jit(solution)/shard_map/ppermute | solution.py:593
  450.2 25.8 %collective-permute-start.30 = (bf16[8,64,2048]{2,1,0:T(8,128)(2,1)}, bf16[8,64,2048]{2,1,0:T(8,128)(2,1)}, u32[]{:S(2)}, u32[]{:S(2)}) collective-permute-start(bf16[8,64,2048]{2,1,0:T(8,128)(2,1)} %bitcast.56), channel_id=1, source_target_pairs={{0,2},{2,0},{4,6},{6,4},{8,10},{10,8},{12,14},{14,12},{16,18},{18,... | collective-permute-start | bytes 6291464 | tf_op jit(solution)/shard_map/ppermute | solution.py:593
  451.4 52.9 %collective-permute-start.26 = (bf16[8,64,2048]{2,1,0:T(8,128)(2,1)}, bf16[8,64,2048]{2,1,0:T(8,128)(2,1)S(1)}, u32[]{:S(2)}, u32[]{:S(2)}) collective-permute-start(bf16[8,64,2048]{2,1,0:T(8,128)(2,1)} %bitcast.54), channel_id=1, source_target_pairs={{0,2},{2,0},{4,6},{6,4},{8,10},{10,8},{12,14},{14,12},{16,18},{18,... | collective-permute-start | bytes 6291464 | tf_op jit(solution)/shard_map/ppermute | solution.py:593
  451.7 53.0 %collective-permute-start.38 = (bf16[8,256,512]{2,1,0:T(8,128)(2,1)}, bf16[8,256,512]{2,1,0:T(8,128)(2,1)}, u32[]{:S(2)}, u32[]{:S(2)}) collective-permute-start(bf16[8,256,512]{2,1,0:T(8,128)(2,1)} %bitcast.64), channel_id=1, source_target_pairs={{0,2},{2,0},{4,6},{6,4},{8,10},{10,8},{12,14},{14,12},{16,18},{18,... | collective-permute-start | bytes 6291464 | tf_op jit(solution)/shard_map/ppermute | solution.py:593
  451.9 54.5 %collective-permute-start.34 = (bf16[8,256,512]{2,1,0:T(8,128)(2,1)}, bf16[8,256,512]{2,1,0:T(8,128)(2,1)}, u32[]{:S(2)}, u32[]{:S(2)}) collective-permute-start(bf16[8,256,512]{2,1,0:T(8,128)(2,1)} %bitcast.62), channel_id=1, source_target_pairs={{0,2},{2,0},{4,6},{6,4},{8,10},{10,8},{12,14},{14,12},{16,18},{18,... | collective-permute-start | bytes 6291464 | tf_op jit(solution)/shard_map/ppermute | solution.py:593
  476.1 19.3 %collective-permute-start.11 = (bf16[4,64,1024]{2,1,0:T(8,128)(2,1)}, bf16[4,64,1024]{2,1,0:T(8,128)(2,1)S(1)}, u32[]{:S(2)}, u32[]{:S(2)}) collective-permute-start(bf16[4,64,1024]{2,1,0:T(8,128)(2,1)} %get-tuple-element.1104), channel_id=1, source_target_pairs={{0,4},{2,6},{4,0},{6,2},{8,12},{10,14},{12,8},{14,10},{16,20},{18,... | collective-permute-start | bytes 1572872 | tf_op jit(solution)/shard_map/ppermute | solution.py:593
  484.1 57.8 %collective-permute-start.31 = (bf16[4,64,2048]{2,1,0:T(8,128)(2,1)}, bf16[4,64,2048]{2,1,0:T(8,128)(2,1)S(1)}, u32[]{:S(2)}, u32[]{:S(2)}) collective-permute-start(bf16[4,64,2048]{2,1,0:T(8,128)(2,1)} %get-tuple-element.1139), channel_id=1, source_target_pairs={{0,4},{2,6},{4,0},{6,2},{8,12},{10,14},{12,8},{14,10},{16,20},{18,... | collective-permute-start | bytes 3145736 | tf_op jit(solution)/shard_map/ppermute | solution.py:593
  495.4 36.5 %collective-permute-start.23 = (bf16[4,80,1024]{2,1,0:T(8,128)(2,1)}, bf16[4,80,1024]{2,1,0:T(8,128)(2,1)S(1)}, u32[]{:S(2)}, u32[]{:S(2)}) collective-permute-start(bf16[4,80,1024]{2,1,0:T(8,128)(2,1)} %get-tuple-element.1125), channel_id=1, source_target_pairs={{0,4},{2,6},{4,0},{6,2},{8,12},{10,14},{12,8},{14,10},{16,20},{18,... | collective-permute-start | bytes 1966088 | tf_op jit(solution)/shard_map/ppermute | solution.py:593
  517.1 37.3 %collective-permute-start.27 = (bf16[4,64,2048]{2,1,0:T(8,128)(2,1)}, bf16[4,64,2048]{2,1,0:T(8,128)(2,1)S(1)}, u32[]{:S(2)}, u32[]{:S(2)}) collective-permute-start(bf16[4,64,2048]{2,1,0:T(8,128)(2,1)} %get-tuple-element.1132), channel_id=1, source_target_pairs={{0,4},{2,6},{4,0},{6,2},{8,12},{10,14},{12,8},{14,10},{16,20},{18,... | collective-permute-start | bytes 3145736 | tf_op jit(solution)/shard_map/ppermute | solution.py:593
  517.8 59.1 %collective-permute-start.39 = (bf16[4,256,512]{2,1,0:T(8,128)(2,1)}, bf16[4,256,512]{2,1,0:T(8,128)(2,1)S(1)}, u32[]{:S(2)}, u32[]{:S(2)}) collective-permute-start(bf16[4,256,512]{2,1,0:T(8,128)(2,1)} %get-tuple-element.1153), channel_id=1, source_target_pairs={{0,4},{2,6},{4,0},{6,2},{8,12},{10,14},{12,8},{14,10},{16,20},{18,... | collective-permute-start | bytes 3145736 | tf_op jit(solution)/shard_map/ppermute | solution.py:593
  520.2 77.4 %collective-permute-start.35 = (bf16[4,256,512]{2,1,0:T(8,128)(2,1)}, bf16[4,256,512]{2,1,0:T(8,128)(2,1)S(1)}, u32[]{:S(2)}, u32[]{:S(2)}) collective-permute-start(bf16[4,256,512]{2,1,0:T(8,128)(2,1)} %get-tuple-element.1146), channel_id=1, source_target_pairs={{0,4},{2,6},{4,0},{6,2},{8,12},{10,14},{12,8},{14,10},{16,20},{18,... | collective-permute-start | bytes 3145736 | tf_op jit(solution)/shard_map/ppermute | solution.py:593
  549.1 58.1 %collective-permute-start.32 = (bf16[2,64,2048]{2,1,0:T(8,128)(2,1)}, bf16[2,64,2048]{2,1,0:T(8,128)(2,1)S(1)}, u32[]{:S(2)}, u32[]{:S(2)}) collective-permute-start(bf16[2,64,2048]{2,1,0:T(8,128)(2,1)} %get-tuple-element.1141), channel_id=1, source_target_pairs={{0,8},{2,10},{4,12},{6,14},{8,0},{10,2},{12,4},{14,6},{16,24},{18,... | collective-permute-start | bytes 1572872 | tf_op jit(solution)/shard_map/ppermute | solution.py:593
  550.5 52.9 %collective-permute-start.24 = (bf16[2,80,1024]{2,1,0:T(8,128)(2,1)S(1)}, bf16[2,80,1024]{2,1,0:T(8,128)(2,1)S(1)}, u32[]{:S(2)}, u32[]{:S(2)}) collective-permute-start(bf16[2,80,1024]{2,1,0:T(8,128)(2,1)S(1)} %copy-done.60), channel_id=1, source_target_pairs={{0,8},{2,10},{4,12},{6,14},{8,0},{10,2},{12,4},{14,6},{16,24},{18,... | collective-permute-start | bytes 983048 | tf_op jit(solution)/shard_map/ppermute | solution.py:593
  557.7 72.6 %collective-permute-start.28 = (bf16[2,64,2048]{2,1,0:T(8,128)(2,1)}, bf16[2,64,2048]{2,1,0:T(8,128)(2,1)S(1)}, u32[]{:S(2)}, u32[]{:S(2)}) collective-permute-start(bf16[2,64,2048]{2,1,0:T(8,128)(2,1)} %get-tuple-element.1134), channel_id=1, source_target_pairs={{0,8},{2,10},{4,12},{6,14},{8,0},{10,2},{12,4},{14,6},{16,24},{18,... | collective-permute-start | bytes 1572872 | tf_op jit(solution)/shard_map/ppermute | solution.py:593
  580.2 52.9 %collective-permute-start.40 = (bf16[2,256,512]{2,1,0:T(8,128)(2,1)}, bf16[2,256,512]{2,1,0:T(8,128)(2,1)S(1)}, u32[]{:S(2)}, u32[]{:S(2)}) collective-permute-start(bf16[2,256,512]{2,1,0:T(8,128)(2,1)} %get-tuple-element.1155), channel_id=1, source_target_pairs={{0,8},{2,10},{4,12},{6,14},{8,0},{10,2},{12,4},{14,6},{16,24},{18,... | collective-permute-start | bytes 1572872 | tf_op jit(solution)/shard_map/ppermute | solution.py:593
  600.9 38.0 %collective-permute-start.36 = (bf16[2,256,512]{2,1,0:T(8,128)(2,1)}, bf16[2,256,512]{2,1,0:T(8,128)(2,1)S(1)}, u32[]{:S(2)}, u32[]{:S(2)}) collective-permute-start(bf16[2,256,512]{2,1,0:T(8,128)(2,1)} %get-tuple-element.1148), channel_id=1, source_target_pairs={{0,8},{2,10},{4,12},{6,14},{8,0},{10,2},{12,4},{14,6},{16,24},{18,... | collective-permute-start | bytes 1572872 | tf_op jit(solution)/shard_map/ppermute | solution.py:593
  606.0 22.4 %collective-permute-start.25 = (bf16[1,80,1024]{2,1,0:T(8,128)(2,1)}, bf16[1,80,1024]{2,1,0:T(8,128)(2,1)S(1)}, u32[]{:S(2)}, u32[]{:S(2)}) collective-permute-start(bf16[1,80,1024]{2,1,0:T(8,128)(2,1)} %get-tuple-element.1129), channel_id=1, source_target_pairs={{0,16},{2,18},{4,20},{6,22},{8,24},{10,26},{12,28},{14,30},{16,0},... | collective-permute-start | bytes 491528 | tf_op jit(solution)/shard_map/ppermute | solution.py:593
  610.0 35.3 %collective-permute-start.33 = (bf16[1,64,2048]{2,1,0:T(8,128)(2,1)}, bf16[1,64,2048]{2,1,0:T(8,128)(2,1)S(1)}, u32[]{:S(2)}, u32[]{:S(2)}) collective-permute-start(bf16[1,64,2048]{2,1,0:T(8,128)(2,1)} %get-tuple-element.1143), channel_id=1, source_target_pairs={{0,16},{2,18},{4,20},{6,22},{8,24},{10,26},{12,28},{14,30},{16,0},... | collective-permute-start | bytes 786440 | tf_op jit(solution)/shard_map/ppermute | solution.py:593
  636.0 20.5 %collective-permute-start.41 = (bf16[1,256,512]{2,1,0:T(8,128)(2,1)}, bf16[1,256,512]{2,1,0:T(8,128)(2,1)S(1)}, u32[]{:S(2)}, u32[]{:S(2)}) collective-permute-start(bf16[1,256,512]{2,1,0:T(8,128)(2,1)} %get-tuple-element.1157), channel_id=1, source_target_pairs={{0,16},{2,18},{4,20},{6,22},{8,24},{10,26},{12,28},{14,30},{16,0},... | collective-permute-start | bytes 786440 | tf_op jit(solution)/shard_map/ppermute | solution.py:593
  641.8 19.0 %collective-permute-start.37 = (bf16[1,256,512]{2,1,0:T(8,128)(2,1)}, bf16[1,256,512]{2,1,0:T(8,128)(2,1)S(1)}, u32[]{:S(2)}, u32[]{:S(2)}) collective-permute-start(bf16[1,256,512]{2,1,0:T(8,128)(2,1)} %get-tuple-element.1150), channel_id=1, source_target_pairs={{0,16},{2,18},{4,20},{6,22},{8,24},{10,26},{12,28},{14,30},{16,0},... | collective-permute-start | bytes 786440 | tf_op jit(solution)/shard_map/ppermute | solution.py:593
  (84 other events, 911.4 us)

commit v2 on v0

v2 whole, which is shorter than its diff:
```python
import math

import jax
import jax.numpy as jnp
from jax import lax
from jax.experimental import pallas as pl
from jax.experimental.pallas import tpu as pltpu
from jax.sharding import PartitionSpec as P

WIDTH = 1024
HEADS = 8
HEAD = 128
FF = 4096
SEG = 512
MEM = 512
CMEM = 512
RATE = 2
COMP = 256
CTX = MEM + CMEM
HALF = SEG // 2
HP = 4

EPS = 1e-05
NEG = -1e30
ROOT_TWO_PI = 0.7978845608028654
SCALE = HEAD**-0.5
LOG2E = math.log2(math.e)
LN2 = math.log(2.0)
BF = jnp.bfloat16
F32 = jnp.float32
PARAMS = pltpu.CompilerParams(vmem_limit_bytes=56 << 20)


def nn(a, b):
    return lax.dot_general(a, b, (((1,), (0,)), ((), ())), preferred_element_type=F32)


def nt(a, b):
    return lax.dot_general(a, b, (((1,), (1,)), ((), ())), preferred_element_type=F32)


def tn(a, b):
    return lax.dot_general(a, b, (((0,), (0,)), ((), ())), preferred_element_type=F32)


def shape(dims, dtype=BF):
    return jax.ShapeDtypeStruct(dims, dtype)


def whole(*dims):
    return pl.BlockSpec(dims, lambda *_: (0,) * len(dims))


def cost(flops, moved, trans=0):
    return pl.CostEstimate(flops=int(flops), bytes_accessed=int(moved), transcendentals=int(trans))


LONG = cost(1e11, 1)
SHORT = cost(1, 1)


def normalise(values):
    centred = values - jnp.mean(values, axis=-1, keepdims=True)
    inverse = lax.rsqrt(jnp.mean(centred * centred, axis=-1, keepdims=True) + EPS)
    return centred * inverse, inverse


def norm_back(unit, inverse, gain, grad):
    scaled = grad * gain
    along = jnp.mean(scaled * unit, axis=-1, keepdims=True)
    return inverse * (scaled - jnp.mean(scaled, axis=-1, keepdims=True) - unit * along)


ANY = pl.BlockSpec(memory_space=pl.ANY)


def call(kernel, name, scalars, ins, outs, scratch, tokens, aliases=None, estimate=LONG, specs=None):
    first = len(scalars) + len(ins)

    def run(*refs):
        kernel(*refs[:first], *refs[first + len(tokens) :])

    return pl.pallas_call(
        run,
        name=name,
        grid_spec=pltpu.PrefetchScalarGridSpec(
            num_scalar_prefetch=len(scalars),
            grid=(1,),
            in_specs=list(specs or [ANY] * len(ins)) + [ANY] * len(tokens),
            out_specs=[ANY] * len(outs),
            scratch_shapes=scratch,
        ),
        out_shape=list(outs),
        input_output_aliases=aliases or {},
        compiler_params=PARAMS,
        cost_estimate=estimate,
    )(*scalars, *ins, *tokens)


class Copies:
    def __init__(self, sems):
        self.sems, self.count, self.named = sems, 0, {}

    def start(self, source, target, name=None):
        copy = pltpu.make_async_copy(source, target, self.sems.at[self.count])
        copy.start()
        self.named[name if name is not None else self.count] = copy
        self.count += 1

    def wait(self, *names):
        for name in names:
            self.named.pop(name).wait()

    def wait_all(self):
        for name in list(self.named):
            self.wait(name)


def tiles(ref, axis, size=1024):
    if axis == 0:
        return [ref.at[pl.ds(i * size, size)] for i in range(ref.shape[0] // size)]
    return [ref.at[:, pl.ds(i * size, size)] for i in range(ref.shape[1] // size)]


def memory_kernel(flags, comp, mem, gain, w, normed, kv, rows, weights, unit_rows, out, sems):
    copies = Copies(sems)
    seqs = comp.shape[0]
    jobs = [(s, j) for s in range(seqs) for j in range(2)]
    for n, (s, j) in enumerate(jobs):
        copies.start((comp, mem)[j].at[s], rows.at[n], ("rows", n))
        if n == 0:
            for t in range(2):
                copies.start(w.at[:, pl.ds((1 + t) * WIDTH, WIDTH)], weights.at[t], ("w", t))

    def unit(n):
        copies.wait(("rows", n))
        keep = (1 - flags[jobs[n][0]]).astype(F32)
        value, _ = normalise(rows[n].astype(F32) * keep)
        unit_rows[n] = (value * gain[...].astype(F32)).astype(BF)

    unit(0)
    for n, (s, j) in enumerate(jobs):
        place = pl.ds(j * MEM, MEM)
        copies.start(unit_rows.at[n], normed.at[s, place])
        for t in range(2):
            if n == 0:
                copies.wait(("w", t))
            out[n, :, t * WIDTH : (t + 1) * WIDTH] = nn(unit_rows[n], weights[t]).astype(BF)
            if t == 0 and n + 1 < len(jobs):
                unit(n + 1)
        copies.start(out.at[n], kv.at[s, place])
    copies.wait_all()


def memory_keyvals(flags, compressed, memory, gain, w_proj, tokens):
    seqs = memory.shape[0]
    return call(
        memory_kernel,
        "memory_keyvals",
        [flags],
        [compressed, memory, gain, w_proj],
        [shape((seqs, CTX, WIDTH)), shape((seqs, CTX, 2 * WIDTH))],
        [
            pltpu.VMEM((2 * seqs, MEM, WIDTH), BF),
            pltpu.VMEM((2, WIDTH, WIDTH), BF),
            pltpu.VMEM((2 * seqs, MEM, WIDTH), BF),
            pltpu.VMEM((2 * seqs, MEM, 2 * WIDTH), BF),
            pltpu.SemaphoreType.DMA((6 * seqs + 2,)),
        ],
        tokens,
        specs=[ANY, ANY, whole(1, WIDTH), ANY],
    )


def fill_masks(flag, bound, bias, unseen):
    key = lax.broadcasted_iota(jnp.int32, (SEG, SEG), 0)
    query = lax.broadcasted_iota(jnp.int32, (SEG, SEG), 1)
    least = jnp.where(query >= bound, bound, 0)
    bias[...] = jnp.where((key <= query) & (key >= least), 0.0, NEG)
    position = lax.broadcasted_iota(jnp.int32, (1, SEG), 1)
    limit = jnp.where(flag == 0, bound, 0)
    unseen[...] = jnp.where(position < limit, 0.0, -NEG)


def gelu_parts(v):
    inner = v * (ROOT_TWO_PI + (0.044715 * ROOT_TWO_PI) * (v * v))
    t = jnp.tanh(inner)
    half = 0.5 + 0.5 * t
    slope = 3.0 * inner - (2.0 * ROOT_TWO_PI) * v
    return v * half, half + half * (1.0 - t) * slope


def attend_heads(first, qkv, kvm, attended, log_total, bias, unseen):
    def cols(base, h):
        return pl.ds(pl.multiple_of(base * WIDTH + (first + h) * HEAD, HEAD), HEAD)

    pieces = [(h, slice(part * HALF, (part + 1) * HALF), (part + 1) * HALF) for h in range(HP) for part in range(2)]

    def scores(h, r, count):
        rows = qkv[r, cols(0, h)]
        return nt(kvm[:, cols(0, h)], rows), nt(qkv[:count, cols(1, h)], rows) + bias[:count, r]

    def weights(h, r, count, on_memory, on_segment):
        hidden = unseen[:, r]
        top = jnp.maximum(
            jnp.max(on_memory, axis=0, keepdims=True) - hidden,
            jnp.max(on_segment, axis=0, keepdims=True),
        )
        p_memory = jnp.exp2(on_memory - (top + hidden))
        p_segment = jnp.exp2(on_segment - top)
        total = jnp.sum(p_memory, axis=0, keepdims=True) + jnp.sum(p_segment, axis=0, keepdims=True)
        log_total[first + h, :, r] = top + jnp.log2(total)
        return p_memory.astype(BF), p_segment.astype(BF), total

    values = {}

    def finish(h, r, count, p_memory, p_segment, total):
        if h not in values:
            values[h] = (kvm[:, cols(1, h)].T, qkv[:, cols(2, h)].T)
        turned = nn(values[h][0], p_memory) + nn(values[h][1][:, :count], p_segment)
        attended[r, cols(0, h)] = (turned * (1.0 / total)).T.astype(BF)

    held, ready = {}, {}
    for step in range(len(pieces) + 2):
        if step < len(pieces):
            held[step] = scores(*pieces[step])
        if 0 <= step - 1 < len(pieces):
            ready[step - 1] = weights(*pieces[step - 1], *held.pop(step - 1))
        if 0 <= step - 2 < len(pieces):
            finish(*pieces[step - 2], *ready.pop(step - 2))


SAVED = (
    ("x", (SEG, WIDTH), BF),
    ("normed", (SEG, WIDTH), BF),
    ("qkv", (SEG, 3 * WIDTH), BF),
    ("attended", (SEG, WIDTH), BF),
    ("log_total", (HEADS, 1, SEG), F32),
    ("residual", (SEG, WIDTH), F32),
    ("ffn_in", (SEG, WIDTH), BF),
    ("hidden", (SEG, FF), BF),
    ("gate", (SEG, FF), BF),
    ("y_low", (SEG, WIDTH // 2), BF),
    ("y_high", (SEG, WIDTH // 2), BF),
)
FS = 512


def forward_kernel(seq, parts, aliased, active, flags, bounds, *refs):
    xs, refs = refs[: len(parts)], refs[len(parts) :]
    (gain, w_proj, kv_memory, w_out, gain_ffn, w_up, b_up, w_down, b_down), refs = refs[:9], refs[9:]
    refs = refs[aliased:]
    y, refs = refs[0], refs[1:]
    out = dict(zip([name for name, _, _ in SAVED], refs))
    refs = refs[len(SAVED) :]
    held = dict(zip([name for name, _, _ in SAVED], refs))
    pool, kvm, wo, total, y_rows, bias, unseen, in_sems, out_sems, feed_sems = refs[len(SAVED) :]

    @pl.when(active[0] == 1)
    def _():
        loads, stores = Copies(in_sems), Copies(out_sems)

        def save(*names):
            for name in names:
                stores.start(held[name], out[name].at[seq])

        x = held["x"]
        for i, (part, lead) in enumerate(zip(xs, parts)):
            wide = WIDTH // len(parts)
            loads.start(part if lead is None else part.at[lead], x.at[:, pl.ds(i * wide, wide)], ("x", i))
        for t, tile in enumerate(tiles(w_proj, 1)):
            loads.start(tile, pool.at[t], ("proj", t))
        loads.start(kv_memory.at[seq], kvm, "kvm")
        loads.start(w_out, wo, "out")
        for t, tile in enumerate(tiles(w_up, 1)):
            loads.start(tile, pool.at[4 + t], ("up", t))
        fill_masks(flags[seq], bounds[seq], bias, unseen)
        loads.wait(*[("x", i) for i in range(len(parts))])
        unit, _ = normalise(x[...].astype(F32))
        held["normed"][...] = (unit * gain[...].astype(F32)).astype(BF)
        for t in range(3):
            loads.wait(("proj", t))
            factor = SCALE * LOG2E if t == 0 else 1.0
            held["qkv"][:, t * WIDTH : (t + 1) * WIDTH] = (nn(held["normed"][...], pool[t]) * factor).astype(BF)
        for t, tile in enumerate(tiles(w_down, 0)):
            loads.start(tile, pool.at[t], ("down", t))
        save("x", "normed", "qkv")
        loads.wait("kvm")

        def heads(g, _):
            attend_heads(g * HP, held["qkv"], kvm, held["attended"], held["log_total"], bias, unseen)
            return 0

        lax.fori_loop(0, HEADS // HP, heads, 0)
        save("attended", "log_total")
        loads.wait("out")
        rows = x[...].astype(F32) + nn(held["attended"][...], wo[...])
        held["residual"][...] = rows
        unit, _ = normalise(rows)
        held["ffn_in"][...] = (unit * gain_ffn[...].astype(F32)).astype(BF)
        save("residual", "ffn_in")
        total[...] = rows + b_down[...].astype(F32)
        loads.wait_all()

        def feed(t, _):
            cuts = [pl.ds(pl.multiple_of(t * 1024 + i * FS, FS), FS) for i in range(1024 // FS)]
            ups = [
                nn(held["ffn_in"][...], pool[4 + t, :, i * FS : (i + 1) * FS]) + b_up[:, c].astype(F32)
                for i, c in enumerate(cuts)
            ]
            added = None
            for i, (c, up) in enumerate(zip(cuts, ups)):
                value, slope = gelu_parts(up)
                value = value.astype(BF)
                held["hidden"][:, c] = value
                held["gate"][:, c] = slope.astype(BF)
                part = nn(value, pool[t, i * FS : (i + 1) * FS])
                added = part if added is None else added + part
            total[...] += added
            for name, sem in (("hidden", 0), ("gate", 1)):
                feed_copy(name, sem, t).start()
            return 0

        def feed_copy(name, sem, t):
            place = pl.ds(pl.multiple_of(t * 1024, 1024), 1024)
            return pltpu.make_async_copy(held[name].at[:, place], out[name].at[seq, :, place], feed_sems.at[sem, t])

        lax.fori_loop(0, FF // 1024, feed, 0)
        rows = total[...].astype(BF)
        y_rows[...] = rows
        held["y_low"][...] = rows[:, : WIDTH // 2]
        held["y_high"][...] = rows[:, WIDTH // 2 :]
        stores.start(y_rows, y)
        save("y_low", "y_high")
        for t in range(FF // 1024):
            feed_copy("hidden", 0, t).wait()
            feed_copy("gate", 1, t).wait()
        stores.wait_all()


def forward(seq, seqs, scalars, xs, kv_memory, params, saved, tokens):
    gain_attn, w_proj, w_out, gain_ffn, w_up, b_up, w_down, b_down = params
    args = [v for v, _ in xs] + [gain_attn, w_proj, kv_memory, w_out, gain_ffn, w_up, b_up, w_down, b_down]
    specs = [ANY] * len(xs) + [
        whole(1, WIDTH), ANY, ANY, ANY, whole(1, WIDTH), ANY, whole(1, FF), ANY, whole(1, WIDTH)
    ]
    aliases = {}
    if saved is not None:
        aliases = {len(scalars) + len(args) + i: 1 + i for i in range(len(SAVED))}
        args += [saved[name] for name, _, _ in SAVED]
        specs += [ANY] * len(SAVED)
    leads = [lead for _, lead in xs]
    results = call(
        lambda *refs: forward_kernel(seq, leads, len(aliases), *refs),
        "forward",
        scalars,
        args,
        [shape((SEG, WIDTH))] + [shape((seqs,) + dims, dtype) for _, dims, dtype in SAVED],
        [pltpu.VMEM(dims, dtype) for _, dims, dtype in SAVED]
        + [
            pltpu.VMEM((8, WIDTH, WIDTH), BF),
            pltpu.VMEM((CTX, 2 * WIDTH), BF),
            pltpu.VMEM((WIDTH, WIDTH), BF),
            pltpu.VMEM((SEG, WIDTH), F32),
            pltpu.VMEM((SEG, WIDTH), BF),
            pltpu.VMEM((SEG, SEG), F32),
            pltpu.VMEM((1, SEG), F32),
            pltpu.SemaphoreType.DMA((16,)),
            pltpu.SemaphoreType.DMA((14,)),
            pltpu.SemaphoreType.DMA((2, FF // 1024)),
        ],
        tokens,
        aliases,
        specs=specs,
    )
    return results[0], dict(zip([name for name, _, _ in SAVED], results[1:]))


FED = (
    ("d_hidden", (SEG, FF), BF),
    ("d_residual", (SEG, WIDTH), F32),
    ("low", (SEG, WIDTH), BF),
    ("d_attended", (SEG, WIDTH), BF),
    ("d_up", (1, FF), F32),
    ("d_down", (1, WIDTH), F32),
)


def feed_back_kernel(seq, leads, aliased, active, *refs):
    gys, refs = refs[: len(leads)], refs[len(leads) :]
    (w_down, gate, w_up, residual, gain, w_out), refs = refs[:6], refs[6:]
    refs = refs[aliased:]
    out = dict(zip([name for name, _, _ in FED], refs))
    refs = refs[len(FED) :]
    held = dict(zip([name for name, _, _ in FED], refs))
    gy_rows, pool, gates, rows, wo, total, in_sems, out_sems = refs[len(FED) :]

    @pl.when(active[0] == 1)
    def _():
        loads, stores = Copies(in_sems), Copies(out_sems)
        for i, (part, lead) in enumerate(zip(gys, leads)):
            wide = WIDTH // len(leads)
            loads.start(part if lead is None else part.at[lead], gy_rows.at[:, pl.ds(i * wide, wide)], ("gy", i))
        downs, ups = tiles(w_down, 0), tiles(w_up, 1)
        for t in range(FF // 1024):
            loads.start(downs[t], pool.at[t], ("down", t))
            loads.start(gate.at[seq, :, pl.ds(t * 1024, 1024)], gates.at[:, pl.ds(t * 1024, 1024)], ("gate", t))
            loads.start(ups[t], pool.at[4 + t], ("up", t))
        loads.start(residual.at[seq], rows, "rows")
        loads.start(w_out, wo, "out")
        loads.wait(*[("gy", i) for i in range(len(leads))])
        held["d_down"][...] = jnp.sum(gy_rows[...].astype(F32), axis=0, keepdims=True)
        for t in range(FF // 1024):
            loads.wait(("down", t), ("gate", t), ("up", t))
            raws = [nt(gy_rows[...], pool[t, i * FS : (i + 1) * FS]) for i in range(1024 // FS)]
            added = None
            for i, raw in enumerate(raws):
                c = slice(t * 1024 + i * FS, t * 1024 + (i + 1) * FS)
                value = (raw * gates[:, c].astype(F32)).astype(BF)
                held["d_hidden"][:, c] = value
                held["d_up"][:, c] = jnp.sum(value.astype(F32), axis=0, keepdims=True)
                part = nt(value, pool[4 + t, :, i * FS : (i + 1) * FS])
                added = part if added is None else added + part
            total[...] = added if t == 0 else total[...] + added
        for name in ("d_hidden", "d_up", "d_down"):
            stores.start(held[name], out[name].at[seq])
        loads.wait("rows", "out")
        unit, inverse = normalise(rows[...])
        grad = gy_rows[...].astype(F32) + norm_back(unit, inverse, gain[...].astype(F32), total[...])
        held["d_residual"][...] = grad
        held["low"][...] = grad.astype(BF)
        held["d_attended"][...] = nt(held["low"][...], wo[...]).astype(BF)
        for name in ("d_residual", "low", "d_attended"):
            stores.start(held[name], out[name].at[seq])
        stores.wait_all()


def feed_back(seq, scalars, gys, saved, params, fed, tokens):
    gain_attn, w_proj, w_out, gain_ffn, w_up, b_up, w_down, b_down = params
    seqs = saved["gate"].shape[0]
    args = [v for v, _ in gys] + [w_down, saved["gate"], w_up, saved["residual"], gain_ffn, w_out]
    specs = [ANY] * (len(gys) + 4) + [whole(1, WIDTH), ANY]
    aliases = {}
    if fed is not None:
        aliases = {len(scalars) + len(args) + i: i for i in range(len(FED))}
        args += [fed[name] for name, _, _ in FED]
        specs += [ANY] * len(FED)
    leads = [lead for _, lead in gys]
    results = call(
        lambda *refs: feed_back_kernel(seq, leads, len(aliases), *refs),
        "feed_back",
        scalars,
        args,
        [shape((seqs,) + dims, dtype) for _, dims, dtype in FED],
        [pltpu.VMEM(dims, dtype) for _, dims, dtype in FED]
        + [
            pltpu.VMEM((SEG, WIDTH), BF),
            pltpu.VMEM((8, WIDTH, WIDTH), BF),
            pltpu.VMEM((SEG, FF), BF),
            pltpu.VMEM((SEG, WIDTH), F32),
            pltpu.VMEM((WIDTH, WIDTH), BF),
            pltpu.VMEM((SEG, WIDTH), F32),
            pltpu.SemaphoreType.DMA((16,)),
            pltpu.SemaphoreType.DMA((8,)),
        ],
        tokens,
        aliases,
        specs=specs,
    )
    return dict(zip([name for name, _, _ in FED], results))


MADE = (
    ("dq", (SEG, WIDTH), BF),
    ("dkx", (SEG, WIDTH), BF),
    ("dvx", (SEG, WIDTH), BF),
    ("dkm", (CTX, WIDTH), BF),
    ("dvm", (CTX, WIDTH), BF),
    ("dx_low", (SEG, WIDTH // 2), BF),
    ("dx_high", (SEG, WIDTH // 2), BF),
)
GROUP = 2


def attend_back_heads(first, qkv, kvm, d_out, out, log_total, made, bias, unseen):
    every, low, high = slice(0, SEG), slice(0, HALF), slice(HALF, SEG)

    def cols(base, h):
        return pl.ds(pl.multiple_of(base * WIDTH + (first + h) * HEAD, HEAD), HEAD)

    for h in range(GROUP):
        c = cols(0, h)
        qh, gh = qkv[:, c], d_out[:, c]
        inner = jnp.sum((gh.astype(F32) * out[:, c].astype(F32)).T, axis=0, keepdims=True)
        level = log_total[first + h]

        def piece(k, v, r, mask):
            logits = nt(k, qh[r])
            if mask is None:
                p = jnp.exp2(logits - (level[:, r] + unseen[:, r]))
            else:
                p = jnp.exp2(logits + mask - level[:, r])
            ds = (p * (nt(v, gh[r]) - inner[:, r])).astype(BF)
            return p.astype(BF), ds

        km, vm, kx, vx = kvm[:, c], kvm[:, cols(1, h)], qkv[:, cols(1, h)], qkv[:, cols(2, h)]
        p_memory, ds_memory = piece(km, vm, every, None)
        p_low, ds_low = piece(kx[low], vx[low], every, bias[low, :])
        p_high, ds_high = piece(kx[high], vx[high], high, bias[high, high])
        made["dvm"][:, c] = nn(p_memory, gh).astype(BF)
        made["dkm"][:, c] = (nn(ds_memory, qh) * LN2).astype(BF)
        made["dvx"][low, c] = nn(p_low, gh).astype(BF)
        made["dkx"][low, c] = (nn(ds_low, qh) * LN2).astype(BF)
        made["dvx"][high, c] = nn(p_high, gh[high]).astype(BF)
        made["dkx"][high, c] = (nn(ds_high, qh[high]) * LN2).astype(BF)
        turned = kx.T
        both = nn(km.T, ds_memory) + nn(turned[:, low], ds_low)
        made["dq"][low, c] = (both[:, low] * SCALE).T.astype(BF)
        made["dq"][high, c] = ((both[:, high] + nn(turned[:, high], ds_high)) * SCALE).T.astype(BF)


def attend_back_kernel(seq, aliased, active, flags, bounds, *refs):
    (qkv_in, kv_memory, d_out_in, out_in, stat_in, w_proj, x_in, gain, d_residual), refs = refs[:9], refs[9:]
    refs = refs[aliased:]
    dx, refs = refs[0], refs[1:]
    result = dict(zip([name for name, _, _ in MADE], refs))
    refs = refs[len(MADE) :]
    made = dict(zip([name for name, _, _ in MADE], refs))
    refs = refs[len(MADE) :]
    qkv, kvm, d_out, out, log_total, pool, x, rows, dx_rows, bias, unseen, in_sems, head_sems, out_sems = refs

    @pl.when(active[0] == 1)
    def _():
        loads, stores = Copies(in_sems), Copies(out_sems)
        wide = GROUP * HEAD
        count = WIDTH // wide

        def head_copies(g):
            g = g * wide if isinstance(g, int) else pl.multiple_of(g * wide, wide)
            sems = head_sems.at[g // wide]
            pairs = [
                (ref.at[seq, :, pl.ds(base * WIDTH + g, wide)], target.at[:, pl.ds(base * WIDTH + g, wide)])
                for ref, target, bases in (
                    (qkv_in, qkv, 3),
                    (kv_memory, kvm, 2),
                    (d_out_in, d_out, 1),
                    (out_in, out, 1),
                )
                for base in range(bases)
            ]
            return [pltpu.make_async_copy(a, b, sems.at[i]) for i, (a, b) in enumerate(pairs)]

        loads.start(stat_in.at[seq], log_total, "stat")
        for g in range(count):
            for copy in head_copies(g):
                copy.start()
        for t, tile in enumerate(tiles(w_proj, 1)):
            loads.start(tile, pool.at[t])
        loads.start(x_in.at[seq], x)
        loads.start(d_residual.at[seq], rows)
        fill_masks(flags[seq], bounds[seq], bias, unseen)
        loads.wait("stat")

        def heads(g, _):
            for copy in head_copies(g):
                copy.wait()
            attend_back_heads(g * GROUP, qkv, kvm, d_out, out, log_total, made, bias, unseen)
            return 0

        lax.fori_loop(0, count, heads, 0)
        for name, _, _ in MADE[:5]:
            stores.start(made[name], result[name].at[seq])
        loads.wait_all()
        grad = nt(made["dq"][...], pool[0]) + nt(made["dkx"][...], pool[1]) + nt(made["dvx"][...], pool[2])
        unit, inverse = normalise(x[...].astype(F32))
        value = (rows[...] + norm_back(unit, inverse, gain[...].astype(F32), grad)).astype(BF)
        dx_rows[...] = value
        made["dx_low"][...] = value[:, : WIDTH // 2]
        made["dx_high"][...] = value[:, WIDTH // 2 :]
        stores.start(dx_rows, dx)
        for name, _, _ in MADE[5:]:
            stores.start(made[name], result[name].at[seq])
        stores.wait_all()


def attend_back(seq, scalars, saved, fed, kv_memory, params, made, tokens, estimate=LONG):
    gain_attn, w_proj, w_out, gain_ffn, w_up, b_up, w_down, b_down = params
    seqs = saved["qkv"].shape[0]
    args = [
        saved["qkv"],
        kv_memory,
        fed["d_attended"],
        saved["attended"],
        saved["log_total"],
        w_proj,
        saved["x"],
        gain_attn,
        fed["d_residual"],
    ]
    specs = [ANY] * 7 + [whole(1, WIDTH), ANY]
    aliases = {}
    if made is not None:
        aliases = {len(scalars) + len(args) + i: 1 + i for i in range(len(MADE))}
        args += [made[name] for name, _, _ in MADE]
        specs += [ANY] * len(MADE)
    results = call(
        lambda *refs: attend_back_kernel(seq, len(aliases), *refs),
        "attend_back",
        scalars,
        args,
        [shape((SEG, WIDTH))] + [shape((seqs,) + dims, dtype) for _, dims, dtype in MADE],
        [pltpu.VMEM(dims, dtype) for _, dims, dtype in MADE]
        + [
            pltpu.VMEM((SEG, 3 * WIDTH), BF),
            pltpu.VMEM((CTX, 2 * WIDTH), BF),
            pltpu.VMEM((SEG, WIDTH), BF),
            pltpu.VMEM((SEG, WIDTH), BF),
            pltpu.VMEM((HEADS, 1, SEG), F32),
            pltpu.VMEM((3, WIDTH, WIDTH), BF),
            pltpu.VMEM((SEG, WIDTH), BF),
            pltpu.VMEM((SEG, WIDTH), F32),
            pltpu.VMEM((SEG, WIDTH), BF),
            pltpu.VMEM((SEG, SEG), F32),
            pltpu.VMEM((1, SEG), F32),
            pltpu.SemaphoreType.DMA((8,)),
            pltpu.SemaphoreType.DMA((WIDTH // (GROUP * HEAD), 7)),
            pltpu.SemaphoreType.DMA((8,)),
        ],
        tokens,
        aliases,
        estimate,
        specs,
    )
    return results[0], dict(zip([name for name, _, _ in MADE], results[1:]))


def compress_kernel(flags, grouped, w, bias, out, rows, weights, result, sems):
    copies = Copies(sems)
    copies.start(grouped, rows, "rows")
    copies.start(w, weights, "w")
    copies.wait("rows", "w")
    for s in range(rows.shape[0]):
        keep = (1 - flags[s]).astype(BF)
        result[s] = (nn(rows[s] * keep, weights[...]) + bias[...].astype(F32)).astype(BF)
        copies.start(result.at[s], out.at[s])
    copies.wait_all()


def compress(flags, memory, w_compress, b_compress, tokens):
    seqs = memory.shape[0]
    wide = RATE * WIDTH
    grouped = memory.reshape(seqs, COMP, wide)
    return call(
        compress_kernel,
        "compress",
        [flags],
        [grouped, w_compress.reshape(wide, WIDTH), b_compress],
        [shape((seqs, COMP, WIDTH))],
        [
            pltpu.VMEM((seqs, COMP, wide), BF),
            pltpu.VMEM((wide, WIDTH), BF),
            pltpu.VMEM((seqs, COMP, WIDTH), BF),
            pltpu.SemaphoreType.DMA((2 + seqs,)),
        ],
        tokens,
        estimate=SHORT,
        specs=[ANY, ANY, whole(1, WIDTH)],
    )


WIDE = 512


def places_of(order, size):
    rest, place = order[1:], {}
    for index in range(size):
        place[index] = sum(((index >> b) & 1) << (len(rest) - 1 - n) for n, b in enumerate(rest))
    return place


class Either(list):
    def __init__(self, arrays, places):
        super().__init__(arrays)
        self.places = places


def either_copies(group, refs, target, sems, base):
    made = []
    for wanted, places in enumerate(group.places):
        copies = []
        for n, (k, lead, row, column) in enumerate(places):
            source = refs[k] if lead is None else refs[k].at[lead]
            rows, columns = source.shape
            to = target.at[pl.ds(row, rows), pl.ds(column, columns)]
            copies.append(pltpu.make_async_copy(source, to, sems.at[base + n]))
        made.append((wanted, copies))
    return made


def weight_kernel(size, groups, tasks, chunks, places, small_chunk, section, mine, *refs):
    total = sum(len(g) for g in groups)
    ins, refs = refs[:total], refs[total:]
    if small_chunk is not None:
        small, refs = refs[0], refs[1:]
    sends, refs = refs[: len(chunks)], refs[len(chunks) :]
    keeps, refs = refs[: len(chunks)], refs[len(chunks) :]
    held, refs = refs[: len(groups)], refs[len(groups) :]
    staged, small_rows, in_sems, out_sems = refs
    loads, stores = Copies(in_sems), Copies(out_sems)
    even = (mine[0] & 1) == 0
    parts, at = [], 0
    for g in groups:
        parts.append(ins[at : at + len(g)])
        at += len(g)

    either = {}
    for key in dict.fromkeys(k for t in tasks for k in (t["left"], t["right"])):
        g, tile = key
        place, row = pl.ds(tile * 1024, 1024), 0
        if isinstance(groups[g], Either):
            for wanted, copies in either_copies(groups[g], parts[g], held[g], in_sems, loads.count):
                pl.when(section[0] == wanted)(lambda copies=copies: [c.start() for c in copies] and None)
            either[g] = either_copies(groups[g], parts[g], held[g], in_sems, loads.count)
            loads.count += max(len(copies) for _, copies in either[g])
            continue
        for n, ref in enumerate(parts[g]):
            loads.start(ref.at[:, place], held[g].at[pl.ds(row, ref.shape[0]), place], key + (n,))
            row += ref.shape[0]
    ready = set()

    if small_chunk is not None:
        for pair in range(size // 2):
            place = places[small_chunk][2 * pair]
            one, two = small[2 * pair], small[2 * pair + 1]
            small_rows[0, place] = jnp.where(even, two, one)
            small_rows[1, place] = jnp.where(even, one, two)
        for i, target in enumerate((sends, keeps)):
            rows = target[small_chunk].shape[1] - 16
            stores.start(small_rows.at[i], target[small_chunk].at[:, pl.ds(rows, 16), pl.ds(0, WIDTH)], ("small", i))

    busy = {}
    for n, task in enumerate(tasks):
        slot = n % 2
        for key in (task["left"], task["right"]):
            if key not in ready:
                ready.add(key)
                if key[0] in either:
                    for wanted, copies in either[key[0]]:
                        pl.when(section[0] == wanted)(lambda copies=copies: [c.wait() for c in copies] and None)
                else:
                    loads.wait(*[key + (m,) for m in range(len(parts[key[0]]))])
        for name in busy.pop(slot, ()):
            stores.wait(name)
        count = size // task["blocks"]
        rows = 1024 // count
        (left, lt), (right, rt) = task["left"], task["right"]
        for cut in range(1024 // WIDE):
            c = slice(cut * WIDE, (cut + 1) * WIDE)
            value = tn(
                held[left][:, lt * 1024 : (lt + 1) * 1024],
                held[right][:, rt * 1024 + cut * WIDE : rt * 1024 + (cut + 1) * WIDE],
            ).astype(BF)
            for pair in range(count // 2):
                one = value[(2 * pair) * rows : (2 * pair + 1) * rows]
                two = value[(2 * pair + 1) * rows : (2 * pair + 2) * rows]
                staged[slot, 0, pair, :, c] = jnp.where(even, two, one)
                staged[slot, 1, pair, :, c] = jnp.where(even, one, two)
        names = []
        for k, first, width, base in task["outs"]:
            for i, target in enumerate((sends, keeps)):
                for pair in range(count // 2):
                    names.append((n, k, i, pair))
                    stores.start(
                        staged.at[slot, i, pair, :, pl.ds(first, width)],
                        target[k].at[places[k][task["block"] * count + 2 * pair], pl.ds(0, rows), pl.ds(base, width)],
                        names[-1],
                    )
        busy[slot] = names
    stores.wait_all()


def weight_grads(section, mine, size, groups, tasks, chunks, tokens, places, small=None, small_chunk=None):
    outs = []
    for k, (blocks, columns) in enumerate(chunks):
        rows = blocks * 1024 // size + (16 if k == small_chunk else 0)
        outs.append(shape((size // 2, rows, columns)))
    args = [v for g in groups for v in g] + ([small] if small is not None else [])
    specs = [ANY] * sum(len(g) for g in groups) + ([whole(*small.shape)] if small is not None else [])
    count = size // tasks[0]["blocks"]

    def buffer(g):
        if isinstance(g, Either):
            return pltpu.VMEM((2 * SEG, WIDTH), BF)
        return pltpu.VMEM((sum(v.shape[0] for v in g), g[0].shape[1]), BF)

    results = call(
        lambda *refs: weight_kernel(size, groups, tasks, chunks, places, small_chunk, *refs),
        "weight_grads",
        [section, mine],
        args,
        outs + outs,
        [buffer(g) for g in groups]
        + [
            pltpu.VMEM((2, 2, count // 2, 1024 // count, 1024), BF),
            pltpu.VMEM((2, size // 2, 16, WIDTH), BF),
            pltpu.SemaphoreType.DMA((sum(len(g) * max(1, g[0].shape[-1] // 1024) for g in groups),)),
            pltpu.SemaphoreType.DMA((2 + sum(count * len(t["outs"]) for t in tasks),)),
        ],
        tokens,
        specs=specs,
    )
    return list(zip(results[: len(chunks)], results[len(chunks) :]))


def halve_kernel(levels, mine, *refs):
    total = len(levels)
    kept, got, refs = refs[:total], refs[total : 2 * total], refs[2 * total :]
    outs = []
    for level in levels:
        outs.append(refs[: 1 if level is None else 2])
        refs = refs[len(outs[-1]) :]
    held, came, refs = refs[:total], refs[total : 2 * total], refs[2 * total :]
    wide, refs = refs[:-2], refs[-2:]
    loads, stores = Copies(refs[0]), Copies(refs[1])
    wide = list(wide)
    for n, level in enumerate(levels):
        if level is None:
            loads.start(kept[n], held[n], (n, 0, 0))
            loads.start(got[n], came[n], (n, 0, 1))
            continue
        half = kept[n].shape[0] // 2
        bit = (mine[0] >> level) & 1
        for j, which in enumerate((1 - bit, bit)):
            place = pl.ds(which * half, half)
            loads.start(kept[n].at[place], held[n].at[j], (n, j, 0))
            loads.start(got[n].at[place], came[n].at[j], (n, j, 1))
    for n, level in enumerate(levels):
        if level is None:
            total_rows = wide.pop(0)
            loads.wait((n, 0, 0), (n, 0, 1))
            total_rows[...] = held[n][0].astype(F32) + came[n][0].astype(F32)
            stores.start(total_rows, outs[n][0])
            continue
        for j, target in enumerate(outs[n]):
            loads.wait((n, j, 0), (n, j, 1))
            held[n][j] = held[n][j] + came[n][j]
            stores.start(held[n].at[j], target)
    stores.wait_all()


def halve(mine, levels, kept, got, tokens, estimate):
    total = len(kept)
    outs, held, wide = [], [], []
    for level, v in zip(levels, kept):
        if level is None:
            outs.append(shape(v.shape[1:], F32))
            wide.append(pltpu.VMEM(v.shape[1:], F32))
            held.append(pltpu.VMEM(v.shape, BF))
        else:
            half = (v.shape[0] // 2,) + v.shape[1:]
            outs += [shape(half)] * 2
            held.append(pltpu.VMEM((2,) + half, BF))
    results = call(
        lambda *refs: halve_kernel(levels, *refs),
        "halve",
        [mine],
        [*kept, *got],
        outs,
        held
        + held
        + wide
        + [pltpu.SemaphoreType.DMA((4 * total,)), pltpu.SemaphoreType.DMA((2 * total,))],
        tokens,
        estimate=estimate,
    )
    results, made = list(results), []
    for level in levels:
        made.append([results.pop(0) for _ in range(1 if level is None else 2)])
    return made


def gather_kernel(targets, ready, small, mine, *refs):
    total = len(targets)
    late = [n for n in range(total) if not ready[n]]
    kept, refs = refs[:total], refs[total:]
    got, refs = dict(zip(late, refs)), refs[len(late) :]
    (w_proj, w_up, gain_attn, gain_ffn), outs, refs = refs[:4], refs[4:12], refs[12:]
    held, refs = dict(zip(late, refs)), refs[len(late) :]
    came, refs = dict(zip(late, refs)), refs[len(late) :]
    sums, (small_rows, b_up, b_down, proj_rows, up_rows, gains), (in_sems, out_sems) = refs[:4], refs[4:10], refs[10:]
    loads, stores = Copies(in_sems), Copies(out_sems)
    rows = proj_rows.shape[0]
    for n, (k, first) in enumerate(targets):
        if ready[n]:
            place = sums[k].at[:, pl.ds(first, kept[n].shape[1])]
            if n == small:
                loads.start(kept[n].at[pl.ds(0, rows)], place, ("sum", n))
                loads.start(kept[n].at[pl.ds(rows, 16), pl.ds(0, WIDTH)], small_rows, "small")
            else:
                loads.start(kept[n], place, ("sum", n))
        else:
            loads.start(kept[n].at[0], held[n], ("kept", n))
            loads.start(got[n].at[0], came[n], ("got", n))
    own = pl.ds(pl.multiple_of(mine[0] * rows, rows), rows)
    loads.start(w_proj.at[own], proj_rows, "proj")
    loads.start(w_up.at[own], up_rows, "up")
    for n, (k, first) in enumerate(targets):
        if ready[n]:
            loads.wait(("sum", n))
            continue
        loads.wait(("kept", n), ("got", n))
        value = held[n][...].astype(F32) + came[n][...].astype(F32)
        sums[k][:, first : first + value.shape[1]] = value
    for k in range(4):
        stores.start(sums[k], outs[k])
    loads.wait("small")
    b_up[...] = small_rows[:1, : b_up.shape[1]]
    b_down[...] = small_rows[:1, b_up.shape[1] : b_up.shape[1] + rows]
    stores.start(b_up, outs[4])
    stores.start(b_down, outs[5])
    loads.wait("proj", "up")
    for n, (weight, grad, gain) in enumerate(((proj_rows, sums[3], gain_attn), (up_rows, sums[1], gain_ffn))):
        along = jnp.sum(weight[...].astype(F32) * grad[...], axis=1, keepdims=True)
        turned = jnp.broadcast_to(along, (rows, 128)).T
        gains[n] = turned[:1, :rows] / gain[...]
        stores.start(gains.at[n], outs[6 + n])
    stores.wait_all()


def gather_up(mine, targets, kept, got, small, w_proj, w_up, own_gain, size, tokens):
    rows = WIDTH // size
    widths = [(FF // size, WIDTH), (rows, FF), (rows, WIDTH), (rows, 3 * WIDTH)]
    outs = [shape(w, F32) for w in widths]
    outs += [shape((1, n), F32) for n in (FF // size, rows, rows, rows)]
    late = [v for v, g in zip(kept, got) if g is not None]
    pieces = [pltpu.VMEM(v.shape[1:], BF) for v in late]
    ready = [g is None for g in got]
    arrived = [g for g in got if g is not None]
    return call(
        lambda *refs: gather_kernel(targets, ready, small, *refs),
        "gather_up",
        [mine],
        [*kept, *arrived, w_proj, w_up, *own_gain],
        outs,
        pieces
        + pieces
        + [pltpu.VMEM(w, F32) for w in widths]
        + [
            pltpu.VMEM((16, WIDTH), F32),
            pltpu.VMEM((1, FF // size), F32),
            pltpu.VMEM((1, rows), F32),
            pltpu.VMEM((rows, 3 * WIDTH), BF),
            pltpu.VMEM((rows, FF), BF),
            pltpu.VMEM((2, 1, rows), F32),
            pltpu.SemaphoreType.DMA((2 * len(kept) + 3,)),
            pltpu.SemaphoreType.DMA((8,)),
        ],
        tokens,
        estimate=SHORT,
        specs=[ANY] * (len(kept) + len(late) + 2) + [whole(1, rows)] * 2,
    )


def pick_kernel(section, first, second, out, held, sems):
    for wanted, source in enumerate((first, second)):

        @pl.when(section[0] == wanted)
        def _(source=source):
            copies = Copies(sems)
            for s in range(held.shape[0]):
                copies.start(source.at[s], held.at[s], ("in", s))
            for s in range(held.shape[0]):
                copies.wait(("in", s))
                copies.start(held.at[s], out.at[s])
            copies.wait_all()


def pick(section, first, second, tokens):
    return call(
        pick_kernel,
        "pick",
        [section],
        [first, second],
        [shape(first.shape)],
        [pltpu.VMEM(first.shape, BF), pltpu.SemaphoreType.DMA((2 * first.shape[0],))],
        tokens,
        estimate=SHORT,
    )[0]


def swap_bit(value, size, bit):
    return lax.ppermute(value, "dp", [(i, i ^ (1 << bit)) for i in range(size)])


def one_way(value, first, second):
    return lax.ppermute(value, "section", [(first, second)])


def both_after(first, second):
    return lax.optimization_barrier((first, second))


def body(
    inputs,
    cotangent,
    memory,
    compressed,
    reset_flags,
    boundary,
    gain_attn,
    projection_weight,
    w_output,
    gain_ffn,
    w_up,
    b_up,
    w_down,
    b_down,
    w_compress,
    b_compress,
):
    section = lax.axis_index("section")
    is_first = section == 0
    size = lax.axis_size("dp")
    mine = lax.axis_index("dp")
    levels = (size - 1).bit_length()
    at_section, at_dp = section.astype(jnp.int32).reshape(1), mine.astype(jnp.int32).reshape(1)
    active = (1 - at_section, at_section)
    seqs, _, width = inputs.shape
    memory, compressed = memory[0], compressed[0]
    w_proj, w_out, w_up, w_down = projection_weight[0], w_output[0], w_up[0], w_down[0]
    params = (gain_attn, w_proj, w_out, gain_ffn, w_up, b_up, w_down, b_down)
    last = [[]]

    other_x = [one_way(inputs[0], 1, 0)]
    normed_memory, kv_memory = memory_keyvals(reset_flags, compressed, memory, gain_attn, w_proj, [])
    last[0] = [kv_memory]
    inputs_later, kv_memory = both_after(inputs, kv_memory)
    other_x.append(one_way(inputs_later[1], 1, 0))

    def ahead(layer, s, xs, saved):
        scalars = [active[layer], reset_flags, boundary]
        y, saved = forward(s, seqs, scalars, xs, kv_memory, params, saved, last[0])
        last[0] = [y]
        return y, saved

    y_a0, saved = ahead(0, 0, ((inputs, 0), (other_x[0], None)), None)
    hop_a = one_way(y_a0, 0, 1)
    y_b0, saved = ahead(0, 1, ((inputs, 1), (other_x[1], None)), saved)
    y_b0, cotangent_later = both_after(y_b0, cotangent)
    y_b0, memory_later = both_after(y_b0, memory)
    hop_b = one_way(y_b0, 0, 1)
    other_gy = one_way(cotangent_later, 0, 1)
    squeezed = compress(reset_flags, memory_later, w_compress[0], b_compress, last[0])[0]
    last[0] = [squeezed]
    y_a1, saved = ahead(1, 0, ((hop_a, None),), saved)
    y_b1, saved = ahead(1, 1, ((hop_b, None),), saved)
    other_y = one_way(saved["y_low"], 1, 0)

    def back(layer, s, gys, fed, made):
        fed = feed_back(s, [active[layer]], gys, saved, params, fed, last[0])
        scalars = [active[layer], reset_flags, boundary]
        dx, made = attend_back(s, scalars, saved, fed, kv_memory, params, made, [], SHORT)
        last[0] = [dx]
        return dx, fed, made

    dx_a1, fed, made = back(1, 0, ((other_gy, 0), (cotangent, 0)), None, None)
    back_a = one_way(dx_a1, 1, 0)
    dx_b1, fed, made = back(1, 1, ((other_gy, 1), (cotangent, 1)), fed, made)
    back_b = one_way(dx_b1, 1, 0)
    dx_a0, fed, made = back(0, 0, ((back_a, None),), fed, made)

    rows_of = lambda v: v.reshape((-1, v.shape[-1]))
    half = WIDTH // 2
    gy_all = Either(
        [back_a, back_b, other_gy, cotangent],
        (
            [(0, None, 0, 0), (1, None, SEG, 0)],
            [(2, 0, 0, 0), (3, 0, 0, half), (2, 1, SEG, 0), (3, 1, SEG, half)],
        ),
    )
    moving, done = {}, {}
    orders = {name: (0, *range(2, levels), 1) for name in ()}

    def send_on(name, send, keep, step):
        order = orders.get(name, tuple(range(levels)))
        moving[name] = (swap_bit(send, size, order[step]), keep, step)

    def halved(*names, estimate=SHORT):
        names = [name for name in names if name in moving]
        if not names:
            return
        which = []
        for name in names:
            step = moving[name][2] + 1
            which.append(None if step == levels else orders.get(name, tuple(range(levels)))[step])
        kept, got = [moving[name][1] for name in names], [moving[name][0] for name in names]
        made = halve(at_dp, which, kept, got, last[0], estimate)
        last[0] = [made[0][0]]
        for name, level, values in zip(names, which, made):
            if level is None:
                done[name] = values[0]
                moving.pop(name)
            else:
                send_on(name, *values, moving[name][2] + 1)

    def grads(names, groups, tasks, chunks, **more):
        places = [places_of(orders.get(name, tuple(range(levels))), size) for name in names]
        made = weight_grads(at_section, at_dp, size, groups, tasks, chunks, last[0], places, **more)
        last[0] = [made[0][0]]
        for name, (send, keep) in zip(names, made):
            send_on(name, send, keep, 0)

    eighth = WIDTH // 8
    grads(
        ("down0", "down1", "down2"),
        [[rows_of(saved["hidden"])], gy_all],
        [
            dict(
                left=(0, t),
                right=(1, 0),
                block=t,
                blocks=FF // WIDTH,
                outs=[(0, 0, 3 * eighth, 0), (1, 3 * eighth, 2 * eighth, 0), (2, 5 * eighth, 3 * eighth, 0)],
            )
            for t in range(FF // WIDTH)
        ],
        [(FF // WIDTH, 3 * eighth), (FF // WIDTH, 2 * eighth), (FF // WIDTH, 3 * eighth)],
    )
    halved("down0")
    halved("down1", "down2")
    fed = feed_back(1, [active[0]], ((back_b, None),), saved, params, fed, last[0])
    last[0] = [fed["d_down"]]
    halved("down0")

    up = jnp.sum(fed["d_up"], axis=(0, 1)).reshape(size, FF // size)
    down = jnp.sum(fed["d_down"], axis=(0, 1)).reshape(size, WIDTH // size)
    row = jnp.concatenate([up, down], axis=1).astype(BF)
    small = jnp.pad(row[:, None, :], ((0, 0), (0, 15), (0, WIDTH - row.shape[1])))
    ffn_in, d_hidden = [rows_of(saved["ffn_in"])], [rows_of(fed["d_hidden"])]
    grads(
        ("up0",),
        [ffn_in, d_hidden],
        [dict(left=(0, 0), right=(1, t), block=0, blocks=1, outs=[(0, 0, WIDTH, t * WIDTH)]) for t in range(2)],
        [(1, 2 * WIDTH)],
    )
    halved("down1", "down0")
    grads(
        ("up1", "out"),
        [ffn_in, d_hidden, [rows_of(saved["attended"])], [rows_of(fed["low"])]],
        [dict(left=(0, 0), right=(1, 2 + t), block=0, blocks=1, outs=[(0, 0, WIDTH, t * WIDTH)]) for t in range(2)]
        + [dict(left=(2, 0), right=(3, 0), block=0, blocks=1, outs=[(1, 0, WIDTH, 0)])],
        [(1, 2 * WIDTH), (1, WIDTH)],
        small=small,
        small_chunk=0,
    )
    halved("down2", "down1", "up0")
    dx_b0, made = attend_back(
        1, [active[0], reset_flags, boundary], saved, fed, kv_memory, params, made, last[0]
    )
    last[0] = [dx_b0]
    outputs = pick(at_section, other_y, saved["y_high"], last[0])
    last[0] = [outputs]
    halved("up0", "up1", "out", "down2", "down1", "down0")
    grads(
        ("key", "value", "query"),
        [
            [rows_of(saved["normed"]), rows_of(normed_memory)],
            [rows_of(made["dkx"]), rows_of(made["dkm"])],
            [rows_of(made["dvx"]), rows_of(made["dvm"])],
            [rows_of(saved["normed"])],
            [rows_of(made["dq"])],
        ],
        [
            dict(left=(0, 0), right=(1, 0), block=0, blocks=1, outs=[(0, 0, WIDTH, 0)]),
            dict(left=(0, 0), right=(2, 0), block=0, blocks=1, outs=[(1, 0, WIDTH, 0)]),
            dict(left=(3, 0), right=(4, 0), block=0, blocks=1, outs=[(2, 0, WIDTH, 0)]),
        ],
        [(1, WIDTH)] * 3,
    )
    halved("up1", estimate=LONG)
    halved("key", "value", "query")
    halved("out", "up0", "down2")
    grad_inputs = pick(at_section, made["dx_low"], one_way(made["dx_high"], 0, 1), last[0])
    last[0] = [grad_inputs]
    for names in (("key", "up1"), ("value", "key", "out", "up0"), ("query", "value", "up1", "out"), ("query", "key")):
        halved(*names)
    while any(step + 1 < levels for _, _, step in moving.values()):
        halved(*[name for name, (_, _, step) in moving.items() if step + 1 < levels])
    if "up1" in moving:
        halved("up1")
    rows = WIDTH // size
    own_gain = [
        lax.dynamic_slice_in_dim(gain, mine * rows, rows, 1).astype(F32) for gain in (gain_attn, gain_ffn)
    ]
    targets = dict(
        down0=(0, 0), down1=(0, 3 * eighth), down2=(0, 5 * eighth), up0=(1, 0), up1=(1, 2 * WIDTH), out=(2, 0),
        query=(3, 0), key=(3, WIDTH), value=(3, 2 * WIDTH),
    )
    names = list(targets)
    g_down, g_up, g_out, g_proj, g_b_up, g_b_down, g_gain_attn, g_gain_ffn = gather_up(
        at_dp,
        [targets[name] for name in names],
        [done[name] if name in done else moving[name][1] for name in names],
        [None if name in done else moving[name][0] for name in names],
        names.index("up1"),
        w_proj,
        w_up,
        own_gain,
        size,
        last[0],
    )
    keep_all = (1 - reset_flags).astype(BF)[:, None, None]
    new_compressed = jnp.concatenate([compressed[:, COMP:] * keep_all, squeezed], axis=1)
    return (
        outputs,
        grad_inputs,
        saved["x"][None],
        new_compressed[None],
        g_gain_attn,
        g_proj[None],
        g_out[None],
        g_gain_ffn,
        g_up[None],
        g_b_up,
        g_down[None],
        g_b_down,
    )


def solution(mesh):
    return jax.shard_map(
        body,
        mesh=mesh,
        in_specs=(
            P("dp", None, "section"),
            P("dp", None, "section"),
            P("section", "dp", None, None),
            P("section", "dp", None, None),
            P("dp"),
            P("dp"),
            P("section", None),
            P("section", None, None),
            P("section", None, None),
            P("section", None),
            P("section", None, None),
            P("section", None),
            P("section", None, None),
            P("section", None),
            P("section", None, None, None),
            P("section", None),
        ),
        out_specs=(
            P("dp", None, "section"),
            P("dp", None, "section"),
            P("section", "dp", None, None),
            P("section", "dp", None, None),
            P("section", "dp"),
            P("section", "dp", None),
            P("section", "dp", None),
            P("section", "dp"),
            P("section", "dp", None),
            P("section", "dp"),
            P("section", "dp", None),
            P("section", "dp"),
        ),
        check_vma=False,
    )
```

time: 1360 us -> 538 us (0.40)
  the two profiles are of different devices: /device:TPU:26 before, /device:TPU:0 now
where the time goes in v2:
time: 538 us; the launch traced here: 530 us
  Pallas kernels  305 us (57%)
  waiting for transfers between devices  143 us (27%)
  starting transfers between devices  52.2 us (10%)
  local copies, waits for them, and re-layouts  20.7 us (4%)
  other arithmetic  6.65 us (1%)
    pallas_call x34, Pallas kernels, call(): pl.pallas_call(run, name=name, grid_spec=pltpu.PrefetchScalarGridSpec(num...  305 us
    ppermute x9, waiting for transfers between devices, one_way(): return lax.ppermute(value, 'section', [(first, second)])  90.7 us
    ppermute x36, waiting for transfers between devices, swap_bit(): return lax.ppermute(value, 'dp', [(i, i ^ 1 << bit) for i in range(size)])  52.7 us
    ppermute x36, starting transfers between devices, swap_bit(): return lax.ppermute(value, 'dp', [(i, i ^ 1 << bit) for i in range(size)])  38.3 us
    unnamed x104, local copies, waits for them, and re-layouts  17.4 us
    ppermute x9, starting transfers between devices, one_way(): return lax.ppermute(value, 'section', [(first, second)])  13.9 us
  transfers between devices with their start and end apart: 45, of which 16 were waited for; matrix products, arithmetic and copies ran while one was open for 2% of the time, Pallas kernels for 51%

profile of v2, /device:TPU:0, one launch (start us, length us, event | category | flops | bytes accessed | tf_op | source)
XLA Modules:
  0.0 530.0 jit_solution(12086755616878332079)
XLA Ops:
  3.0 15.3 %memory_keyvals.1 = (bf16[2,1024,1024]{2,1,0:T(8,128)(2,1)}, bf16[2,1024,2048]{2,1,0:T(8,128)(2,1)}) custom-call(s32[2]{0:T(128)} %refs_1_.15, bf16[2,512,1024]{2,1,0:T(8,128)(2,1)} %bitcast.61, bf16[2,512,1024]{2,1,0:T(8,128)(2,1)} %bitcast.59, bf16[1,1024]{1,0:T(2,128)(2,1)} %refs_10_.11, bf16[1024,3072]{1,0:T(8,128)(2,1)} %bitcast.32), custom_call_target="tpu_custom_call" | custom-call | flops 99999997952 | bytes 1 | tf_op jit(solution)/shard_map/memory_keyvals/pallas_call | solution.py:83
  20.5 32.7 %forward.4 = (bf16[512,1024]{1,0:T(8,128)(2,1)}, bf16[2,512,1024]{2,1,0:T(8,128)(2,1)}, bf16[2,512,1024]{2,1,0:T(8,128)(2,1)}, bf16[2,512,3072]{2,1,0:T(8,128)(2...) custom-call(s32[1]{0:T(128)S(6)} %sub.6.refs_0_, ...), custom_call_target="tpu_custom_call" | custom-call | flops 99999997952 | bytes 1 | tf_op jit(solution)/shard_map/forward/pallas_call | solution.py:83
  56.4 33.1 %forward.5 = (bf16[512,1024]{1,0:T(8,128)(2,1)}, bf16[2,512,1024]{2,1,0:T(8,128)(2,1)}, bf16[2,512,1024]{2,1,0:T(8,128)(2,1)}, bf16[2,512,3072]{2,1,0:T(8,128)(2...) custom-call(s32[1]{0:T(128)S(6)} %sub.6.refs_0_, ...), custom_call_target="tpu_custom_call", output_to_operand_aliasing={{1}: (14, {}), {2}: (15, {}), {3}: (16, {}), {4}: (17, {}),... | custom-call | flops 99999997952 | bytes 1 | tf_op jit(solution)/shard_map/forward/pallas_call | solution.py:83
  95.5 7.3 %compress.1.refs_24_ = bf16[2,256,1024]{2,1,0:T(8,128)(2,1)} custom-call(s32[2]{0:T(128)} %refs_1_.15, bf16[2,256,2048]{2,1,0:T(8,128)(2,1)} %reshape.107.refs_1_, bf16[2048,1024]{1,0:T(8,128)(2,1)} %bitcast.58, bf16[1,1024]{1,0:T(2,128)(2,1)} %refs_3_.7, bf16[512,1024]{1,0:T(8,128)(2,1)} %get-tuple-element.228.refs_4_), custom_call_target="tpu_custom_call" | custom-call | flops 1 | bytes 1 | tf_op jit(solution)/shard_map/compress/pallas_call | solution.py:83
  104.7 11.8 %collective-permute-done.2.refs_3_ = bf16[512,1024]{1,0:T(8,128)(2,1)S(1)} collective-permute-done((bf16[512,1024]{1,0:T(8,128)(2,1)S(1)}, bf16[512,1024]{1,0:T(8,128)(2,1)S(1)}, u32[]{:S(2)}, u32[]{:S(2)}) %collective-permute-start.2) | collective-permute-done | bytes 1048608 | tf_op jit(solution)/shard_map/ppermute | solution.py:996
  119.4 19.4 %collective-permute-done.5.refs_1_.refs_5_ = bf16[2,512,512]{2,1,0:T(8,128)(2,1)} collective-permute-done((bf16[2,512,512]{2,1,0:T(8,128)(2,1)}, bf16[2,512,512]{2,1,0:T(8,128)(2,1)}, u32[]{:S(2)}, u32[]{:S(2)}) %collective-permute-start.5) | collective-permute-done | bytes 1048608 | tf_op jit(solution)/shard_map/ppermute | solution.py:996
  140.1 5.8 %attend_back.4 = (bf16[512,1024]{1,0:T(8,128)(2,1)}, bf16[2,512,1024]{2,1,0:T(8,128)(2,1)}, bf16[2,512,1024]{2,1,0:T(8,128)(2,1)}, bf16[2,512,1024]{2,1,0:T(8,12...) custom-call(s32[1]{0:T(128)} %bitcast.refs_0_, ...), custom_call_target="tpu_custom_call" | custom-call | flops 1 | bytes 1 | tf_op jit(solution)/shard_map/attend_back/pallas_call | solution.py:83
  147.3 5.8 %feed_back.5 = (bf16[2,512,4096]{2,1,0:T(8,128)(2,1)}, f32[2,512,1024]{2,1,0:T(8,128)}, bf16[2,512,1024]{2,1,0:T(8,128)(2,1)}, bf16[2,512,1024]{2,1,0:T(8,128)(2...) custom-call(s32[1]{0:T(128)} %bitcast.refs_0_, ...), custom_call_target="tpu_custom_call", output_to_operand_aliasing={{0}: (9, {}), {1}: (10, {}), {2}: (11, {}), {3}: (12, {}), ... | custom-call | flops 99999997952 | bytes 1 | tf_op jit(solution)/shard_map/feed_back/pallas_call | solution.py:83
  153.0 5.9 %attend_back.5 = (bf16[512,1024]{1,0:T(8,128)(2,1)}, bf16[2,512,1024]{2,1,0:T(8,128)(2,1)}, bf16[2,512,1024]{2,1,0:T(8,128)(2,1)}, bf16[2,512,1024]{2,1,0:T(8,12...) custom-call(s32[1]{0:T(128)} %bitcast.refs_0_, ...), custom_call_target="tpu_custom_call", output_to_operand_aliasing={{1}: (12, {}), {2}: (13, {}), {3}: (14, {}), {4}: (15, {}),... | custom-call | flops 1 | bytes 1 | tf_op jit(solution)/shard_map/attend_back/pallas_call | solution.py:83
  160.3 59.5 %collective-permute-done.7.refs_1_.refs_3_ = bf16[512,1024]{1,0:T(8,128)(2,1)S(1)} collective-permute-done((bf16[512,1024]{1,0:T(8,128)(2,1)}, bf16[512,1024]{1,0:T(8,128)(2,1)S(1)}, u32[]{:S(2)}, u32[]{:S(2)}) %collective-permute-start.7) | collective-permute-done | bytes 1048608 | tf_op jit(solution)/shard_map/ppermute | solution.py:996
  220.8 17.2 %feed_back.6 = (bf16[2,512,4096]{2,1,0:T(8,128)(2,1)}, f32[2,512,1024]{2,1,0:T(8,128)}, bf16[2,512,1024]{2,1,0:T(8,128)(2,1)}, bf16[2,512,1024]{2,1,0:T(8,128)(2...) custom-call(s32[1]{0:T(128)S(6)} %sub.6.refs_0_, ...), custom_call_target="tpu_custom_call", output_to_operand_aliasing={{0}: (8, {}), {1}: (9, {}), {2}: (10, {}), {3}: (11, {}), {... | custom-call | flops 99999997952 | bytes 1 | tf_op jit(solution)/shard_map/feed_back/pallas_call | solution.py:83
  238.0 25.8 %attend_back.6 = (bf16[512,1024]{1,0:T(8,128)(2,1)}, bf16[2,512,1024]{2,1,0:T(8,128)(2,1)}, bf16[2,512,1024]{2,1,0:T(8,128)(2,1)}, bf16[2,512,1024]{2,1,0:T(8,12...) custom-call(s32[1]{0:T(128)S(6)} %sub.6.refs_0_, ...), custom_call_target="tpu_custom_call", output_to_operand_aliasing={{1}: (12, {}), {2}: (13, {}), {3}: (14, {}), {4}: (15, {}),... | custom-call | flops 1 | bytes 1 | tf_op jit(solution)/shard_map/attend_back/pallas_call | solution.py:83
  264.7 13.6 %weight_grads.4 = (bf16[8,256,384]{2,1,0:T(8,128)(2,1)}, bf16[8,256,256]{2,1,0:T(8,128)(2,1)}, bf16[8,256,384]{2,1,0:T(8,128)(2,1)}, bf16[8,256,384]{2,1,0:T(8,1...) custom-call(s32[1]{0:T(128)} %bitcast.refs_0_, s32[1]{0:T(128)} %bitcast.10.refs_1_.refs_0_, ...), custom_call_target="tpu_custom_call" | custom-call | flops 99999997952 | bytes 1 | tf_op jit(solution)/shard_map/weight_grads/pallas_call | solution.py:83
  283.2 2.9 halve.13
  289.5 4.0 halve.14
  293.8 17.4 %feed_back.7 = (bf16[2,512,4096]{2,1,0:T(8,128)(2,1)}, f32[2,512,1024]{2,1,0:T(8,128)}, bf16[2,512,1024]{2,1,0:T(8,128)(2,1)}, bf16[2,512,1024]{2,1,0:T(8,128)(2...) custom-call(s32[1]{0:T(128)S(6)} %sub.6.refs_0_, ...), custom_call_target="tpu_custom_call", output_to_operand_aliasing={{0}: (8, {}), {1}: (9, {}), {2}: (10, {}), {3}: (11, {}), {... | custom-call | flops 99999997952 | bytes 1 | tf_op jit(solution)/shard_map/feed_back/pallas_call | solution.py:83
  320.1 8.7 %weight_grads.5 = (bf16[8,64,2048]{2,1,0:T(8,128)(2,1)}, bf16[8,64,2048]{2,1,0:T(8,128)(2,1)}) custom-call(s32[1]{0:T(128)} %bitcast.refs_0_, s32[1]{0:T(128)} %bitcast.10.refs_1_.refs_0_, bf16[1024,1024]{1,0:T(8,128)(2,1)} %bitcast.89, bf16[1024,4096]{1,0:T(8,128)(2,1)} %bitcast.84, bf16[2,256,384]{2,1,0:T(8,128)(2,1)} %get-tuple-element.321.refs_4_), custom_call_target="tpu_custom_call" | custom-call | flops 99999997952 | bytes 1 | tf_op jit(solution)/shard_map/weight_grads/pallas_call | solution.py:83
  336.3 12.4 %weight_grads.6 = (bf16[8,80,2048]{2,1,0:T(8,128)(2,1)}, bf16[8,64,1024]{2,1,0:T(8,128)(2,1)}, bf16[8,80,2048]{2,1,0:T(8,128)(2,1)}, bf16[8,64,1024]{2,1,0:T(8,128)(2,1)}) custom-call(s32[1]{0:T(128)} %bitcast.refs_0_, s32[1]{0:T(128)} %bitcast.10.refs_1_.refs_0_, bf16[1024,1024]{1,0:T(8,128)(2,1)} %bitcast.90, bf16[1024,4096]{1,0:T(8,128)(2,1)} %bitcast.85, ...), custom_call_target="tpu_custom_call" | custom-call | flops 99999997952 | bytes 1 | tf_op jit(solution)/shard_map/weight_grads/pallas_call | solution.py:83
  350.6 4.4 halve.17
  356.5 25.5 %attend_back.7 = (bf16[512,1024]{1,0:T(8,128)(2,1)}, bf16[2,512,1024]{2,1,0:T(8,128)(2,1)}, bf16[2,512,1024]{2,1,0:T(8,128)(2,1)}, bf16[2,512,1024]{2,1,0:T(8,12...) custom-call(s32[1]{0:T(128)S(6)} %sub.6.refs_0_, ...), custom_call_target="tpu_custom_call", output_to_operand_aliasing={{1}: (12, {}), {2}: (13, {}), {3}: (14, {}), {4}: (15, {}),... | custom-call | flops 99999997952 | bytes 1 | tf_op jit(solution)/shard_map/attend_back/pallas_call | solution.py:83
  386.5 7.0 %halve.18 = (bf16[2,64,2048]{2,1,0:T(8,128)(2,1)}, bf16[2,64,2048]{2,1,0:T(8,128)(2,1)}, bf16[4,80,2048]{2,1,0:T(8,128)(2,1)}, bf16[4,80,2048]{2,1,0:T(8,128)(2,...) custom-call(s32[1]{0:T(128)} %bitcast.10.refs_1_.refs_0_, ...), custom_call_target="tpu_custom_call" | custom-call | flops 1 | bytes 1 | tf_op jit(solution)/shard_map/halve/pallas_call | solution.py:83
  395.3 22.5 %weight_grads.7 = (bf16[8,64,1024]{2,1,0:T(8,128)(2,1)}, bf16[8,64,1024]{2,1,0:T(8,128)(2,1)}, bf16[8,64,1024]{2,1,0:T(8,128)(2,1)}, bf16[8,64,1024]{2,1,0:T(8,1...) custom-call(s32[1]{0:T(128)} %bitcast.refs_0_, s32[1]{0:T(128)} %bitcast.10.refs_1_.refs_0_, ...), custom_call_target="tpu_custom_call" | custom-call | flops 99999997952 | bytes 1 | tf_op jit(solution)/shard_map/weight_grads/pallas_call | solution.py:83
  421.1 3.5 collective-permute-done.30.refs_2_
  432.2 4.5 halve.20
  439.3 18.2 %collective-permute-done.25.refs_5_ = bf16[2,64,2048]{2,1,0:T(8,128)(2,1)S(1)} collective-permute-done((bf16[2,64,2048]{2,1,0:T(8,128)(2,1)S(1)}, bf16[2,64,2048]{2,1,0:T(8,128)(2,1)S(1)}, u32[]{:S(2)}, u32[]{:S(2)}) %collective-permute-start.25) | collective-permute-done | bytes 524320 | tf_op jit(solution)/shard_map/ppermute | solution.py:992
  461.5 3.4 collective-permute-start.36
  477.3 6.0 %collective-permute-done.34.refs_6_ = bf16[2,64,1024]{2,1,0:T(8,128)(2,1)S(1)} collective-permute-done((bf16[2,64,1024]{2,1,0:T(8,128)(2,1)}, bf16[2,64,1024]{2,1,0:T(8,128)(2,1)S(1)}, u32[]{:S(2)}, u32[]{:S(2)}) %collective-permute-start.34) | collective-permute-done | bytes 262176 | tf_op jit(solution)/shard_map/ppermute | solution.py:992
  490.0 4.2 collective-permute-done.40.refs_8_
  494.2 3.7 collective-permute-done.38.refs_6_
  507.3 3.9 collective-permute-done.42.refs_4_
  519.0 5.6 %collective-permute-done.43.refs_10_ = bf16[1,64,1024]{2,1,0:T(8,128)(2,1)S(1)} collective-permute-done((bf16[1,64,1024]{2,1,0:T(8,128)(2,1)}, bf16[1,64,1024]{2,1,0:T(8,128)(2,1)S(1)}, u32[]{:S(2)}, u32[]{:S(2)}) %collective-permute-start.43) | collective-permute-done | bytes 131104 | tf_op jit(solution)/shard_map/ppermute | solution.py:992
  525.3 4.4 gather_up.1
  (209 shorter events, 112.5 us)
Async XLA Ops:
  1.7 18.0 %collective-permute-start.1 = (bf16[512,512]{1,0:T(8,128)(2,1)S(1)}, bf16[512,512]{1,0:T(8,128)(2,1)S(1)}, u32[]{:S(2)}, u32[]{:S(2)}) collective-permute-start(bf16[512,512]{1,0:T(8,128)(2,1)S(1)} %slice_bitcast_fusion), channel_id=1, source_target_pairs={{1,0},{3,2},{5,4},{7,6},{9,8},{11,10},{13,12},{15,14},{17,16},{19,... | collective-permute-start | bytes 1572872 | tf_op jit(solution)/shard_map/ppermute | solution.py:996
  18.4 37.2 %collective-permute-start = (bf16[512,512]{1,0:T(8,128)(2,1)S(1)}, bf16[512,512]{1,0:T(8,128)(2,1)S(1)}, u32[]{:S(2)}, u32[]{:S(2)}) collective-permute-start(bf16[512,512]{1,0:T(8,128)(2,1)S(1)} %slice_bitcast_fusion.1), channel_id=1, source_target_pairs={{1,0},{3,2},{5,4},{7,6},{9,8},{11,10},{13,12},{15,14},{17,16},{19,... | collective-permute-start | bytes 1572872 | tf_op jit(solution)/shard_map/ppermute | solution.py:996
  53.2 49.6 %collective-permute-start.3 = (bf16[512,1024]{1,0:T(8,128)(2,1)}, bf16[512,1024]{1,0:T(8,128)(2,1)}, u32[]{:S(2)}, u32[]{:S(2)}) collective-permute-start(bf16[512,1024]{1,0:T(8,128)(2,1)} %get-tuple-element.225.refs_25_), channel_id=1, source_target_pairs={{0,1},{2,3},{4,5},{6,7},{8,9},{10,11},{12,13},{14,15},{16,17},{18,... | collective-permute-start | bytes 3145736 | tf_op jit(solution)/shard_map/ppermute | solution.py:996
  91.7 24.8 %collective-permute-start.2 = (bf16[512,1024]{1,0:T(8,128)(2,1)S(1)}, bf16[512,1024]{1,0:T(8,128)(2,1)S(1)}, u32[]{:S(2)}, u32[]{:S(2)}) collective-permute-start(bf16[512,1024]{1,0:T(8,128)(2,1)S(1)} %copy-done.15), channel_id=1, source_target_pairs={{0,1},{2,3},{4,5},{6,7},{8,9},{10,11},{12,13},{14,15},{16,17},{18,... | collective-permute-start | bytes 3145736 | tf_op jit(solution)/shard_map/ppermute | solution.py:996
  93.0 45.8 %collective-permute-start.5 = (bf16[2,512,512]{2,1,0:T(8,128)(2,1)}, bf16[2,512,512]{2,1,0:T(8,128)(2,1)}, u32[]{:S(2)}, u32[]{:S(2)}) collective-permute-start(bf16[2,512,512]{2,1,0:T(8,128)(2,1)} %refs_6_.4), channel_id=1, source_target_pairs={{0,1},{2,3},{4,5},{6,7},{8,9},{10,11},{12,13},{14,15},{16,17},{18,... | collective-permute-start | bytes 3145736 | tf_op jit(solution)/shard_map/ppermute | solution.py:996
  146.0 73.8 %collective-permute-start.7 = (bf16[512,1024]{1,0:T(8,128)(2,1)}, bf16[512,1024]{1,0:T(8,128)(2,1)S(1)}, u32[]{:S(2)}, u32[]{:S(2)}) collective-permute-start(bf16[512,1024]{1,0:T(8,128)(2,1)} %get-tuple-element.269.refs_15_), channel_id=1, source_target_pairs={{1,0},{3,2},{5,4},{7,6},{9,8},{11,10},{13,12},{15,14},{17,16},{19,... | collective-permute-start | bytes 3145736 | tf_op jit(solution)/shard_map/ppermute | solution.py:996
  159.0 104.8 %collective-permute-start.6 = (bf16[512,1024]{1,0:T(8,128)(2,1)}, bf16[512,1024]{1,0:T(8,128)(2,1)S(1)}, u32[]{:S(2)}, u32[]{:S(2)}) collective-permute-start(bf16[512,1024]{1,0:T(8,128)(2,1)} %get-tuple-element.279.refs_14_), channel_id=1, source_target_pairs={{1,0},{3,2},{5,4},{7,6},{9,8},{11,10},{13,12},{15,14},{17,16},{19,... | collective-permute-start | bytes 3145736 | tf_op jit(solution)/shard_map/ppermute | solution.py:996
  279.0 76.7 %collective-permute-start.4 = (bf16[2,512,512]{2,1,0:T(8,128)(2,1)}, bf16[2,512,512]{2,1,0:T(8,128)(2,1)}, u32[]{:S(2)}, u32[]{:S(2)}) collective-permute-start(bf16[2,512,512]{2,1,0:T(8,128)(2,1)} %get-tuple-element.253), channel_id=1, source_target_pairs={{1,0},{3,2},{5,4},{7,6},{9,8},{11,10},{13,12},{15,14},{17,16},{19,... | collective-permute-start | bytes 3145736 | tf_op jit(solution)/shard_map/ppermute | solution.py:996
  286.1 29.3 %collective-permute-start.11 = (bf16[4,256,384]{2,1,0:T(8,128)(2,1)}, bf16[4,256,384]{2,1,0:T(8,128)(2,1)S(1)}, u32[]{:S(2)}, u32[]{:S(2)}) collective-permute-start(bf16[4,256,384]{2,1,0:T(8,128)(2,1)} %get-tuple-element.305.refs_5_), channel_id=1, source_target_pairs={{0,4},{2,6},{4,0},{6,2},{8,12},{10,14},{12,8},{14,10},{16,20},{18,... | collective-permute-start | bytes 2359304 | tf_op jit(solution)/shard_map/ppermute | solution.py:992
  293.5 35.4 %collective-permute-start.12 = (bf16[4,256,256]{2,1,0:T(8,128)(2,1)}, bf16[4,256,256]{2,1,0:T(8,128)(2,1)}, u32[]{:S(2)}, u32[]{:S(2)}) collective-permute-start(bf16[4,256,256]{2,1,0:T(8,128)(2,1)} %get-tuple-element.306.refs_14_), channel_id=1, source_target_pairs={{0,4},{2,6},{4,0},{6,2},{8,12},{10,14},{12,8},{14,10},{16,20},{18,... | collective-permute-start | bytes 1572872 | tf_op jit(solution)/shard_map/ppermute | solution.py:992
  312.8 36.0 %collective-permute-start.14 = (bf16[4,256,384]{2,1,0:T(8,128)(2,1)}, bf16[4,256,384]{2,1,0:T(8,128)(2,1)}, u32[]{:S(2)}, u32[]{:S(2)}) collective-permute-start(bf16[4,256,384]{2,1,0:T(8,128)(2,1)} %get-tuple-element.327), channel_id=1, source_target_pairs={{0,4},{2,6},{4,0},{6,2},{8,12},{10,14},{12,8},{14,10},{16,20},{18,... | collective-permute-start | bytes 2359304 | tf_op jit(solution)/shard_map/ppermute | solution.py:992
  328.8 20.5 %collective-permute-start.16 = (bf16[8,64,2048]{2,1,0:T(8,128)(2,1)}, bf16[8,64,2048]{2,1,0:T(8,128)(2,1)S(1)}, u32[]{:S(2)}, u32[]{:S(2)}) collective-permute-start(bf16[8,64,2048]{2,1,0:T(8,128)(2,1)} %get-tuple-element.324.refs_5_), channel_id=1, source_target_pairs={{0,2},{2,0},{4,6},{6,4},{8,10},{10,8},{12,14},{14,12},{16,18},{18,... | collective-permute-start | bytes 6291464 | tf_op jit(solution)/shard_map/ppermute | solution.py:992
  332.1 16.7 %collective-permute-start.15 = (bf16[2,256,256]{2,1,0:T(8,128)(2,1)}, bf16[2,256,256]{2,1,0:T(8,128)(2,1)S(1)}, u32[]{:S(2)}, u32[]{:S(2)}) collective-permute-start(bf16[2,256,256]{2,1,0:T(8,128)(2,1)} %get-tuple-element.328.refs_7_), channel_id=1, source_target_pairs={{0,8},{2,10},{4,12},{6,14},{8,0},{10,2},{12,4},{14,6},{16,24},{18,... | collective-permute-start | bytes 786440 | tf_op jit(solution)/shard_map/ppermute | solution.py:992
  333.7 22.4 %collective-permute-start.23 = (bf16[1,256,384]{2,1,0:T(8,128)(2,1)}, bf16[1,256,384]{2,1,0:T(8,128)(2,1)S(1)}, u32[]{:S(2)}, u32[]{:S(2)}) collective-permute-start(bf16[1,256,384]{2,1,0:T(8,128)(2,1)} %get-tuple-element.345), channel_id=1, source_target_pairs={{0,16},{2,18},{4,20},{6,22},{8,24},{10,26},{12,28},{14,30},{16,0},... | collective-permute-start | bytes 589832 | tf_op jit(solution)/shard_map/ppermute | solution.py:992
  348.7 35.5 %collective-permute-start.19 = (bf16[8,80,2048]{2,1,0:T(8,128)(2,1)}, bf16[8,80,2048]{2,1,0:T(8,128)(2,1)S(1)}, u32[]{:S(2)}, u32[]{:S(2)}) collective-permute-start(bf16[8,80,2048]{2,1,0:T(8,128)(2,1)} %get-tuple-element.331.refs_7_), channel_id=1, source_target_pairs={{0,2},{2,0},{4,6},{6,4},{8,10},{10,8},{12,14},{14,12},{16,18},{18,... | collective-permute-start | bytes 7864328 | tf_op jit(solution)/shard_map/ppermute | solution.py:992
  348.8 35.3 %collective-permute-start.20 = (bf16[8,64,1024]{2,1,0:T(8,128)(2,1)}, bf16[8,64,1024]{2,1,0:T(8,128)(2,1)S(1)}, u32[]{:S(2)}, u32[]{:S(2)}) collective-permute-start(bf16[8,64,1024]{2,1,0:T(8,128)(2,1)} %get-tuple-element.343), channel_id=1, source_target_pairs={{0,2},{2,0},{4,6},{6,4},{8,10},{10,8},{12,14},{14,12},{16,18},{18,... | collective-permute-start | bytes 3145736 | tf_op jit(solution)/shard_map/ppermute | solution.py:992
  355.1 29.2 %collective-permute-start.18 = (bf16[4,64,2048]{2,1,0:T(8,128)(2,1)}, bf16[4,64,2048]{2,1,0:T(8,128)(2,1)S(1)}, u32[]{:S(2)}, u32[]{:S(2)}) collective-permute-start(bf16[4,64,2048]{2,1,0:T(8,128)(2,1)} %get-tuple-element.342), channel_id=1, source_target_pairs={{0,4},{2,6},{4,0},{6,2},{8,12},{10,14},{12,8},{14,10},{16,20},{18,... | collective-permute-start | bytes 3145736 | tf_op jit(solution)/shard_map/ppermute | solution.py:992
  355.6 28.5 %collective-permute-start.21 = (bf16[2,256,384]{2,1,0:T(8,128)(2,1)}, bf16[2,256,384]{2,1,0:T(8,128)(2,1)S(1)}, u32[]{:S(2)}, u32[]{:S(2)}) collective-permute-start(bf16[2,256,384]{2,1,0:T(8,128)(2,1)} %get-tuple-element.332.refs_19_), channel_id=1, source_target_pairs={{0,8},{2,10},{4,12},{6,14},{8,0},{10,2},{12,4},{14,6},{16,24},{18,... | collective-permute-start | bytes 1179656 | tf_op jit(solution)/shard_map/ppermute | solution.py:992
  356.1 28.1 %collective-permute-start.22 = (bf16[1,256,256]{2,1,0:T(8,128)(2,1)}, bf16[1,256,256]{2,1,0:T(8,128)(2,1)S(1)}, u32[]{:S(2)}, u32[]{:S(2)}) collective-permute-start(bf16[1,256,256]{2,1,0:T(8,128)(2,1)} %get-tuple-element.344), channel_id=1, source_target_pairs={{0,16},{2,18},{4,20},{6,22},{8,24},{10,26},{12,28},{14,30},{16,0},... | collective-permute-start | bytes 393224 | tf_op jit(solution)/shard_map/ppermute | solution.py:992
  393.5 31.1 %collective-permute-start.30 = (bf16[4,80,2048]{2,1,0:T(8,128)(2,1)}, bf16[4,80,2048]{2,1,0:T(8,128)(2,1)S(1)}, u32[]{:S(2)}, u32[]{:S(2)}) collective-permute-start(bf16[4,80,2048]{2,1,0:T(8,128)(2,1)} %get-tuple-element.366), channel_id=1, source_target_pairs={{0,4},{2,6},{4,0},{6,2},{8,12},{10,14},{12,8},{14,10},{16,20},{18,... | collective-permute-start | bytes 3932168 | tf_op jit(solution)/shard_map/ppermute | solution.py:992
  417.9 43.6 %collective-permute-start.17 = (bf16[2,512,512]{2,1,0:T(8,128)(2,1)S(1)}, bf16[2,512,512]{2,1,0:T(8,128)(2,1)S(1)}, u32[]{:S(2)}, u32[]{:S(2)}) collective-permute-start(bf16[2,512,512]{2,1,0:T(8,128)(2,1)S(1)} %copy-done), channel_id=1, source_target_pairs={{0,1},{2,3},{4,5},{6,7},{8,9},{10,11},{12,13},{14,15},{16,17},{18,... | collective-permute-start | bytes 3145736 | tf_op jit(solution)/shard_map/ppermute | solution.py:996
  420.7 18.5 %collective-permute-start.24 = (bf16[4,64,1024]{2,1,0:T(8,128)(2,1)S(1)}, bf16[4,64,1024]{2,1,0:T(8,128)(2,1)S(1)}, u32[]{:S(2)}, u32[]{:S(2)}) collective-permute-start(bf16[4,64,1024]{2,1,0:T(8,128)(2,1)S(1)} %copy-done.47), channel_id=1, source_target_pairs={{0,4},{2,6},{4,0},{6,2},{8,12},{10,14},{12,8},{14,10},{16,20},{18,... | collective-permute-start | bytes 1572872 | tf_op jit(solution)/shard_map/ppermute | solution.py:992
  424.6 12.2 %collective-permute-start.26 = (bf16[1,256,384]{2,1,0:T(8,128)(2,1)}, bf16[1,256,384]{2,1,0:T(8,128)(2,1)S(1)}, u32[]{:S(2)}, u32[]{:S(2)}) collective-permute-start(bf16[1,256,384]{2,1,0:T(8,128)(2,1)} %get-tuple-element.351), channel_id=1, source_target_pairs={{0,16},{2,18},{4,20},{6,22},{8,24},{10,26},{12,28},{14,30},{16,0},... | collective-permute-start | bytes 589832 | tf_op jit(solution)/shard_map/ppermute | solution.py:992
  429.7 37.4 %collective-permute-start.32 = (bf16[2,80,2048]{2,1,0:T(8,128)(2,1)}, bf16[2,80,2048]{2,1,0:T(8,128)(2,1)S(1)}, u32[]{:S(2)}, u32[]{:S(2)}) collective-permute-start(bf16[2,80,2048]{2,1,0:T(8,128)(2,1)} %get-tuple-element.367.refs_7_), channel_id=1, source_target_pairs={{0,8},{2,10},{4,12},{6,14},{8,0},{10,2},{12,4},{14,6},{16,24},{18,... | collective-permute-start | bytes 1966088 | tf_op jit(solution)/shard_map/ppermute | solution.py:992
  431.3 26.3 %collective-permute-start.25 = (bf16[2,64,2048]{2,1,0:T(8,128)(2,1)S(1)}, bf16[2,64,2048]{2,1,0:T(8,128)(2,1)S(1)}, u32[]{:S(2)}, u32[]{:S(2)}) collective-permute-start(bf16[2,64,2048]{2,1,0:T(8,128)(2,1)S(1)} %copy-done.46), channel_id=1, source_target_pairs={{0,8},{2,10},{4,12},{6,14},{8,0},{10,2},{12,4},{14,6},{16,24},{18,... | collective-permute-start | bytes 1572872 | tf_op jit(solution)/shard_map/ppermute | solution.py:992
  436.8 30.2 %collective-permute-start.31 = (bf16[4,64,1024]{2,1,0:T(8,128)(2,1)}, bf16[4,64,1024]{2,1,0:T(8,128)(2,1)S(1)}, u32[]{:S(2)}, u32[]{:S(2)}) collective-permute-start(bf16[4,64,1024]{2,1,0:T(8,128)(2,1)} %get-tuple-element.368.refs_7_), channel_id=1, source_target_pairs={{0,4},{2,6},{4,0},{6,2},{8,12},{10,14},{12,8},{14,10},{16,20},{18,... | collective-permute-start | bytes 1572872 | tf_op jit(solution)/shard_map/ppermute | solution.py:992
  439.2 38.1 %collective-permute-start.33 = (bf16[4,64,1024]{2,1,0:T(8,128)(2,1)}, bf16[4,64,1024]{2,1,0:T(8,128)(2,1)S(1)}, u32[]{:S(2)}, u32[]{:S(2)}) collective-permute-start(bf16[4,64,1024]{2,1,0:T(8,128)(2,1)} %get-tuple-element.379), channel_id=1, source_target_pairs={{0,4},{2,6},{4,0},{6,2},{8,12},{10,14},{12,8},{14,10},{16,20},{18,... | collective-permute-start | bytes 1572872 | tf_op jit(solution)/shard_map/ppermute | solution.py:992
  460.9 13.6 %collective-permute-start.35 = (bf16[2,64,1024]{2,1,0:T(8,128)(2,1)}, bf16[2,64,1024]{2,1,0:T(8,128)(2,1)S(1)}, u32[]{:S(2)}, u32[]{:S(2)}) collective-permute-start(bf16[2,64,1024]{2,1,0:T(8,128)(2,1)} %get-tuple-element.369.refs_3_), channel_id=1, source_target_pairs={{0,8},{2,10},{4,12},{6,14},{8,0},{10,2},{12,4},{14,6},{16,24},{18,... | collective-permute-start | bytes 786440 | tf_op jit(solution)/shard_map/ppermute | solution.py:992
  461.5 15.8 %collective-permute-start.36 = (bf16[1,64,2048]{2,1,0:T(8,128)(2,1)}, bf16[1,64,2048]{2,1,0:T(8,128)(2,1)S(1)}, u32[]{:S(2)}, u32[]{:S(2)}) collective-permute-start(bf16[1,64,2048]{2,1,0:T(8,128)(2,1)} %get-tuple-element.381), channel_id=1, source_target_pairs={{0,16},{2,18},{4,20},{6,22},{8,24},{10,26},{12,28},{14,30},{16,0},... | collective-permute-start | bytes 786440 | tf_op jit(solution)/shard_map/ppermute | solution.py:992
  470.5 12.9 %collective-permute-start.34 = (bf16[2,64,1024]{2,1,0:T(8,128)(2,1)}, bf16[2,64,1024]{2,1,0:T(8,128)(2,1)S(1)}, u32[]{:S(2)}, u32[]{:S(2)}) collective-permute-start(bf16[2,64,1024]{2,1,0:T(8,128)(2,1)} %get-tuple-element.380.refs_9_), channel_id=1, source_target_pairs={{0,8},{2,10},{4,12},{6,14},{8,0},{10,2},{12,4},{14,6},{16,24},{18,... | collective-permute-start | bytes 786440 | tf_op jit(solution)/shard_map/ppermute | solution.py:992
  470.6 19.2 %collective-permute-start.37 = (bf16[4,64,1024]{2,1,0:T(8,128)(2,1)S(1)}, bf16[4,64,1024]{2,1,0:T(8,128)(2,1)S(1)}, u32[]{:S(2)}, u32[]{:S(2)}) collective-permute-start(bf16[4,64,1024]{2,1,0:T(8,128)(2,1)S(1)} %copy-done.45), channel_id=1, source_target_pairs={{0,4},{2,6},{4,0},{6,2},{8,12},{10,14},{12,8},{14,10},{16,20},{18,... | collective-permute-start | bytes 1572872 | tf_op jit(solution)/shard_map/ppermute | solution.py:992
  474.5 15.5 %collective-permute-start.39 = (bf16[1,80,2048]{2,1,0:T(8,128)(2,1)}, bf16[1,80,2048]{2,1,0:T(8,128)(2,1)S(1)}, u32[]{:S(2)}, u32[]{:S(2)}) collective-permute-start(bf16[1,80,2048]{2,1,0:T(8,128)(2,1)} %get-tuple-element.389), channel_id=1, source_target_pairs={{0,16},{2,18},{4,20},{6,22},{8,24},{10,26},{12,28},{14,30},{16,0},... | collective-permute-start | bytes 983048 | tf_op jit(solution)/shard_map/ppermute | solution.py:992
  (65 other events, 439.4 us)

commit v3 on v2

--- a/solution.py
+++ b/solution.py
@@ -18,7 +18,7 @@
 COMP = 256
 CTX = MEM + CMEM
 HALF = SEG // 2
-HP = 4
+HP = 8
 
 EPS = 1e-05
 NEG = -1e30
@@ -71,7 +71,7 @@
     return inverse * (scaled - jnp.mean(scaled, axis=-1, keepdims=True) - unit * along)
 
 
-ANY = pl.BlockSpec(memory_space=pl.ANY)
+ANY = pl.BlockSpec(memory_space=pltpu.HBM)
 
 
 def call(kernel, name, scalars, ins, outs, scratch, tokens, aliases=None, estimate=LONG, specs=None):
@@ -122,50 +122,45 @@
     return [ref.at[:, pl.ds(i * size, size)] for i in range(ref.shape[1] // size)]
 
 
-def memory_kernel(flags, comp, mem, gain, w, normed, kv, rows, weights, unit_rows, out, sems):
+def memory_kernel(seq, flags, comp, mem, gain, w, normed, kv, rows, weights, unit_rows, out, sems):
     copies = Copies(sems)
-    seqs = comp.shape[0]
-    jobs = [(s, j) for s in range(seqs) for j in range(2)]
-    for n, (s, j) in enumerate(jobs):
-        copies.start((comp, mem)[j].at[s], rows.at[n], ("rows", n))
-        if n == 0:
-            for t in range(2):
-                copies.start(w.at[:, pl.ds((1 + t) * WIDTH, WIDTH)], weights.at[t], ("w", t))
+    for n, source in enumerate((comp, mem)):
+        copies.start(source.at[seq], rows.at[n], ("rows", n))
+        copies.start(w.at[:, pl.ds((1 + n) * WIDTH, WIDTH)], weights.at[n], ("w", n))
+    keep = (1 - flags[seq]).astype(F32)
 
     def unit(n):
         copies.wait(("rows", n))
-        keep = (1 - flags[jobs[n][0]]).astype(F32)
         value, _ = normalise(rows[n].astype(F32) * keep)
         unit_rows[n] = (value * gain[...].astype(F32)).astype(BF)
 
     unit(0)
-    for n, (s, j) in enumerate(jobs):
-        place = pl.ds(j * MEM, MEM)
-        copies.start(unit_rows.at[n], normed.at[s, place])
+    for n in range(2):
+        place = pl.ds(n * MEM, MEM)
+        copies.start(unit_rows.at[n], normed.at[0, place])
         for t in range(2):
             if n == 0:
                 copies.wait(("w", t))
             out[n, :, t * WIDTH : (t + 1) * WIDTH] = nn(unit_rows[n], weights[t]).astype(BF)
-            if t == 0 and n + 1 < len(jobs):
-                unit(n + 1)
-        copies.start(out.at[n], kv.at[s, place])
+            if n == 0 and t == 0:
+                unit(1)
+        copies.start(out.at[n], kv.at[0, place])
     copies.wait_all()
 
 
-def memory_keyvals(flags, compressed, memory, gain, w_proj, tokens):
-    seqs = memory.shape[0]
+def memory_keyvals(seq, flags, compressed, memory, gain, w_proj, tokens):
     return call(
-        memory_kernel,
+        lambda *refs: memory_kernel(seq, *refs),
         "memory_keyvals",
         [flags],
         [compressed, memory, gain, w_proj],
-        [shape((seqs, CTX, WIDTH)), shape((seqs, CTX, 2 * WIDTH))],
+        [shape((1, CTX, WIDTH)), shape((1, CTX, 2 * WIDTH))],
         [
-            pltpu.VMEM((2 * seqs, MEM, WIDTH), BF),
+            pltpu.VMEM((2, MEM, WIDTH), BF),
             pltpu.VMEM((2, WIDTH, WIDTH), BF),
-            pltpu.VMEM((2 * seqs, MEM, WIDTH), BF),
-            pltpu.VMEM((2 * seqs, MEM, 2 * WIDTH), BF),
-            pltpu.SemaphoreType.DMA((6 * seqs + 2,)),
+            pltpu.VMEM((2, MEM, WIDTH), BF),
+            pltpu.VMEM((2, MEM, 2 * WIDTH), BF),
+            pltpu.SemaphoreType.DMA((8,)),
         ],
         tokens,
         specs=[ANY, ANY, whole(1, WIDTH), ANY],
@@ -270,7 +265,7 @@
             loads.start(part if lead is None else part.at[lead], x.at[:, pl.ds(i * wide, wide)], ("x", i))
         for t, tile in enumerate(tiles(w_proj, 1)):
             loads.start(tile, pool.at[t], ("proj", t))
-        loads.start(kv_memory.at[seq], kvm, "kvm")
+        loads.start(kv_memory.at[0], kvm, "kvm")
         loads.start(w_out, wo, "out")
         for t, tile in enumerate(tiles(w_up, 1)):
             loads.start(tile, pool.at[4 + t], ("up", t))
@@ -303,7 +298,7 @@
         loads.wait_all()
 
         def feed(t, _):
-            cuts = [pl.ds(pl.multiple_of(t * 1024 + i * FS, FS), FS) for i in range(1024 // FS)]
+            cuts = [pl.ds(t * 1024 + i * FS, FS) for i in range(1024 // FS)]
             ups = [
                 nn(held["ffn_in"][...], pool[4 + t, :, i * FS : (i + 1) * FS]) + b_up[:, c].astype(F32)
                 for i, c in enumerate(cuts)
@@ -322,10 +317,11 @@
             return 0
 
         def feed_copy(name, sem, t):
-            place = pl.ds(pl.multiple_of(t * 1024, 1024), 1024)
+            place = pl.ds(t * 1024, 1024)
             return pltpu.make_async_copy(held[name].at[:, place], out[name].at[seq, :, place], feed_sems.at[sem, t])
 
-        lax.fori_loop(0, FF // 1024, feed, 0)
+        for t in range(FF // 1024):
+            feed(t, 0)
         rows = total[...].astype(BF)
         y_rows[...] = rows
         held["y_low"][...] = rows[:, : WIDTH // 2]
@@ -338,7 +334,7 @@
         stores.wait_all()
 
 
-def forward(seq, seqs, scalars, xs, kv_memory, params, saved, tokens):
+def forward(seq, seqs, scalars, xs, kv_memory, params, saved, tokens, estimate):
     gain_attn, w_proj, w_out, gain_ffn, w_up, b_up, w_down, b_down = params
     args = [v for v, _ in xs] + [gain_attn, w_proj, kv_memory, w_out, gain_ffn, w_up, b_up, w_down, b_down]
     specs = [ANY] * len(xs) + [
@@ -371,7 +367,8 @@
         ],
         tokens,
         aliases,
-        specs=specs,
+        estimate,
+        specs,
     )
     return results[0], dict(zip([name for name, _, _ in SAVED], results[1:]))
 
@@ -398,9 +395,10 @@
     @pl.when(active[0] == 1)
     def _():
         loads, stores = Copies(in_sems), Copies(out_sems)
-        for i, (part, lead) in enumerate(zip(gys, leads)):
-            wide = WIDTH // len(leads)
-            loads.start(part if lead is None else part.at[lead], gy_rows.at[:, pl.ds(i * wide, wide)], ("gy", i))
+        for i, (part, (lead, row, column)) in enumerate(zip(gys, leads)):
+            source = part if lead is None else part.at[lead]
+            tall, wide = source.shape
+            loads.start(source, gy_rows.at[pl.ds(row, tall), pl.ds(column, wide)], ("gy", i))
         downs, ups = tiles(w_down, 0), tiles(w_up, 1)
         for t in range(FF // 1024):
             loads.start(downs[t], pool.at[t], ("down", t))
@@ -435,17 +433,17 @@
         stores.wait_all()
 
 
-def feed_back(seq, scalars, gys, saved, params, fed, tokens):
+def feed_back(seq, scalars, gys, saved, params, fed, tokens, estimate=LONG):
     gain_attn, w_proj, w_out, gain_ffn, w_up, b_up, w_down, b_down = params
     seqs = saved["gate"].shape[0]
-    args = [v for v, _ in gys] + [w_down, saved["gate"], w_up, saved["residual"], gain_ffn, w_out]
+    args = [v for v, *_ in gys] + [w_down, saved["gate"], w_up, saved["residual"], gain_ffn, w_out]
     specs = [ANY] * (len(gys) + 4) + [whole(1, WIDTH), ANY]
     aliases = {}
     if fed is not None:
         aliases = {len(scalars) + len(args) + i: i for i in range(len(FED))}
         args += [fed[name] for name, _, _ in FED]
         specs += [ANY] * len(FED)
-    leads = [lead for _, lead in gys]
+    leads = [place for _, *place in gys]
     results = call(
         lambda *refs: feed_back_kernel(seq, leads, len(aliases), *refs),
         "feed_back",
@@ -465,7 +463,8 @@
         ],
         tokens,
         aliases,
-        specs=specs,
+        estimate,
+        specs,
     )
     return dict(zip([name for name, _, _ in FED], results))
 
@@ -519,7 +518,7 @@
         made["dq"][high, c] = ((both[:, high] + nn(turned[:, high], ds_high)) * SCALE).T.astype(BF)
 
 
-def attend_back_kernel(seq, aliased, active, flags, bounds, *refs):
+def attend_back_kernel(seq, part, aliased, active, flags, bounds, *refs):
     (qkv_in, kv_memory, d_out_in, out_in, stat_in, w_proj, x_in, gain, d_residual), refs = refs[:9], refs[9:]
     refs = refs[aliased:]
     dx, refs = refs[0], refs[1:]
@@ -539,12 +538,12 @@
             g = g * wide if isinstance(g, int) else pl.multiple_of(g * wide, wide)
             sems = head_sems.at[g // wide]
             pairs = [
-                (ref.at[seq, :, pl.ds(base * WIDTH + g, wide)], target.at[:, pl.ds(base * WIDTH + g, wide)])
-                for ref, target, bases in (
-                    (qkv_in, qkv, 3),
-                    (kv_memory, kvm, 2),
-                    (d_out_in, d_out, 1),
-                    (out_in, out, 1),
+                (ref.at[lead, :, pl.ds(base * WIDTH + g, wide)], target.at[:, pl.ds(base * WIDTH + g, wide)])
+                for ref, lead, target, bases in (
+                    (qkv_in, seq, qkv, 3),
+                    (kv_memory, 0, kvm, 2),
+                    (d_out_in, seq, d_out, 1),
+                    (out_in, seq, out, 1),
                 )
                 for base in range(bases)
             ]
@@ -571,19 +570,21 @@
         for name, _, _ in MADE[:5]:
             stores.start(made[name], result[name].at[seq])
         loads.wait_all()
-        grad = nt(made["dq"][...], pool[0]) + nt(made["dkx"][...], pool[1]) + nt(made["dvx"][...], pool[2])
-        unit, inverse = normalise(x[...].astype(F32))
-        value = (rows[...] + norm_back(unit, inverse, gain[...].astype(F32), grad)).astype(BF)
-        dx_rows[...] = value
-        made["dx_low"][...] = value[:, : WIDTH // 2]
-        made["dx_high"][...] = value[:, WIDTH // 2 :]
-        stores.start(dx_rows, dx)
-        for name, _, _ in MADE[5:]:
-            stores.start(made[name], result[name].at[seq])
+        top = slice(0, part)
+        grad = nt(made["dq"][top], pool[0]) + nt(made["dkx"][top], pool[1]) + nt(made["dvx"][top], pool[2])
+        unit, inverse = normalise(x[top].astype(F32))
+        value = (rows[top] + norm_back(unit, inverse, gain[...].astype(F32), grad)).astype(BF)
+        dx_rows[top] = value
+        stores.start(dx_rows.at[pl.ds(0, part)], dx)
+        if part == SEG:
+            made["dx_low"][...] = value[:, : WIDTH // 2]
+            made["dx_high"][...] = value[:, WIDTH // 2 :]
+            for name, _, _ in MADE[5:]:
+                stores.start(made[name], result[name].at[seq])
         stores.wait_all()
 
 
-def attend_back(seq, scalars, saved, fed, kv_memory, params, made, tokens, estimate=LONG):
+def attend_back(seq, scalars, saved, fed, kv_memory, params, made, tokens, estimate=LONG, part=SEG):
     gain_attn, w_proj, w_out, gain_ffn, w_up, b_up, w_down, b_down = params
     seqs = saved["qkv"].shape[0]
     args = [
@@ -604,11 +605,11 @@
         args += [made[name] for name, _, _ in MADE]
         specs += [ANY] * len(MADE)
     results = call(
-        lambda *refs: attend_back_kernel(seq, len(aliases), *refs),
+        lambda *refs: attend_back_kernel(seq, part, len(aliases), *refs),
         "attend_back",
         scalars,
         args,
-        [shape((SEG, WIDTH))] + [shape((seqs,) + dims, dtype) for _, dims, dtype in MADE],
+        [shape((part, WIDTH))] + [shape((seqs,) + dims, dtype) for _, dims, dtype in MADE],
         [pltpu.VMEM(dims, dtype) for _, dims, dtype in MADE]
         + [
             pltpu.VMEM((SEG, 3 * WIDTH), BF),
@@ -634,6 +635,50 @@
     return results[0], dict(zip([name for name, _, _ in MADE], results[1:]))
 
 
+def project_back_kernel(seq, active, dq, dkx, dvx, w_proj, x, gain, d_residual, dx, grads, pool, xs, rows, dx_rows, sems):
+    @pl.when(active[0] == 1)
+    def _():
+        copies = Copies(sems)
+        place = pl.ds(SEG - HALF, HALF)
+        for n, (ref, tile) in enumerate(zip((dq, dkx, dvx), tiles(w_proj, 1))):
+            copies.start(ref.at[seq, place], grads.at[n], ("grad", n))
+            copies.start(tile, pool.at[n], ("w", n))
+        copies.start(x.at[seq, place], xs, "x")
+        copies.start(d_residual.at[seq, place], rows, "rows")
+        grad = None
+        for n in range(3):
+            copies.wait(("grad", n), ("w", n))
+            term = nt(grads[n], pool[n])
+            grad = term if grad is None else grad + term
+        copies.wait_all()
+        unit, inverse = normalise(xs[...].astype(F32))
+        dx_rows[...] = (rows[...] + norm_back(unit, inverse, gain[...].astype(F32), grad)).astype(BF)
+        copies.start(dx_rows, dx)
+        copies.wait_all()
+
+
+def project_back(seq, scalars, saved, fed, params, made, tokens):
+    gain_attn, w_proj = params[:2]
+    return call(
+        lambda *refs: project_back_kernel(seq, *refs),
+        "project_back",
+        scalars,
+        [made["dq"], made["dkx"], made["dvx"], w_proj, saved["x"], gain_attn, fed["d_residual"]],
+        [shape((HALF, WIDTH))],
+        [
+            pltpu.VMEM((3, HALF, WIDTH), BF),
+            pltpu.VMEM((3, WIDTH, WIDTH), BF),
+            pltpu.VMEM((HALF, WIDTH), BF),
+            pltpu.VMEM((HALF, WIDTH), F32),
+            pltpu.VMEM((HALF, WIDTH), BF),
+            pltpu.SemaphoreType.DMA((9,)),
+        ],
+        tokens,
+        estimate=LONG,
+        specs=[ANY] * 5 + [whole(1, WIDTH), ANY],
+    )[0]
+
+
 def compress_kernel(flags, grouped, w, bias, out, rows, weights, result, sems):
     copies = Copies(sems)
     copies.start(grouped, rows, "rows")
@@ -650,21 +695,23 @@
     seqs = memory.shape[0]
     wide = RATE * WIDTH
     grouped = memory.reshape(seqs, COMP, wide)
-    return call(
-        compress_kernel,
-        "compress",
-        [flags],
-        [grouped, w_compress.reshape(wide, WIDTH), b_compress],
-        [shape((seqs, COMP, WIDTH))],
-        [
-            pltpu.VMEM((seqs, COMP, wide), BF),
-            pltpu.VMEM((wide, WIDTH), BF),
-            pltpu.VMEM((seqs, COMP, WIDTH), BF),
-            pltpu.SemaphoreType.DMA((2 + seqs,)),
-        ],
-        tokens,
-        estimate=SHORT,
-        specs=[ANY, ANY, whole(1, WIDTH)],
+    return list(
+        call(
+            compress_kernel,
+            "compress",
+            [flags],
+            [grouped, w_compress.reshape(wide, WIDTH), b_compress],
+            [shape((seqs, COMP, WIDTH))],
+            [
+                pltpu.VMEM((seqs, COMP, wide), BF),
+                pltpu.VMEM((wide, WIDTH), BF),
+                pltpu.VMEM((seqs, COMP, WIDTH), BF),
+                pltpu.SemaphoreType.DMA((2 + seqs,)),
+            ],
+            tokens,
+            estimate=SHORT,
+            specs=[ANY, ANY, whole(1, WIDTH)],
+        )
     )
 
 
@@ -680,7 +727,7 @@
 
 class Either(list):
     def __init__(self, arrays, places):
-        super().__init__(arrays)
+        super().__init__((v, None) for v in arrays)
         self.places = places
 
 
@@ -697,37 +744,192 @@
     return made
 
 
-def weight_kernel(size, groups, tasks, chunks, places, small_chunk, section, mine, *refs):
+class Sides:
+    def __init__(self, groups, tasks, ins, held, section, loads):
+        self.groups, self.held, self.section, self.loads = groups, held, section, loads
+        self.parts, self.either, self.ready, at = [], {}, set(), 0
+        for g in groups:
+            self.parts.append(ins[at : at + len(g)])
+            at += len(g)
+        for key in dict.fromkeys(k for t in tasks for k in (t["left"], t["right"])):
+            g, tile = key
+            if isinstance(groups[g], Either):
+                choices = either_copies(groups[g], self.parts[g], held[g], loads.sems, loads.count)
+                for wanted, copies in choices:
+                    pl.when(section[0] == wanted)(lambda copies=copies: [c.start() for c in copies] and None)
+                self.either[g] = choices
+                loads.count += max(len(copies) for _, copies in choices)
+                continue
+            place, row = pl.ds(tile * 1024, 1024), 0
+            for n, (ref, (_, lead)) in enumerate(zip(self.parts[g], groups[g])):
+                rows = ref.shape[-2]
+                source = ref.at[:, place] if lead is None else ref.at[lead, :, place]
+                loads.start(source, held[g].at[pl.ds(row, rows), place], key + (n,))
+                row += rows
+
+    def wait(self, task):
+        for key in (task["left"], task["right"]):
+            if key in self.ready:
+                continue
+            self.ready.add(key)
+            if key[0] in self.either:
+                for wanted, copies in self.either[key[0]]:
+                    pl.when(self.section[0] == wanted)(lambda copies=copies: [c.wait() for c in copies] and None)
+            else:
+                self.loads.wait(*[key + (m,) for m in range(len(self.parts[key[0]]))])
+
+    def product(self, task, first, width):
+        (left, lt), (right, rt) = task["left"], task["right"]
+        return tn(
+            self.held[left][:, lt * 1024 : (lt + 1) * 1024],
+            self.held[right][:, rt * 1024 + first : rt * 1024 + first + width],
+        )
+
+
+def side_buffers(groups):
+    made = []
+    for g in groups:
+        if isinstance(g, Either):
+            made.append(pltpu.VMEM((SEG, WIDTH), BF))
+        else:
+            made.append(pltpu.VMEM((sum(v.shape[-2] for v, _ in g), g[0][0].shape[-1]), BF))
+    return made, sum(len(g) * max(1, g[0][0].shape[-1] // 1024) for g in groups)
+
+
+def early_kernel(groups, jobs, outs, section, *refs):
     total = sum(len(g) for g in groups)
     ins, refs = refs[:total], refs[total:]
+    outs, refs = refs[:outs], refs[outs:]
+    held, (staged, side_sems, out_sems) = refs[: len(groups)], refs[len(groups) :]
+    parts, at = [], 0
+    for g in groups:
+        parts.append(ins[at : at + len(g)])
+        at += len(g)
+    first, used = {}, 0
+    for g, group in enumerate(groups):
+        first[g] = used
+        used += len(group) * max(1, held[g].shape[1] // 1024)
+
+    def place(t):
+        return pl.ds(t * 1024 if isinstance(t, int) else pl.multiple_of(t * 1024, 1024), 1024)
+
+    def side(g, t, act):
+        if isinstance(groups[g], Either):
+            for wanted, copies in either_copies(groups[g], parts[g], held[g], side_sems, first[g]):
+                pl.when(section[0] == wanted)(lambda copies=copies: [act(c) for c in copies] and None)
+            return
+        row, many = 0, held[g].shape[1] // 1024
+        for n, (ref, (_, lead)) in enumerate(zip(parts[g], groups[g])):
+            rows = ref.shape[-2]
+            sem = side_sems.at[first[g] + n * many + t]
+            target = held[g].at[pl.ds(row, rows), place(t)]
+            act(pltpu.make_async_copy(ref.at[lead, :, place(t)], target, sem))
+            row += rows
+
+    begin, end = (lambda copy: copy.start()), (lambda copy: copy.wait())
+    done = set()
+    for job in jobs:
+        for key, loops in ((job["left"], job["loop"] == "left"), (job["right"], job["loop"] == "right")):
+            if key in done:
+                continue
+            done.add(key)
+            for t in range(job["count"]) if loops else [0]:
+                side(key, t, begin)
+
+    n, done = 0, set()
+    for job in jobs:
+        left, right, loop = job["left"], job["right"], job["loop"]
+        for key, loops in ((left, loop == "left"), (right, loop == "right")):
+            if not loops and key not in done:
+                done.add(key)
+                side(key, 0, end)
+
+        def store(t, slot, job=job):
+            row, column = job["at"]
+            if loop == "left":
+                row += t * 1024
+            elif loop == "right":
+                column += t * 1024
+            if not isinstance(t, int):
+                row, column = pl.multiple_of(row, 1024), pl.multiple_of(column, 1024)
+            target = outs[job["out"]].at[pl.ds(row, 1024), pl.ds(column, 1024)]
+            return pltpu.make_async_copy(staged.at[slot], target, out_sems.at[slot])
+
+        def step(t, _, job=job, base=n):
+            slot = (base + t) % 2
+            if loop is not None:
+                side(left if loop == "left" else right, t, end)
+            lt, rt = (t if loop == "left" else 0), (t if loop == "right" else 0)
+
+            @pl.when(base + t >= 2)
+            def _():
+                store(t, slot).wait()
+
+            product = tn(held[left][:, place(lt)], held[right][:, place(rt)])
+            staged[slot] = product.astype(BF)
+            store(t, slot).start()
+            return 0
+
+        if job["count"] == 1:
+            step(0, 0)
+        else:
+            lax.fori_loop(0, job["count"], step, 0)
+        n += job["count"]
+    for slot in range(2):
+        pltpu.make_async_copy(staged.at[slot], outs[0].at[pl.ds(0, 1024), pl.ds(0, 1024)], out_sems.at[slot]).wait()
+
+
+def early_grads(section, groups, jobs, outs, tokens):
+    buffers, loads = side_buffers(groups)
+    return list(
+        call(
+            lambda *refs: early_kernel(groups, jobs, len(outs), *refs),
+            "early_grads",
+            [section],
+            [v for g in groups for v, _ in g],
+            [shape(dims) for dims in outs],
+            buffers
+            + [
+                pltpu.VMEM((2, 1024, 1024), BF),
+                pltpu.SemaphoreType.DMA((loads,)),
+                pltpu.SemaphoreType.DMA((2,)),
+            ],
+            tokens,
+            estimate=SHORT,
+        )
+    )
+
+
+def unset(dims, tokens):
+    def kernel(*refs):
+        pass
+
+    return list(call(kernel, "unset", [], [], [shape(d) for d in dims], [], tokens, estimate=SHORT))
+
+
+def weight_kernel(size, groups, tasks, chunks, places, small_chunk, bases, section, mine, *refs):
+    total = sum(len(g) for g in groups)
+    ins, base, refs = refs[:total], refs[total : total + 2 * bases], refs[total + 2 * bases :]
     if small_chunk is not None:
         small, refs = refs[0], refs[1:]
     sends, refs = refs[: len(chunks)], refs[len(chunks) :]
     keeps, refs = refs[: len(chunks)], refs[len(chunks) :]
     held, refs = refs[: len(groups)], refs[len(groups) :]
-    staged, small_rows, in_sems, out_sems = refs
+    staged, small_rows, so_far, in_sems, out_sems, base_sems = refs
     loads, stores = Copies(in_sems), Copies(out_sems)
     even = (mine[0] & 1) == 0
-    parts, at = [], 0
-    for g in groups:
-        parts.append(ins[at : at + len(g)])
-        at += len(g)
-
-    either = {}
-    for key in dict.fromkeys(k for t in tasks for k in (t["left"], t["right"])):
-        g, tile = key
-        place, row = pl.ds(tile * 1024, 1024), 0
-        if isinstance(groups[g], Either):
-            for wanted, copies in either_copies(groups[g], parts[g], held[g], in_sems, loads.count):
-                pl.when(section[0] == wanted)(lambda copies=copies: [c.start() for c in copies] and None)
-            either[g] = either_copies(groups[g], parts[g], held[g], in_sems, loads.count)
-            loads.count += max(len(copies) for _, copies in either[g])
-            continue
-        for n, ref in enumerate(parts[g]):
-            loads.start(ref.at[:, place], held[g].at[pl.ds(row, ref.shape[0]), place], key + (n,))
-            row += ref.shape[0]
-    ready = set()
-
+    sides = Sides(groups, tasks, ins, held, section, loads)
+
+    def base_copy(n, which=0):
+        k, row, column = tasks[n]["base"]
+        source = base[k + which * bases].at[pl.ds(row, 1024), pl.ds(column, 1024)]
+        return pltpu.make_async_copy(source, so_far.at[n % 2], base_sems.at[n % 2])
+
+    def begin_base(n):
+        for which in range(2):
+            pl.when(section[0] == which)(lambda which=which: base_copy(n, which).start())
+
+    begin_base(0)
     if small_chunk is not None:
         for pair in range(size // 2):
             place = places[small_chunk][2 * pair]
@@ -736,77 +938,72 @@
             small_rows[1, place] = jnp.where(even, one, two)
         for i, target in enumerate((sends, keeps)):
             rows = target[small_chunk].shape[1] - 16
-            stores.start(small_rows.at[i], target[small_chunk].at[:, pl.ds(rows, 16), pl.ds(0, WIDTH)], ("small", i))
+            stores.start(
+                small_rows.at[i], target[small_chunk].at[:, pl.ds(rows, 16), pl.ds(0, WIDTH)], ("small", i)
+            )
 
     busy = {}
     for n, task in enumerate(tasks):
         slot = n % 2
-        for key in (task["left"], task["right"]):
-            if key not in ready:
-                ready.add(key)
-                if key[0] in either:
-                    for wanted, copies in either[key[0]]:
-                        pl.when(section[0] == wanted)(lambda copies=copies: [c.wait() for c in copies] and None)
-                else:
-                    loads.wait(*[key + (m,) for m in range(len(parts[key[0]]))])
+        sides.wait(task)
         for name in busy.pop(slot, ()):
             stores.wait(name)
+        base_copy(n).wait()
+        if n + 1 < len(tasks):
+            begin_base(n + 1)
         count = size // task["blocks"]
         rows = 1024 // count
-        (left, lt), (right, rt) = task["left"], task["right"]
         for cut in range(1024 // WIDE):
             c = slice(cut * WIDE, (cut + 1) * WIDE)
-            value = tn(
-                held[left][:, lt * 1024 : (lt + 1) * 1024],
-                held[right][:, rt * 1024 + cut * WIDE : rt * 1024 + (cut + 1) * WIDE],
-            ).astype(BF)
+            value = (sides.product(task, cut * WIDE, WIDE) + so_far[slot, :, c].astype(F32)).astype(BF)
             for pair in range(count // 2):
                 one = value[(2 * pair) * rows : (2 * pair + 1) * rows]
                 two = value[(2 * pair + 1) * rows : (2 * pair + 2) * rows]
                 staged[slot, 0, pair, :, c] = jnp.where(even, two, one)
                 staged[slot, 1, pair, :, c] = jnp.where(even, one, two)
         names = []
-        for k, first, width, base in task["outs"]:
+        for k, first, width, start in task["outs"]:
             for i, target in enumerate((sends, keeps)):
                 for pair in range(count // 2):
                     names.append((n, k, i, pair))
                     stores.start(
                         staged.at[slot, i, pair, :, pl.ds(first, width)],
-                        target[k].at[places[k][task["block"] * count + 2 * pair], pl.ds(0, rows), pl.ds(base, width)],
+                        target[k].at[places[k][task["block"] * count + 2 * pair], pl.ds(0, rows), pl.ds(start, width)],
                         names[-1],
                     )
         busy[slot] = names
     stores.wait_all()
 
 
-def weight_grads(section, mine, size, groups, tasks, chunks, tokens, places, small=None, small_chunk=None):
+def weight_grads(
+    section, mine, size, groups, bases, tasks, chunks, tokens, places, small=None, small_chunk=None, estimate=LONG
+):
     outs = []
     for k, (blocks, columns) in enumerate(chunks):
         rows = blocks * 1024 // size + (16 if k == small_chunk else 0)
         outs.append(shape((size // 2, rows, columns)))
-    args = [v for g in groups for v in g] + ([small] if small is not None else [])
-    specs = [ANY] * sum(len(g) for g in groups) + ([whole(*small.shape)] if small is not None else [])
+    args = [v for g in groups for v, _ in g] + [v for side in zip(*bases) for v in side]
+    args += [small] if small is not None else []
+    specs = [ANY] * (sum(len(g) for g in groups) + 2 * len(bases)) + ([whole(*small.shape)] if small is not None else [])
     count = size // tasks[0]["blocks"]
-
-    def buffer(g):
-        if isinstance(g, Either):
-            return pltpu.VMEM((2 * SEG, WIDTH), BF)
-        return pltpu.VMEM((sum(v.shape[0] for v in g), g[0].shape[1]), BF)
-
+    buffers, loads = side_buffers(groups)
     results = call(
-        lambda *refs: weight_kernel(size, groups, tasks, chunks, places, small_chunk, *refs),
+        lambda *refs: weight_kernel(size, groups, tasks, chunks, places, small_chunk, len(bases), *refs),
         "weight_grads",
         [section, mine],
         args,
         outs + outs,
-        [buffer(g) for g in groups]
+        buffers
         + [
             pltpu.VMEM((2, 2, count // 2, 1024 // count, 1024), BF),
             pltpu.VMEM((2, size // 2, 16, WIDTH), BF),
-            pltpu.SemaphoreType.DMA((sum(len(g) * max(1, g[0].shape[-1] // 1024) for g in groups),)),
+            pltpu.VMEM((2, 1024, 1024), BF),
+            pltpu.SemaphoreType.DMA((loads,)),
             pltpu.SemaphoreType.DMA((2 + sum(count * len(t["outs"]) for t in tasks),)),
+            pltpu.SemaphoreType.DMA((2,)),
         ],
         tokens,
+        estimate=estimate,
         specs=specs,
     )
     return list(zip(results[: len(chunks)], results[len(chunks) :]))
@@ -1032,54 +1229,131 @@
     last = [[]]
 
     other_x = [one_way(inputs[0], 1, 0)]
-    normed_memory, kv_memory = memory_keyvals(reset_flags, compressed, memory, gain_attn, w_proj, [])
-    last[0] = [kv_memory]
-    inputs_later, kv_memory = both_after(inputs, kv_memory)
+    normed_memory, kv_memory = [], []
+
+    def keyvals(s):
+        normed, kv = memory_keyvals(s, reset_flags, compressed, memory, gain_attn, w_proj, last[0])
+        last[0] = [kv]
+        normed_memory.append(normed)
+        kv_memory.append(kv)
+
+    keyvals(0)
+    kv_memory[0], inputs_later = both_after(kv_memory[0], inputs)
     other_x.append(one_way(inputs_later[1], 1, 0))
 
-    def ahead(layer, s, xs, saved):
+    def ahead(layer, s, xs, saved, estimate):
         scalars = [active[layer], reset_flags, boundary]
-        y, saved = forward(s, seqs, scalars, xs, kv_memory, params, saved, last[0])
+        y, saved = forward(s, seqs, scalars, xs, kv_memory[s], params, saved, last[0], estimate)
         last[0] = [y]
         return y, saved
 
-    y_a0, saved = ahead(0, 0, ((inputs, 0), (other_x[0], None)), None)
+    y_a0, saved = ahead(0, 0, ((inputs, 0), (other_x[0], None)), None, LONG)
     hop_a = one_way(y_a0, 0, 1)
-    y_b0, saved = ahead(0, 1, ((inputs, 1), (other_x[1], None)), saved)
+    keyvals(1)
+    y_b0, saved = ahead(0, 1, ((inputs, 1), (other_x[1], None)), saved, SHORT)
     y_b0, cotangent_later = both_after(y_b0, cotangent)
-    y_b0, memory_later = both_after(y_b0, memory)
     hop_b = one_way(y_b0, 0, 1)
-    other_gy = one_way(cotangent_later, 0, 1)
-    squeezed = compress(reset_flags, memory_later, w_compress[0], b_compress, last[0])[0]
-    last[0] = [squeezed]
-    y_a1, saved = ahead(1, 0, ((hop_a, None),), saved)
-    y_b1, saved = ahead(1, 1, ((hop_b, None),), saved)
-    other_y = one_way(saved["y_low"], 1, 0)
-
-    def back(layer, s, gys, fed, made):
-        fed = feed_back(s, [active[layer]], gys, saved, params, fed, last[0])
+    other_gy = [one_way(cotangent_later[s], 0, 1) for s in range(seqs)]
+
+    def squeeze(layer):
+        tokens = last[0]
+        work = lambda: compress(reset_flags, memory, w_compress[0], b_compress, tokens)
+        skip = lambda: unset([(seqs, COMP, WIDTH)], tokens)
+        made = lax.cond(section == layer, work, skip)[0]
+        last[0] = [made]
+        return made
+
+    squeezed_first = squeeze(0)
+
+    def back(layer, s, gys, fed, made, estimate, part=SEG):
+        fed = feed_back(s, [active[layer]], gys, saved, params, fed, last[0], estimate)
         scalars = [active[layer], reset_flags, boundary]
-        dx, made = attend_back(s, scalars, saved, fed, kv_memory, params, made, [], SHORT)
+        dx, made = attend_back(s, scalars, saved, fed, kv_memory[s], params, made, [], SHORT, part)
         last[0] = [dx]
         return dx, fed, made
 
-    dx_a1, fed, made = back(1, 0, ((other_gy, 0), (cotangent, 0)), None, None)
+    y_a1, saved = ahead(1, 0, ((hop_a, None),), saved, SHORT)
+    dx_a1, fed, made = back(1, 0, ((other_gy[0], None, 0, 0), (cotangent, 0, 0, width)), None, None, SHORT)
     back_a = one_way(dx_a1, 1, 0)
-    dx_b1, fed, made = back(1, 1, ((other_gy, 1), (cotangent, 1)), fed, made)
-    back_b = one_way(dx_b1, 1, 0)
-    dx_a0, fed, made = back(0, 0, ((back_a, None),), fed, made)
-
-    rows_of = lambda v: v.reshape((-1, v.shape[-1]))
-    half = WIDTH // 2
-    gy_all = Either(
-        [back_a, back_b, other_gy, cotangent],
-        (
-            [(0, None, 0, 0), (1, None, SEG, 0)],
-            [(2, 0, 0, 0), (3, 0, 0, half), (2, 1, SEG, 0), (3, 1, SEG, half)],
+    y_b1, saved = ahead(1, 1, ((hop_b, None),), saved, SHORT)
+    other_y = one_way(saved["y_low"], 1, 0)
+    dx_b1, fed, made = back(1, 1, ((other_gy[1], None, 0, 0), (cotangent, 1, 0, width)), fed, made, SHORT, HALF)
+    rest = project_back(1, [active[1]], saved, fed, params, made, [dx_b1, back_a])
+    back_b = [one_way(dx_b1, 1, 0), one_way(rest, 1, 0)]
+    last[0] = [rest]
+    dx_a0, fed, made = back(0, 0, ((back_a, None, 0, 0),), fed, made, SHORT)
+
+    def gy_of(s, arrived):
+        count = len(arrived)
+        first = [(n, None, n * (SEG // count), 0) for n in range(count)]
+        second = [(count, None, 0, 0), (count + 1, s, 0, WIDTH // 2)]
+        return Either([*arrived, other_gy[s], cotangent], (first, second))
+
+    tall = FF // WIDTH
+    kinds = lambda: dict(
+        down=(
+            [[(saved["hidden"], 0)], gy_of(0, [back_a])],
+            [dict(left=0, right=1, loop="left", count=tall, out=0, at=(0, 0))],
+            [(FF, WIDTH)],
         ),
-    )
+        up=(
+            [[(saved["ffn_in"], 0)], [(fed["d_hidden"], 0)], [(saved["attended"], 0)], [(fed["low"], 0)]],
+            [
+                dict(left=0, right=1, loop="right", count=tall, out=0, at=(0, 0)),
+                dict(left=2, right=3, loop=None, count=1, out=1, at=(0, 0)),
+            ],
+            [(WIDTH, FF), (WIDTH, WIDTH)],
+        ),
+        proj=(
+            [
+                [(saved["normed"], 0), (normed_memory[0], 0)],
+                [(made["dkx"], 0), (made["dkm"], 0)],
+                [(made["dvx"], 0), (made["dvm"], 0)],
+                [(saved["normed"], 0)],
+                [(made["dq"], 0)],
+            ],
+            [
+                dict(left=0, right=1, loop=None, count=1, out=0, at=(0, WIDTH)),
+                dict(left=0, right=2, loop=None, count=1, out=0, at=(0, 2 * WIDTH)),
+                dict(left=3, right=4, loop=None, count=1, out=0, at=(0, 0)),
+            ],
+            [(WIDTH, 3 * WIDTH)],
+        ),
+    )
+
+    def early(tokens, *which):
+        groups, jobs, outs = [], [], []
+        for kind in which:
+            more, jobs_more, outs_more = kinds()[kind]
+            for job in jobs_more:
+                jobs.append(
+                    dict(
+                        job,
+                        left=job["left"] + len(groups),
+                        right=job["right"] + len(groups),
+                        out=job["out"] + len(outs),
+                    )
+                )
+            groups, outs = groups + more, outs + outs_more
+        return early_grads(at_section, groups, jobs, outs, tokens)
+
+    sizes = {kind: value[2] for kind, value in kinds().items()}
+    tokens = last[0]
+    base_down, up_first, out_first, proj_first = lax.cond(
+        is_first,
+        lambda: early(tokens, "down", "up", "proj"),
+        lambda: early(tokens, "down") + unset(sizes["up"] + sizes["proj"], tokens),
+    )
+    last[0] = [base_down]
+
+    def early_second(kind):
+        tokens = last[0]
+        made_late = lax.cond(is_first, lambda: unset(sizes[kind], tokens), lambda: early(tokens, kind))
+        last[0] = [made_late[0]]
+        return made_late
+
     moving, done = {}, {}
-    orders = {name: (0, *range(2, levels), 1) for name in ()}
+    orders = {name: (0, *range(2, levels), 1) for name in ("up0",)}
 
     def send_on(name, send, keep, step):
         order = orders.get(name, tuple(range(levels)))
@@ -1103,9 +1377,9 @@
             else:
                 send_on(name, *values, moving[name][2] + 1)
 
-    def grads(names, groups, tasks, chunks, **more):
+    def grads(names, groups, bases, tasks, chunks, **more):
         places = [places_of(orders.get(name, tuple(range(levels))), size) for name in names]
-        made = weight_grads(at_section, at_dp, size, groups, tasks, chunks, last[0], places, **more)
+        made = weight_grads(at_section, at_dp, size, groups, bases, tasks, chunks, last[0], places, **more)
         last[0] = [made[0][0]]
         for name, (send, keep) in zip(names, made):
             send_on(name, send, keep, 0)
@@ -1113,11 +1387,13 @@
     eighth = WIDTH // 8
     grads(
         ("down0", "down1", "down2"),
-        [[rows_of(saved["hidden"])], gy_all],
+        [[(saved["hidden"], 1)], gy_of(1, back_b)],
+        [(base_down, base_down)],
         [
             dict(
                 left=(0, t),
                 right=(1, 0),
+                base=(0, t * WIDTH, 0),
                 block=t,
                 blocks=FF // WIDTH,
                 outs=[(0, 0, 3 * eighth, 0), (1, 3 * eighth, 2 * eighth, 0), (2, 5 * eighth, 3 * eighth, 0)],
@@ -1128,61 +1404,72 @@
     )
     halved("down0")
     halved("down1", "down2")
-    fed = feed_back(1, [active[0]], ((back_b, None),), saved, params, fed, last[0])
+    fed = feed_back(1, [active[0]], [(part, None, n * HALF, 0) for n, part in enumerate(back_b)], saved, params, fed, last[0])
     last[0] = [fed["d_down"]]
+    up_second, out_second = early_second("up")
     halved("down0")
 
     up = jnp.sum(fed["d_up"], axis=(0, 1)).reshape(size, FF // size)
     down = jnp.sum(fed["d_down"], axis=(0, 1)).reshape(size, WIDTH // size)
     row = jnp.concatenate([up, down], axis=1).astype(BF)
     small = jnp.pad(row[:, None, :], ((0, 0), (0, 15), (0, WIDTH - row.shape[1])))
-    ffn_in, d_hidden = [rows_of(saved["ffn_in"])], [rows_of(fed["d_hidden"])]
     grads(
-        ("up0",),
-        [ffn_in, d_hidden],
-        [dict(left=(0, 0), right=(1, t), block=0, blocks=1, outs=[(0, 0, WIDTH, t * WIDTH)]) for t in range(2)],
-        [(1, 2 * WIDTH)],
-    )
-    halved("down1", "down0")
-    grads(
-        ("up1", "out"),
-        [ffn_in, d_hidden, [rows_of(saved["attended"])], [rows_of(fed["low"])]],
-        [dict(left=(0, 0), right=(1, 2 + t), block=0, blocks=1, outs=[(0, 0, WIDTH, t * WIDTH)]) for t in range(2)]
-        + [dict(left=(2, 0), right=(3, 0), block=0, blocks=1, outs=[(1, 0, WIDTH, 0)])],
-        [(1, 2 * WIDTH), (1, WIDTH)],
+        ("up0", "up1", "out"),
+        [[(saved["ffn_in"], 1)], [(fed["d_hidden"], 1)], [(saved["attended"], 1)], [(fed["low"], 1)]],
+        [(up_first, up_second), (out_first, out_second)],
+        [
+            dict(
+                left=(0, 0),
+                right=(1, t),
+                base=(0, 0, t * WIDTH),
+                block=0,
+                blocks=1,
+                outs=[(t // 2, 0, WIDTH, (t % 2) * WIDTH)],
+            )
+            for t in range(tall)
+        ]
+        + [dict(left=(2, 0), right=(3, 0), base=(1, 0, 0), block=0, blocks=1, outs=[(2, 0, WIDTH, 0)])],
+        [(1, 2 * WIDTH), (1, 2 * WIDTH), (1, WIDTH)],
         small=small,
-        small_chunk=0,
-    )
-    halved("down2", "down1", "up0")
+        small_chunk=1,
+        estimate=SHORT,
+    )
+    halved("down1", "down2", "down0", estimate=LONG)
+    halved("up1")
+    halved("up0", "out")
     dx_b0, made = attend_back(
-        1, [active[0], reset_flags, boundary], saved, fed, kv_memory, params, made, last[0]
+        1, [active[0], reset_flags, boundary], saved, fed, kv_memory[1], params, made, last[0]
     )
     last[0] = [dx_b0]
+    (proj_second,) = early_second("proj")
+    squeezed_second = squeeze(1)
     outputs = pick(at_section, other_y, saved["y_high"], last[0])
     last[0] = [outputs]
-    halved("up0", "up1", "out", "down2", "down1", "down0")
+    halved("up1", "up0", "down1", "down2", "down0")
     grads(
         ("key", "value", "query"),
         [
-            [rows_of(saved["normed"]), rows_of(normed_memory)],
-            [rows_of(made["dkx"]), rows_of(made["dkm"])],
-            [rows_of(made["dvx"]), rows_of(made["dvm"])],
-            [rows_of(saved["normed"])],
-            [rows_of(made["dq"])],
+            [(saved["normed"], 1), (normed_memory[1], 0)],
+            [(made["dkx"], 1), (made["dkm"], 1)],
+            [(made["dvx"], 1), (made["dvm"], 1)],
+            [(saved["normed"], 1)],
+            [(made["dq"], 1)],
         ],
+        [(proj_first, proj_second)],
         [
-            dict(left=(0, 0), right=(1, 0), block=0, blocks=1, outs=[(0, 0, WIDTH, 0)]),
-            dict(left=(0, 0), right=(2, 0), block=0, blocks=1, outs=[(1, 0, WIDTH, 0)]),
-            dict(left=(3, 0), right=(4, 0), block=0, blocks=1, outs=[(2, 0, WIDTH, 0)]),
+            dict(left=(0, 0), right=(1, 0), base=(0, 0, WIDTH), block=0, blocks=1, outs=[(0, 0, WIDTH, 0)]),
+            dict(left=(0, 0), right=(2, 0), base=(0, 0, 2 * WIDTH), block=0, blocks=1, outs=[(1, 0, WIDTH, 0)]),
+            dict(left=(3, 0), right=(4, 0), base=(0, 0, 0), block=0, blocks=1, outs=[(2, 0, WIDTH, 0)]),
         ],
         [(1, WIDTH)] * 3,
-    )
-    halved("up1", estimate=LONG)
+        estimate=SHORT,
+    )
+    halved("out", "up1", "up0", "down1", "down2", estimate=LONG)
     halved("key", "value", "query")
-    halved("out", "up0", "down2")
     grad_inputs = pick(at_section, made["dx_low"], one_way(made["dx_high"], 0, 1), last[0])
     last[0] = [grad_inputs]
-    for names in (("key", "up1"), ("value", "key", "out", "up0"), ("query", "value", "up1", "out"), ("query", "key")):
+    halved("up0", estimate=LONG)
+    for names in (("key", "up1", "out"), ("value", "key"), ("query", "value", "out"), ("query", "key")):
         halved(*names)
     while any(step + 1 < levels for _, _, step in moving.values()):
         halved(*[name for name, (_, _, step) in moving.items() if step + 1 < levels])
@@ -1210,6 +1497,7 @@
         last[0],
     )
     keep_all = (1 - reset_flags).astype(BF)[:, None, None]
+    squeezed = jnp.where(is_first, squeezed_first, squeezed_second)
     new_compressed = jnp.concatenate([compressed[:, COMP:] * keep_all, squeezed], axis=1)
     return (
         outputs,

time: 538 us -> 510 us (0.948)
  the two profiles are of different devices: /device:TPU:0 before, /device:TPU:26 now
where the time goes in v3:
time: 510 us; the launch traced here: 502 us
  Pallas kernels  329 us (65%)
  waiting for transfers between devices  86.3 us (17%)
  starting transfers between devices  50.7 us (10%)
  local copies, waits for them, and re-layouts  23.9 us (5%)
  other arithmetic  5.2 us (1%)
    pallas_call x41, Pallas kernels, call(): pl.pallas_call(run, name=name, grid_spec=pltpu.PrefetchScalarGridSpec(num...  329 us
    ppermute x36, waiting for transfers between devices, swap_bit(): return lax.ppermute(value, 'dp', [(i, i ^ 1 << bit) for i in range(size)])  57.4 us
    ppermute x36, starting transfers between devices, swap_bit(): return lax.ppermute(value, 'dp', [(i, i ^ 1 << bit) for i in range(size)])  30.6 us
    ppermute x11, waiting for transfers between devices, one_way(): return lax.ppermute(value, 'section', [(first, second)])  28.9 us
    ppermute x11, starting transfers between devices, one_way(): return lax.ppermute(value, 'section', [(first, second)])  20.1 us
    unnamed x124, local copies, waits for them, and re-layouts  16.8 us
  transfers between devices with their start and end apart: 47, of which 12 were waited for; matrix products, arithmetic and copies ran while one was open for 2% of the time, Pallas kernels for 61%

profile of v3, /device:TPU:26, one launch (start us, length us, event | category | flops | bytes accessed | tf_op | source)
XLA Modules:
  0.0 501.7 jit_solution(3825176934394228930)
XLA Ops:
  4.2 10.2 %memory_keyvals.2 = (bf16[1,1024,1024]{2,1,0:T(8,128)(2,1)}, bf16[1,1024,2048]{2,1,0:T(8,128)(2,1)}) custom-call(s32[2]{0:T(128)} %refs_1_.15, bf16[2,512,1024]{2,1,0:T(8,128)(2,1)} %bitcast.71, bf16[2,512,1024]{2,1,0:T(8,128)(2,1)} %bitcast.69, bf16[1,1024]{1,0:T(2,128)(2,1)} %refs_10_.11, bf16[1024,3072]{1,0:T(8,128)(2,1)} %bitcast.38), custom_call_target="tpu_custom_call" | custom-call | flops 99999997952 | bytes 1 | tf_op jit(solution)/shard_map/memory_keyvals/pallas_call | solution.py:83
  18.1 7.8 %forward.4 = (bf16[512,1024]{1,0:T(8,128)(2,1)}, bf16[2,512,1024]{2,1,0:T(8,128)(2,1)}, bf16[2,512,1024]{2,1,0:T(8,128)(2,1)S(1)}, bf16[2,512,3072]{2,1,0:T(8,12...) custom-call(s32[1]{0:T(128)S(6)} %sub.6.refs_0_, ...), custom_call_target="tpu_custom_call" | custom-call | flops 99999997952 | bytes 1 | tf_op jit(solution)/shard_map/forward/pallas_call | solution.py:83
  27.3 9.9 %memory_keyvals.3 = (bf16[1,1024,1024]{2,1,0:T(8,128)(2,1)}, bf16[1,1024,2048]{2,1,0:T(8,128)(2,1)}) custom-call(s32[2]{0:T(128)S(1)} %copy-done.50, bf16[2,512,1024]{2,1,0:T(8,128)(2,1)} %bitcast.72, bf16[2,512,1024]{2,1,0:T(8,128)(2,1)} %bitcast.70, bf16[1,1024]{1,0:T(2,128)(2,1)} %refs_10_.11, bf16[1024,3072]{1,0:T(8,128)(2,1)} %bitcast.40, ...), custom_call_target="tpu_custom_call" | custom-call | flops 99999997952 | bytes 1 | tf_op jit(solution)/shard_map/memory_keyvals/pallas_call | solution.py:83
  37.3 6.9 %forward.5 = (bf16[512,1024]{1,0:T(8,128)(2,1)}, bf16[2,512,1024]{2,1,0:T(8,128)(2,1)}, bf16[2,512,1024]{2,1,0:T(8,128)(2,1)S(1)}, bf16[2,512,3072]{2,1,0:T(8,12...) custom-call(s32[1]{0:T(128)S(6)} %sub.6.refs_0_, ...), custom_call_target="tpu_custom_call", output_to_operand_aliasing={{1}: (14, {}), {2}: (15, {}), {3}: (16, {}), {4}: (17, {}),... | custom-call | flops 1 | bytes 1 | tf_op jit(solution)/shard_map/forward/pallas_call | solution.py:83
  50.5 21.9 %collective-permute-done.3.refs_3_ = bf16[512,1024]{1,0:T(8,128)(2,1)} collective-permute-done((bf16[512,1024]{1,0:T(8,128)(2,1)}, bf16[512,1024]{1,0:T(8,128)(2,1)}, u32[]{:S(2)}, u32[]{:S(2)}) %collective-permute-start.3) | collective-permute-done | bytes 1048608 | tf_op jit(solution)/shard_map/ppermute | solution.py:1193
  72.4 29.9 %forward.6 = (bf16[512,1024]{1,0:T(8,128)(2,1)}, bf16[2,512,1024]{2,1,0:T(8,128)(2,1)}, bf16[2,512,1024]{2,1,0:T(8,128)(2,1)S(1)}, bf16[2,512,3072]{2,1,0:T(8,12...) custom-call(s32[1]{0:T(128)} %bitcast.2.refs_0_, ...), custom_call_target="tpu_custom_call", output_to_operand_aliasing={{1}: (13, {}), {2}: (14, {}), {3}: (15, {}), {4}: (16, {}),... | custom-call | flops 1 | bytes 1 | tf_op jit(solution)/shard_map/forward/pallas_call | solution.py:83
  102.3 6.9 %collective-permute-done.4.refs_1_ = bf16[512,512]{1,0:T(8,128)(2,1)} collective-permute-done((bf16[512,512]{1,0:T(8,128)(2,1)}, bf16[512,512]{1,0:T(8,128)(2,1)}, u32[]{:S(2)}, u32[]{:S(2)}) %collective-permute-start.4) | collective-permute-done | bytes 524320 | tf_op jit(solution)/shard_map/ppermute | solution.py:1193
  109.2 16.8 %feed_back.4 = (bf16[2,512,4096]{2,1,0:T(8,128)(2,1)}, f32[2,512,1024]{2,1,0:T(8,128)}, bf16[2,512,1024]{2,1,0:T(8,128)(2,1)}, bf16[2,512,1024]{2,1,0:T(8,128)(2...) custom-call(s32[1]{0:T(128)} %bitcast.2.refs_0_, bf16[512,512]{1,0:T(8,128)(2,1)} %collective-permute-done.4.refs_1_, ...), custom_call_target="tpu_custom_call" | custom-call | flops 1 | bytes 1 | tf_op jit(solution)/shard_map/feed_back/pallas_call | solution.py:83
  126.0 24.0 %attend_back.4 = (bf16[512,1024]{1,0:T(8,128)(2,1)}, bf16[2,512,1024]{2,1,0:T(8,128)(2,1)}, bf16[2,512,1024]{2,1,0:T(8,128)(2,1)}, bf16[2,512,1024]{2,1,0:T(8,12...) custom-call(s32[1]{0:T(128)} %bitcast.2.refs_0_, ...), custom_call_target="tpu_custom_call" | custom-call | flops 1 | bytes 1 | tf_op jit(solution)/shard_map/attend_back/pallas_call | solution.py:83
  153.6 30.1 %forward.7 = (bf16[512,1024]{1,0:T(8,128)(2,1)}, bf16[2,512,1024]{2,1,0:T(8,128)(2,1)}, bf16[2,512,1024]{2,1,0:T(8,128)(2,1)S(1)}, bf16[2,512,3072]{2,1,0:T(8,12...) custom-call(s32[1]{0:T(128)} %bitcast.2.refs_0_, ...), custom_call_target="tpu_custom_call", output_to_operand_aliasing={{1}: (13, {}), {2}: (14, {}), {3}: (15, {}), {4}: (16, {}),... | custom-call | flops 1 | bytes 1 | tf_op jit(solution)/shard_map/forward/pallas_call | solution.py:83
  183.7 18.1 %feed_back.5 = (bf16[2,512,4096]{2,1,0:T(8,128)(2,1)}, f32[2,512,1024]{2,1,0:T(8,128)}, bf16[2,512,1024]{2,1,0:T(8,128)(2,1)}, bf16[2,512,1024]{2,1,0:T(8,128)(2...) custom-call(s32[1]{0:T(128)} %bitcast.2.refs_0_, ...), custom_call_target="tpu_custom_call", output_to_operand_aliasing={{0}: (9, {}), {1}: (10, {}), {2}: (11, {}), {3}: (12, {}), ... | custom-call | flops 1 | bytes 1 | tf_op jit(solution)/shard_map/feed_back/pallas_call | solution.py:83
  201.8 21.6 %attend_back.5 = (bf16[256,1024]{1,0:T(8,128)(2,1)}, bf16[2,512,1024]{2,1,0:T(8,128)(2,1)}, bf16[2,512,1024]{2,1,0:T(8,128)(2,1)}, bf16[2,512,1024]{2,1,0:T(8,12...) custom-call(s32[1]{0:T(128)} %bitcast.2.refs_0_, ...), custom_call_target="tpu_custom_call", output_to_operand_aliasing={{1}: (12, {}), {2}: (13, {}), {3}: (14, {}), {4}: (15, {}),... | custom-call | flops 1 | bytes 1 | tf_op jit(solution)/shard_map/attend_back/pallas_call | solution.py:83
  225.5 6.8 %project_back.1.refs_14_ = bf16[256,1024]{1,0:T(8,128)(2,1)} custom-call(s32[1]{0:T(128)} %bitcast.2.refs_0_, bf16[2,512,1024]{2,1,0:T(8,128)(2,1)} %get-tuple-element.446.refs_1_.refs_12_, bf16[2,512,1024]{2,1,0:T(8,128)(2,1)} %get-tuple-element.447.refs_2_.refs_13_, bf16[2,512,1024]{2,1,0:T(8,128)(2,1)} %get-tuple-element.448.refs_3_.refs_14_, ...), custom_call_target="tpu_custom_call" | custom-call | flops 99999997952 | bytes 1 | tf_op jit(solution)/shard_map/project_back/pallas_call | solution.py:83
  236.1 11.6 %attend_back.6 = (bf16[512,1024]{1,0:T(8,128)(2,1)}, bf16[2,512,1024]{2,1,0:T(8,128)(2,1)}, bf16[2,512,1024]{2,1,0:T(8,128)(2,1)}, bf16[2,512,1024]{2,1,0:T(8,12...) custom-call(s32[1]{0:T(128)S(6)} %sub.6.refs_0_, ...), custom_call_target="tpu_custom_call", output_to_operand_aliasing={{1}: (12, {}), {2}: (13, {}), {3}: (14, {}), {4}: (15, {}),... | custom-call | flops 1 | bytes 1 | tf_op jit(solution)/shard_map/attend_back/pallas_call | solution.py:83
  247.7 9.2 %conditional.6 = ((bf16[4096,1024]{1,0:T(8,128)(2,1)}, bf16[1024,4096]{1,0:T(8,128)(2,1)}, bf16[1024,1024]{1,0:T(8,128)(2,1)}, bf16[1024,3072]{1,0:T(8,128)(2,1)})) conditional(s32[]{:T(128)} %convert_element_type.28, (s32[1]{0:T(128)}, bf16[2,512,4096]{2,1,0:T(8,128)(2,1)}, bf16[512,1024]{1,0:T(8,128)(2,1)}, bf16[512,512]{1,0:T(8,128)(2,1)}, ...), branch_computations={%region_2.0_spmd, %region_3.0_spmd} | conditional | flops 2 | bytes 42 | solution.py:1342
  247.8 8.9 %early_grads.4 = bf16[4096,1024]{1,0:T(8,128)(2,1)} custom-call(s32[1]{0:T(128)} %get-tuple-element.114.refs_0_, bf16[2,512,4096]{2,1,0:T(8,128)(2,1)} %get-tuple-element.115.refs_1_, bf16[512,1024]{1,0:T(8,128)(2,1)} %get-tuple-element.116.refs_2_, bf16[512,512]{1,0:T(8,128)(2,1)} %get-tuple-element.117.refs_3_, ...), custom_call_target="tpu_custom_call" | custom-call | flops 1 | bytes 1 | tf_op jit(solution)/shard_map/cond/branch_0_fun/early_grads/pallas_call | solution.py:83
  256.9 11.5 %weight_grads.3 = (bf16[8,256,384]{2,1,0:T(8,128)(2,1)}, bf16[8,256,256]{2,1,0:T(8,128)(2,1)}, bf16[8,256,384]{2,1,0:T(8,128)(2,1)}, bf16[8,256,384]{2,1,0:T(8,1...) custom-call(s32[1]{0:T(128)} %bitcast.2.refs_0_, s32[1]{0:T(128)} %bitcast.13.refs_1_.refs_0_, ...), custom_call_target="tpu_custom_call" | custom-call | flops 99999997952 | bytes 1 | tf_op jit(solution)/shard_map/weight_grads/pallas_call | solution.py:83
  287.5 9.6 %conditional.7 = ((bf16[1024,4096]{1,0:T(8,128)(2,1)}, bf16[1024,1024]{1,0:T(8,128)(2,1)})) conditional(s32[]{:T(128)} %convert_element_type.28, (s32[1]{0:T(128)}, bf16[2,512,1024]{2,1,0:T(8,128)(2,1)S(1)}, bf16[2,512,4096]{2,1,0:T(8,128)(2,1)}, bf16[2,512,1024]{2,1,0:T(8,128)(2,1)S(1)}, bf16[2,512,1024]{2,1,0:T(8,128)(2,1)}, ...), branch_computations={%region_4.0_spmd, %region_5.0_spmd} | conditional | flops 1 | bytes 9 | solution.py:1351
  287.5 9.4 %early_grads.6 = (bf16[1024,4096]{1,0:T(8,128)(2,1)}, bf16[1024,1024]{1,0:T(8,128)(2,1)}) custom-call(s32[1]{0:T(128)} %get-tuple-element.140.refs_0_, bf16[2,512,1024]{2,1,0:T(8,128)(2,1)S(1)} %get-tuple-element.141.refs_1_, bf16[2,512,4096]{2,1,0:T(8,128)(2,1)} %get-tuple-element.142.refs_2_, bf16[2,512,1024]{2,1,0:T(8,128)(2,1)S(1)} %get-tuple-element.143.refs_3_, ...), custom_call_target="tpu_custom_call" | custom-call | flops 1 | bytes 1 | tf_op jit(solution)/shard_map/cond/branch_0_fun/early_grads/pallas_call | solution.py:83
  304.2 15.5 %weight_grads.4 = (bf16[8,64,2048]{2,1,0:T(8,128)(2,1)}, bf16[8,80,2048]{2,1,0:T(8,128)(2,1)}, bf16[8,64,1024]{2,1,0:T(8,128)(2,1)}, bf16[8,64,2048]{2,1,0:T(8,1...) custom-call(s32[1]{0:T(128)} %bitcast.2.refs_0_, s32[1]{0:T(128)} %bitcast.13.refs_1_.refs_0_, ...), custom_call_target="tpu_custom_call" | custom-call | flops 1 | bytes 1 | tf_op jit(solution)/shard_map/weight_grads/pallas_call | solution.py:83
  344.7 16.3 %conditional.8 = (bf16[1024,3072]{1,0:T(8,128)(2,1)}) conditional(s32[]{:T(128)} %convert_element_type.28, (s32[1]{0:T(128)}, bf16[2,512,1024]{2,1,0:T(8,128)(2,1)S(1)}, bf16[1,1024,1024]{2,1,0:T(8,128)(2,1)}, bf16[2,512,1024]{2,1,0:T(8,128)(2,1)}, bf16[2,1024,1024]{2,1,0:T(8,128)(2,1)}, /*index=5*/bf16[2,512,1024]{2,1,0:T(8,128)(2,1)}, ...), branch_computations={%region_8.9_spmd, %region_9.10_spmd} | conditional | flops 1 | bytes 9 | solution.py:1351
  348.7 12.3 %early_grads.7 = bf16[1024,3072]{1,0:T(8,128)(2,1)} custom-call(s32[1]{0:T(128)} %get-tuple-element.146.refs_0_, bf16[2,512,1024]{2,1,0:T(8,128)(2,1)S(1)} %get-tuple-element.147.refs_1_.refs_7_, bf16[1,1024,1024]{2,1,0:T(8,128)(2,1)} %get-tuple-element.148.refs_2_, bf16[2,512,1024]{2,1,0:T(8,128)(2,1)} %get-tuple-element.149.refs_3_, ...), custom_call_target="tpu_custom_call" | custom-call | flops 1 | bytes 1 | tf_op jit(solution)/shard_map/cond/branch_0_fun/early_grads/pallas_call | solution.py:83
  361.0 10.3 %conditional.9 = (bf16[2,256,1024]{2,1,0:T(8,128)(2,1)S(1)}) conditional(s32[]{:T(128)} %convert_element_type.29, bf16[1024,3072]{1,0:T(8,128)(2,1)} %get-tuple-element.597.refs_11_, (bf16[1,2,512,1024]{3,2,1,0:T(8,128)(2,1)}, bf16[1,2,1024,1024]{3,2,1,0:T(8,128)(2,1)}, s32[2]{0:T(128)S(1)}, bf16[1,1024]{1,0:T(2,128)(2,1)S(1)}, ...), branch_computations={%region_10.11_spmd, %region_11.12_spmd} | conditional | flops 1 | bytes 4194313 | solution.py:1262
  365.0 6.0 %compress.3 = bf16[2,256,1024]{2,1,0:T(8,128)(2,1)S(1)} custom-call(s32[2]{0:T(128)S(1)} %get-tuple-element.155.refs_0_, bf16[2,256,2048]{2,1,0:T(8,128)(2,1)} %reshape_squeeze.5.refs_1_, bf16[2048,1024]{1,0:T(8,128)(2,1)} %bitcast.68, bf16[1,1024]{1,0:T(2,128)(2,1)S(1)} %get-tuple-element.158.refs_3_, bf16[1024,3072]{1,0:T(8,128)(2,1)} %get-tuple-element.159.refs_4_), custom_call_target="tpu_custom_call" | custom-call | flops 1 | bytes 1 | tf_op jit(solution)/shard_map/cond/branch_1_fun/compress/pallas_call | solution.py:83
  374.6 4.9 halve.20
  387.2 14.1 %weight_grads.5 = (bf16[8,64,1024]{2,1,0:T(8,128)(2,1)}, bf16[8,64,1024]{2,1,0:T(8,128)(2,1)}, bf16[8,64,1024]{2,1,0:T(8,128)(2,1)}, bf16[8,64,1024]{2,1,0:T(8,1...) custom-call(s32[1]{0:T(128)} %bitcast.2.refs_0_, s32[1]{0:T(128)} %bitcast.13.refs_1_.refs_0_, ...), custom_call_target="tpu_custom_call" | custom-call | flops 1 | bytes 1 | tf_op jit(solution)/shard_map/weight_grads/pallas_call | solution.py:83
  403.0 18.1 %collective-permute-done.32.refs_9_ = bf16[1,256,256]{2,1,0:T(8,128)(2,1)S(1)} collective-permute-done((bf16[1,256,256]{2,1,0:T(8,128)(2,1)}, bf16[1,256,256]{2,1,0:T(8,128)(2,1)S(1)}, u32[]{:S(2)}, u32[]{:S(2)}) %collective-permute-start.32) | collective-permute-done | bytes 131104 | tf_op jit(solution)/shard_map/ppermute | solution.py:1189
  443.6 6.0 %collective-permute-done.35.refs_4_ = bf16[4,64,1024]{2,1,0:T(8,128)(2,1)S(1)} collective-permute-done((bf16[4,64,1024]{2,1,0:T(8,128)(2,1)}, bf16[4,64,1024]{2,1,0:T(8,128)(2,1)S(1)}, u32[]{:S(2)}, u32[]{:S(2)}) %collective-permute-start.35) | collective-permute-done | bytes 524320 | tf_op jit(solution)/shard_map/ppermute | solution.py:1189
  455.0 5.9 %collective-permute-done.38.refs_3_ = bf16[4,64,1024]{2,1,0:T(8,128)(2,1)S(1)} collective-permute-done((bf16[4,64,1024]{2,1,0:T(8,128)(2,1)}, bf16[4,64,1024]{2,1,0:T(8,128)(2,1)S(1)}, u32[]{:S(2)}, u32[]{:S(2)}) %collective-permute-start.38) | collective-permute-done | bytes 524320 | tf_op jit(solution)/shard_map/ppermute | solution.py:1189
  470.8 5.4 %collective-permute-done.42.refs_6_ = bf16[1,64,1024]{2,1,0:T(8,128)(2,1)S(1)} collective-permute-done((bf16[1,64,1024]{2,1,0:T(8,128)(2,1)}, bf16[1,64,1024]{2,1,0:T(8,128)(2,1)S(1)}, u32[]{:S(2)}, u32[]{:S(2)}) %collective-permute-start.42) | collective-permute-done | bytes 131104 | tf_op jit(solution)/shard_map/ppermute | solution.py:1189
  480.1 6.7 %collective-permute-done.43.refs_3_ = bf16[2,64,1024]{2,1,0:T(8,128)(2,1)S(1)} collective-permute-done((bf16[2,64,1024]{2,1,0:T(8,128)(2,1)}, bf16[2,64,1024]{2,1,0:T(8,128)(2,1)S(1)}, u32[]{:S(2)}, u32[]{:S(2)}) %collective-permute-start.43) | collective-permute-done | bytes 262176 | tf_op jit(solution)/shard_map/ppermute | solution.py:1189
  491.1 5.1 %collective-permute-done.45.refs_10_ = bf16[1,64,1024]{2,1,0:T(8,128)(2,1)S(1)} collective-permute-done((bf16[1,64,1024]{2,1,0:T(8,128)(2,1)}, bf16[1,64,1024]{2,1,0:T(8,128)(2,1)S(1)}, u32[]{:S(2)}, u32[]{:S(2)}) %collective-permute-start.45) | collective-permute-done | bytes 131104 | tf_op jit(solution)/shard_map/ppermute | solution.py:1189
  (247 shorter events, 142.8 us)
Async XLA Ops:
  1.7 15.6 %collective-permute-start.1 = (bf16[512,512]{1,0:T(8,128)(2,1)S(1)}, bf16[512,512]{1,0:T(8,128)(2,1)S(1)}, u32[]{:S(2)}, u32[]{:S(2)}) collective-permute-start(bf16[512,512]{1,0:T(8,128)(2,1)S(1)} %slice_bitcast_fusion.2), channel_id=1, source_target_pairs={{1,0},{3,2},{5,4},{7,6},{9,8},{11,10},{13,12},{15,14},{17,16},{19,... | collective-permute-start | bytes 1572872 | tf_op jit(solution)/shard_map/ppermute | solution.py:1193
  15.3 22.0 %collective-permute-start = (bf16[512,512]{1,0:T(8,128)(2,1)}, bf16[512,512]{1,0:T(8,128)(2,1)}, u32[]{:S(2)}, u32[]{:S(2)}) collective-permute-start(bf16[512,512]{1,0:T(8,128)(2,1)} %slice_bitcast_fusion.3), channel_id=1, source_target_pairs={{1,0},{3,2},{5,4},{7,6},{9,8},{11,10},{13,12},{15,14},{17,16},{19,... | collective-permute-start | bytes 1572872 | tf_op jit(solution)/shard_map/ppermute | solution.py:1193
  26.0 46.4 %collective-permute-start.3 = (bf16[512,1024]{1,0:T(8,128)(2,1)}, bf16[512,1024]{1,0:T(8,128)(2,1)}, u32[]{:S(2)}, u32[]{:S(2)}) collective-permute-start(bf16[512,1024]{1,0:T(8,128)(2,1)} %get-tuple-element.379.refs_5_), channel_id=1, source_target_pairs={{0,1},{2,3},{4,5},{6,7},{8,9},{10,11},{12,13},{14,15},{16,17},{18,... | collective-permute-start | bytes 3145736 | tf_op jit(solution)/shard_map/ppermute | solution.py:1193
  47.8 61.4 %collective-permute-start.4 = (bf16[512,512]{1,0:T(8,128)(2,1)}, bf16[512,512]{1,0:T(8,128)(2,1)}, u32[]{:S(2)}, u32[]{:S(2)}) collective-permute-start(bf16[512,512]{1,0:T(8,128)(2,1)} %get-tuple-element.581), channel_id=1, source_target_pairs={{0,1},{2,3},{4,5},{6,7},{8,9},{10,11},{12,13},{14,15},{16,17},{18,... | collective-permute-start | bytes 1572872 | tf_op jit(solution)/shard_map/ppermute | solution.py:1193
  49.1 104.4 %collective-permute-start.2 = (bf16[512,1024]{1,0:T(8,128)(2,1)}, bf16[512,1024]{1,0:T(8,128)(2,1)}, u32[]{:S(2)}, u32[]{:S(2)}) collective-permute-start(bf16[512,1024]{1,0:T(8,128)(2,1)} %get-tuple-element.393), channel_id=1, source_target_pairs={{0,1},{2,3},{4,5},{6,7},{8,9},{10,11},{12,13},{14,15},{16,17},{18,... | collective-permute-start | bytes 3145736 | tf_op jit(solution)/shard_map/ppermute | solution.py:1193
  150.0 75.5 %collective-permute-start.8 = (bf16[512,1024]{1,0:T(8,128)(2,1)}, bf16[512,1024]{1,0:T(8,128)(2,1)}, u32[]{:S(2)}, u32[]{:S(2)}) collective-permute-start(bf16[512,1024]{1,0:T(8,128)(2,1)} %get-tuple-element.420.refs_24_), channel_id=1, source_target_pairs={{1,0},{3,2},{5,4},{7,6},{9,8},{11,10},{13,12},{15,14},{17,16},{19,... | collective-permute-start | bytes 3145736 | tf_op jit(solution)/shard_map/ppermute | solution.py:1193
  152.3 31.4 %collective-permute-start.6 = (bf16[512,512]{1,0:T(8,128)(2,1)S(1)}, bf16[512,512]{1,0:T(8,128)(2,1)}, u32[]{:S(2)}, u32[]{:S(2)}) collective-permute-start(bf16[512,512]{1,0:T(8,128)(2,1)S(1)} %copy-done.36), channel_id=1, source_target_pairs={{0,1},{2,3},{4,5},{6,7},{8,9},{10,11},{12,13},{14,15},{16,17},{18,... | collective-permute-start | bytes 1572872 | tf_op jit(solution)/shard_map/ppermute | solution.py:1193
  223.4 33.5 %collective-permute-start.7 = (bf16[256,1024]{1,0:T(8,128)(2,1)}, bf16[256,1024]{1,0:T(8,128)(2,1)}, u32[]{:S(2)}, u32[]{:S(2)}) collective-permute-start(bf16[256,1024]{1,0:T(8,128)(2,1)} %get-tuple-element.445.refs_8_), channel_id=1, source_target_pairs={{1,0},{3,2},{5,4},{7,6},{9,8},{11,10},{13,12},{15,14},{17,16},{19,... | collective-permute-start | bytes 1572872 | tf_op jit(solution)/shard_map/ppermute | solution.py:1193
  232.4 24.5 %collective-permute-start.9 = (bf16[256,1024]{1,0:T(8,128)(2,1)}, bf16[256,1024]{1,0:T(8,128)(2,1)}, u32[]{:S(2)}, u32[]{:S(2)}) collective-permute-start(bf16[256,1024]{1,0:T(8,128)(2,1)} %project_back.1.refs_14_), channel_id=1, source_target_pairs={{1,0},{3,2},{5,4},{7,6},{9,8},{11,10},{13,12},{15,14},{17,16},{19,... | collective-permute-start | bytes 1572872 | tf_op jit(solution)/shard_map/ppermute | solution.py:1193
  276.1 21.0 %collective-permute-start.13 = (bf16[4,256,384]{2,1,0:T(8,128)(2,1)}, bf16[4,256,384]{2,1,0:T(8,128)(2,1)S(1)}, u32[]{:S(2)}, u32[]{:S(2)}) collective-permute-start(bf16[4,256,384]{2,1,0:T(8,128)(2,1)} %get-tuple-element.478.refs_5_), channel_id=1, source_target_pairs={{0,4},{2,6},{4,0},{6,2},{8,12},{10,14},{12,8},{14,10},{16,20},{18,... | collective-permute-start | bytes 2359304 | tf_op jit(solution)/shard_map/ppermute | solution.py:1189
  283.2 41.0 %collective-permute-start.18 = (bf16[4,256,384]{2,1,0:T(8,128)(2,1)}, bf16[4,256,384]{2,1,0:T(8,128)(2,1)}, u32[]{:S(2)}, u32[]{:S(2)}) collective-permute-start(bf16[4,256,384]{2,1,0:T(8,128)(2,1)} %get-tuple-element.503), channel_id=1, source_target_pairs={{0,4},{2,6},{4,0},{6,2},{8,12},{10,14},{12,8},{14,10},{16,20},{18,... | collective-permute-start | bytes 2359304 | tf_op jit(solution)/shard_map/ppermute | solution.py:1189
  283.8 40.4 %collective-permute-start.17 = (bf16[4,256,256]{2,1,0:T(8,128)(2,1)}, bf16[4,256,256]{2,1,0:T(8,128)(2,1)}, u32[]{:S(2)}, u32[]{:S(2)}) collective-permute-start(bf16[4,256,256]{2,1,0:T(8,128)(2,1)} %get-tuple-element.479.refs_15_), channel_id=1, source_target_pairs={{0,4},{2,6},{4,0},{6,2},{8,12},{10,14},{12,8},{14,10},{16,20},{18,... | collective-permute-start | bytes 1572872 | tf_op jit(solution)/shard_map/ppermute | solution.py:1189
  300.3 24.4 %collective-permute-start.19 = (bf16[2,256,384]{2,1,0:T(8,128)(2,1)}, bf16[2,256,384]{2,1,0:T(8,128)(2,1)}, u32[]{:S(2)}, u32[]{:S(2)}) collective-permute-start(bf16[2,256,384]{2,1,0:T(8,128)(2,1)} %get-tuple-element.493.refs_11_), channel_id=1, source_target_pairs={{0,8},{2,10},{4,12},{6,14},{8,0},{10,2},{12,4},{14,6},{16,24},{18,... | collective-permute-start | bytes 1179656 | tf_op jit(solution)/shard_map/ppermute | solution.py:1189
  300.8 38.8 %collective-permute-start.5 = (bf16[2,512,512]{2,1,0:T(8,128)(2,1)S(1)}, bf16[2,512,512]{2,1,0:T(8,128)(2,1)}, u32[]{:S(2)}, u32[]{:S(2)}) collective-permute-start(bf16[2,512,512]{2,1,0:T(8,128)(2,1)S(1)} %copy-done.18), channel_id=1, source_target_pairs={{1,0},{3,2},{5,4},{7,6},{9,8},{11,10},{13,12},{15,14},{17,16},{19,... | collective-permute-start | bytes 3145736 | tf_op jit(solution)/shard_map/ppermute | solution.py:1193
  327.5 46.3 %collective-permute-start.24 = (bf16[2,256,384]{2,1,0:T(8,128)(2,1)}, bf16[2,256,384]{2,1,0:T(8,128)(2,1)S(1)}, u32[]{:S(2)}, u32[]{:S(2)}) collective-permute-start(bf16[2,256,384]{2,1,0:T(8,128)(2,1)} %get-tuple-element.522), channel_id=1, source_target_pairs={{0,8},{2,10},{4,12},{6,14},{8,0},{10,2},{12,4},{14,6},{16,24},{18,... | collective-permute-start | bytes 1179656 | tf_op jit(solution)/shard_map/ppermute | solution.py:1189
  328.0 45.8 %collective-permute-start.23 = (bf16[2,256,256]{2,1,0:T(8,128)(2,1)}, bf16[2,256,256]{2,1,0:T(8,128)(2,1)}, u32[]{:S(2)}, u32[]{:S(2)}) collective-permute-start(bf16[2,256,256]{2,1,0:T(8,128)(2,1)} %get-tuple-element.504.refs_3_), channel_id=1, source_target_pairs={{0,8},{2,10},{4,12},{6,14},{8,0},{10,2},{12,4},{14,6},{16,24},{18,... | collective-permute-start | bytes 786440 | tf_op jit(solution)/shard_map/ppermute | solution.py:1189
  333.4 40.4 %collective-permute-start.25 = (bf16[1,256,384]{2,1,0:T(8,128)(2,1)}, bf16[1,256,384]{2,1,0:T(8,128)(2,1)}, u32[]{:S(2)}, u32[]{:S(2)}) collective-permute-start(bf16[1,256,384]{2,1,0:T(8,128)(2,1)} %get-tuple-element.523), channel_id=1, source_target_pairs={{0,16},{2,18},{4,20},{6,22},{8,24},{10,26},{12,28},{14,30},{16,0},... | collective-permute-start | bytes 589832 | tf_op jit(solution)/shard_map/ppermute | solution.py:1189
  333.8 40.0 %collective-permute-start.21 = (bf16[4,80,2048]{2,1,0:T(8,128)(2,1)}, bf16[4,80,2048]{2,1,0:T(8,128)(2,1)}, u32[]{:S(2)}, u32[]{:S(2)}) collective-permute-start(bf16[4,80,2048]{2,1,0:T(8,128)(2,1)} %get-tuple-element.505.refs_5_), channel_id=1, source_target_pairs={{0,4},{2,6},{4,0},{6,2},{8,12},{10,14},{12,8},{14,10},{16,20},{18,... | collective-permute-start | bytes 3932168 | tf_op jit(solution)/shard_map/ppermute | solution.py:1189
  339.6 34.2 %collective-permute-start.22 = (bf16[4,64,2048]{2,1,0:T(8,128)(2,1)}, bf16[4,64,2048]{2,1,0:T(8,128)(2,1)}, u32[]{:S(2)}, u32[]{:S(2)}) collective-permute-start(bf16[4,64,2048]{2,1,0:T(8,128)(2,1)} %get-tuple-element.506.refs_19_), channel_id=1, source_target_pairs={{0,8},{2,10},{4,12},{6,14},{8,0},{10,2},{12,4},{14,6},{16,24},{18,... | collective-permute-start | bytes 3145736 | tf_op jit(solution)/shard_map/ppermute | solution.py:1189
  379.4 42.2 %collective-permute-start.30 = (bf16[2,80,2048]{2,1,0:T(8,128)(2,1)}, bf16[2,80,2048]{2,1,0:T(8,128)(2,1)}, u32[]{:S(2)}, u32[]{:S(2)}) collective-permute-start(bf16[2,80,2048]{2,1,0:T(8,128)(2,1)} %get-tuple-element.524.refs_12_), channel_id=1, source_target_pairs={{0,8},{2,10},{4,12},{6,14},{8,0},{10,2},{12,4},{14,6},{16,24},{18,... | collective-permute-start | bytes 1966088 | tf_op jit(solution)/shard_map/ppermute | solution.py:1189
  380.4 20.9 %collective-permute-start.29 = (bf16[4,64,1024]{2,1,0:T(8,128)(2,1)S(1)}, bf16[4,64,1024]{2,1,0:T(8,128)(2,1)}, u32[]{:S(2)}, u32[]{:S(2)}) collective-permute-start(bf16[4,64,1024]{2,1,0:T(8,128)(2,1)S(1)} %copy-done.55), channel_id=1, source_target_pairs={{0,4},{2,6},{4,0},{6,2},{8,12},{10,14},{12,8},{14,10},{16,20},{18,... | collective-permute-start | bytes 1572872 | tf_op jit(solution)/shard_map/ppermute | solution.py:1189
  381.7 39.9 %collective-permute-start.31 = (bf16[2,64,2048]{2,1,0:T(8,128)(2,1)}, bf16[2,64,2048]{2,1,0:T(8,128)(2,1)}, u32[]{:S(2)}, u32[]{:S(2)}) collective-permute-start(bf16[2,64,2048]{2,1,0:T(8,128)(2,1)} %get-tuple-element.537), channel_id=1, source_target_pairs={{0,16},{2,18},{4,20},{6,22},{8,24},{10,26},{12,28},{14,30},{16,0},... | collective-permute-start | bytes 1572872 | tf_op jit(solution)/shard_map/ppermute | solution.py:1189
  384.3 36.8 %collective-permute-start.33 = (bf16[1,256,384]{2,1,0:T(8,128)(2,1)}, bf16[1,256,384]{2,1,0:T(8,128)(2,1)S(1)}, u32[]{:S(2)}, u32[]{:S(2)}) collective-permute-start(bf16[1,256,384]{2,1,0:T(8,128)(2,1)} %get-tuple-element.539), channel_id=1, source_target_pairs={{0,16},{2,18},{4,20},{6,22},{8,24},{10,26},{12,28},{14,30},{16,0},... | collective-permute-start | bytes 589832 | tf_op jit(solution)/shard_map/ppermute | solution.py:1189
  384.6 36.4 %collective-permute-start.32 = (bf16[1,256,256]{2,1,0:T(8,128)(2,1)}, bf16[1,256,256]{2,1,0:T(8,128)(2,1)S(1)}, u32[]{:S(2)}, u32[]{:S(2)}) collective-permute-start(bf16[1,256,256]{2,1,0:T(8,128)(2,1)} %get-tuple-element.538), channel_id=1, source_target_pairs={{0,16},{2,18},{4,20},{6,22},{8,24},{10,26},{12,28},{14,30},{16,0},... | collective-permute-start | bytes 393224 | tf_op jit(solution)/shard_map/ppermute | solution.py:1189
  401.3 34.7 %collective-permute-start.20 = (bf16[2,512,512]{2,1,0:T(8,128)(2,1)S(1)}, bf16[2,512,512]{2,1,0:T(8,128)(2,1)S(1)}, u32[]{:S(2)}, u32[]{:S(2)}) collective-permute-start(bf16[2,512,512]{2,1,0:T(8,128)(2,1)S(1)} %copy-done.23), channel_id=1, source_target_pairs={{0,1},{2,3},{4,5},{6,7},{8,9},{10,11},{12,13},{14,15},{16,17},{18,... | collective-permute-start | bytes 3145736 | tf_op jit(solution)/shard_map/ppermute | solution.py:1193
  425.1 14.0 %collective-permute-start.34 = (bf16[1,64,2048]{2,1,0:T(8,128)(2,1)}, bf16[1,64,2048]{2,1,0:T(8,128)(2,1)S(1)}, u32[]{:S(2)}, u32[]{:S(2)}) collective-permute-start(bf16[1,64,2048]{2,1,0:T(8,128)(2,1)} %get-tuple-element.546), channel_id=1, source_target_pairs={{0,4},{2,6},{4,0},{6,2},{8,12},{10,14},{12,8},{14,10},{16,20},{18,... | collective-permute-start | bytes 786440 | tf_op jit(solution)/shard_map/ppermute | solution.py:1189
  425.7 17.9 %collective-permute-start.36 = (bf16[1,80,2048]{2,1,0:T(8,128)(2,1)}, bf16[1,80,2048]{2,1,0:T(8,128)(2,1)S(1)}, u32[]{:S(2)}, u32[]{:S(2)}) collective-permute-start(bf16[1,80,2048]{2,1,0:T(8,128)(2,1)} %get-tuple-element.550), channel_id=1, source_target_pairs={{0,16},{2,18},{4,20},{6,22},{8,24},{10,26},{12,28},{14,30},{16,0},... | collective-permute-start | bytes 983048 | tf_op jit(solution)/shard_map/ppermute | solution.py:1189
  425.7 16.0 %collective-permute-start.37 = (bf16[2,64,1024]{2,1,0:T(8,128)(2,1)}, bf16[2,64,1024]{2,1,0:T(8,128)(2,1)S(1)}, u32[]{:S(2)}, u32[]{:S(2)}) collective-permute-start(bf16[2,64,1024]{2,1,0:T(8,128)(2,1)} %get-tuple-element.540.refs_7_), channel_id=1, source_target_pairs={{0,8},{2,10},{4,12},{6,14},{8,0},{10,2},{12,4},{14,6},{16,24},{18,... | collective-permute-start | bytes 786440 | tf_op jit(solution)/shard_map/ppermute | solution.py:1189
  434.5 15.1 %collective-permute-start.35 = (bf16[4,64,1024]{2,1,0:T(8,128)(2,1)}, bf16[4,64,1024]{2,1,0:T(8,128)(2,1)S(1)}, u32[]{:S(2)}, u32[]{:S(2)}) collective-permute-start(bf16[4,64,1024]{2,1,0:T(8,128)(2,1)} %get-tuple-element.541.refs_3_), channel_id=1, source_target_pairs={{0,4},{2,6},{4,0},{6,2},{8,12},{10,14},{12,8},{14,10},{16,20},{18,... | collective-permute-start | bytes 1572872 | tf_op jit(solution)/shard_map/ppermute | solution.py:1189
  436.1 24.8 %collective-permute-start.38 = (bf16[4,64,1024]{2,1,0:T(8,128)(2,1)}, bf16[4,64,1024]{2,1,0:T(8,128)(2,1)S(1)}, u32[]{:S(2)}, u32[]{:S(2)}) collective-permute-start(bf16[4,64,1024]{2,1,0:T(8,128)(2,1)} %get-tuple-element.555), channel_id=1, source_target_pairs={{0,4},{2,6},{4,0},{6,2},{8,12},{10,14},{12,8},{14,10},{16,20},{18,... | collective-permute-start | bytes 1572872 | tf_op jit(solution)/shard_map/ppermute | solution.py:1189
  453.4 17.3 %collective-permute-start.40 = (bf16[4,64,1024]{2,1,0:T(8,128)(2,1)}, bf16[4,64,1024]{2,1,0:T(8,128)(2,1)}, u32[]{:S(2)}, u32[]{:S(2)}) collective-permute-start(bf16[4,64,1024]{2,1,0:T(8,128)(2,1)} %get-tuple-element.559), channel_id=1, source_target_pairs={{0,4},{2,6},{4,0},{6,2},{8,12},{10,14},{12,8},{14,10},{16,20},{18,... | collective-permute-start | bytes 1572872 | tf_op jit(solution)/shard_map/ppermute | solution.py:1189
  463.8 12.3 %collective-permute-start.41 = (bf16[2,64,1024]{2,1,0:T(8,128)(2,1)}, bf16[2,64,1024]{2,1,0:T(8,128)(2,1)S(1)}, u32[]{:S(2)}, u32[]{:S(2)}) collective-permute-start(bf16[2,64,1024]{2,1,0:T(8,128)(2,1)} %get-tuple-element.560.refs_7_), channel_id=1, source_target_pairs={{0,8},{2,10},{4,12},{6,14},{8,0},{10,2},{12,4},{14,6},{16,24},{18,... | collective-permute-start | bytes 786440 | tf_op jit(solution)/shard_map/ppermute | solution.py:1189
  (77 other events, 513.1 us)

commit v4 on v3

--- a/solution.py
+++ b/solution.py
@@ -1255,15 +1255,14 @@
     hop_b = one_way(y_b0, 0, 1)
     other_gy = [one_way(cotangent_later[s], 0, 1) for s in range(seqs)]
 
-    def squeeze(layer):
-        tokens = last[0]
-        work = lambda: compress(reset_flags, memory, w_compress[0], b_compress, tokens)
-        skip = lambda: unset([(seqs, COMP, WIDTH)], tokens)
-        made = lax.cond(section == layer, work, skip)[0]
-        last[0] = [made]
-        return made
-
-    squeezed_first = squeeze(0)
+    def squeeze_now(tokens):
+        return compress(reset_flags, memory, w_compress[0], b_compress, tokens)
+
+    tokens = last[0]
+    (squeezed_first,) = lax.cond(
+        is_first, lambda: squeeze_now(tokens), lambda: unset([(seqs, COMP, WIDTH)], tokens)
+    )
+    last[0] = [squeezed_first]
 
     def back(layer, s, gys, fed, made, estimate, part=SEG):
         fed = feed_back(s, [active[layer]], gys, saved, params, fed, last[0], estimate)
@@ -1346,9 +1345,13 @@
     )
     last[0] = [base_down]
 
-    def early_second(kind):
+    def early_second(kind, more=None, dims=()):
         tokens = last[0]
-        made_late = lax.cond(is_first, lambda: unset(sizes[kind], tokens), lambda: early(tokens, kind))
+        made_late = lax.cond(
+            is_first,
+            lambda: unset(sizes[kind] + list(dims), tokens),
+            lambda: early(tokens, kind) + (more(tokens) if more else []),
+        )
         last[0] = [made_late[0]]
         return made_late
 
@@ -1441,8 +1444,7 @@
         1, [active[0], reset_flags, boundary], saved, fed, kv_memory[1], params, made, last[0]
     )
     last[0] = [dx_b0]
-    (proj_second,) = early_second("proj")
-    squeezed_second = squeeze(1)
+    proj_second, squeezed_second = early_second("proj", squeeze_now, [(seqs, COMP, WIDTH)])
     outputs = pick(at_section, other_y, saved["y_high"], last[0])
     last[0] = [outputs]
     halved("up1", "up0", "down1", "down2", "down0")
@@ -1464,13 +1466,17 @@
         [(1, WIDTH)] * 3,
         estimate=SHORT,
     )
-    halved("out", "up1", "up0", "down1", "down2", estimate=LONG)
+    halved("out", "up1", "up0", estimate=LONG)
     halved("key", "value", "query")
-    grad_inputs = pick(at_section, made["dx_low"], one_way(made["dx_high"], 0, 1), last[0])
+    leaving, token = both_after(made["dx_high"], last[0][0])
+    last[0] = [token]
+    halved("up0", "down1", "down2", estimate=LONG)
+    halved("key", "up1", "out")
+    halved("value", "key")
+    grad_inputs = pick(at_section, made["dx_low"], one_way(leaving, 0, 1), last[0])
     last[0] = [grad_inputs]
-    halved("up0", estimate=LONG)
-    for names in (("key", "up1", "out"), ("value", "key"), ("query", "value", "out"), ("query", "key")):
-        halved(*names)
+    halved("query", "value", "out")
+    halved("query", "key")
     while any(step + 1 < levels for _, _, step in moving.values()):
         halved(*[name for name, (_, _, step) in moving.items() if step + 1 < levels])
     if "up1" in moving:

time: 510 us -> 513 us (level)
    unnamed x124 -> x128, local copies, waits for them, and re-layouts: 16.8 us -> 14.8 us
  transfers between devices with their start and end apart: 47 -> 47, of which waited for: 12 -> 13; matrix products, arithmetic and copies ran while one was open for 2% -> 2% of each run, Pallas kernels for 61% -> 61%
where the time goes in v4:
time: 513 us; the launch traced here: 504 us
  Pallas kernels  329 us (64%)
  waiting for transfers between devices  89.9 us (18%)
  starting transfers between devices  50.1 us (10%)
  local copies, waits for them, and re-layouts  21.9 us (4%)
  loops' own time  6.05 us (1%)
  other arithmetic  5.25 us (1%)
    pallas_call x41, Pallas kernels, call(): pl.pallas_call(run, name=name, grid_spec=pltpu.PrefetchScalarGridSpec(num...  329 us
    ppermute x36, waiting for transfers between devices, swap_bit(): return lax.ppermute(value, 'dp', [(i, i ^ 1 << bit) for i in range(size)])  61 us
    ppermute x36, starting transfers between devices, swap_bit(): return lax.ppermute(value, 'dp', [(i, i ^ 1 << bit) for i in range(size)])  30 us
    ppermute x11, waiting for transfers between devices, one_way(): return lax.ppermute(value, 'section', [(first, second)])  28.9 us
    ppermute x11, starting transfers between devices, one_way(): return lax.ppermute(value, 'section', [(first, second)])  20.1 us
    unnamed x128, local copies, waits for them, and re-layouts  14.8 us
  transfers between devices with their start and end apart: 47, of which 13 were waited for; matrix products, arithmetic and copies ran while one was open for 2% of the time, Pallas kernels for 61%

profile of v4, /device:TPU:26, one launch (start us, length us, event | category | flops | bytes accessed | tf_op | source)
XLA Modules:
  0.0 504.2 jit_solution(2725493036073542070)
XLA Ops:
  4.2 10.2 %memory_keyvals.2 = (bf16[1,1024,1024]{2,1,0:T(8,128)(2,1)}, bf16[1,1024,2048]{2,1,0:T(8,128)(2,1)}) custom-call(s32[2]{0:T(128)} %refs_1_.15, bf16[2,512,1024]{2,1,0:T(8,128)(2,1)} %bitcast.71, bf16[2,512,1024]{2,1,0:T(8,128)(2,1)} %bitcast.69, bf16[1,1024]{1,0:T(2,128)(2,1)} %refs_10_.11, bf16[1024,3072]{1,0:T(8,128)(2,1)} %bitcast.38), custom_call_target="tpu_custom_call" | custom-call | flops 99999997952 | bytes 1 | tf_op jit(solution)/shard_map/memory_keyvals/pallas_call | solution.py:83
  18.2 7.8 %forward.4 = (bf16[512,1024]{1,0:T(8,128)(2,1)}, bf16[2,512,1024]{2,1,0:T(8,128)(2,1)}, bf16[2,512,1024]{2,1,0:T(8,128)(2,1)S(1)}, bf16[2,512,3072]{2,1,0:T(8,12...) custom-call(s32[1]{0:T(128)S(6)} %sub.6.refs_0_, ...), custom_call_target="tpu_custom_call" | custom-call | flops 99999997952 | bytes 1 | tf_op jit(solution)/shard_map/forward/pallas_call | solution.py:83
  27.3 9.9 %memory_keyvals.3 = (bf16[1,1024,1024]{2,1,0:T(8,128)(2,1)}, bf16[1,1024,2048]{2,1,0:T(8,128)(2,1)}) custom-call(s32[2]{0:T(128)S(1)} %copy-done.49, bf16[2,512,1024]{2,1,0:T(8,128)(2,1)} %bitcast.72, bf16[2,512,1024]{2,1,0:T(8,128)(2,1)} %bitcast.70, bf16[1,1024]{1,0:T(2,128)(2,1)} %refs_10_.11, bf16[1024,3072]{1,0:T(8,128)(2,1)} %bitcast.40, ...), custom_call_target="tpu_custom_call" | custom-call | flops 99999997952 | bytes 1 | tf_op jit(solution)/shard_map/memory_keyvals/pallas_call | solution.py:83
  37.3 6.9 %forward.5 = (bf16[512,1024]{1,0:T(8,128)(2,1)}, bf16[2,512,1024]{2,1,0:T(8,128)(2,1)}, bf16[2,512,1024]{2,1,0:T(8,128)(2,1)S(1)}, bf16[2,512,3072]{2,1,0:T(8,12...) custom-call(s32[1]{0:T(128)S(6)} %sub.6.refs_0_, ...), custom_call_target="tpu_custom_call", output_to_operand_aliasing={{1}: (14, {}), {2}: (15, {}), {3}: (16, {}), {4}: (17, {}),... | custom-call | flops 1 | bytes 1 | tf_op jit(solution)/shard_map/forward/pallas_call | solution.py:83
  50.5 21.9 %collective-permute-done.3.refs_3_ = bf16[512,1024]{1,0:T(8,128)(2,1)} collective-permute-done((bf16[512,1024]{1,0:T(8,128)(2,1)}, bf16[512,1024]{1,0:T(8,128)(2,1)}, u32[]{:S(2)}, u32[]{:S(2)}) %collective-permute-start.3) | collective-permute-done | bytes 1048608 | tf_op jit(solution)/shard_map/ppermute | solution.py:1193
  72.4 29.9 %forward.6 = (bf16[512,1024]{1,0:T(8,128)(2,1)}, bf16[2,512,1024]{2,1,0:T(8,128)(2,1)}, bf16[2,512,1024]{2,1,0:T(8,128)(2,1)S(1)}, bf16[2,512,3072]{2,1,0:T(8,12...) custom-call(s32[1]{0:T(128)} %bitcast.2.refs_0_, ...), custom_call_target="tpu_custom_call", output_to_operand_aliasing={{1}: (13, {}), {2}: (14, {}), {3}: (15, {}), {4}: (16, {}),... | custom-call | flops 1 | bytes 1 | tf_op jit(solution)/shard_map/forward/pallas_call | solution.py:83
  102.3 7.0 %collective-permute-done.4.refs_1_ = bf16[512,512]{1,0:T(8,128)(2,1)} collective-permute-done((bf16[512,512]{1,0:T(8,128)(2,1)}, bf16[512,512]{1,0:T(8,128)(2,1)}, u32[]{:S(2)}, u32[]{:S(2)}) %collective-permute-start.4) | collective-permute-done | bytes 524320 | tf_op jit(solution)/shard_map/ppermute | solution.py:1193
  109.3 16.8 %feed_back.4 = (bf16[2,512,4096]{2,1,0:T(8,128)(2,1)}, f32[2,512,1024]{2,1,0:T(8,128)}, bf16[2,512,1024]{2,1,0:T(8,128)(2,1)}, bf16[2,512,1024]{2,1,0:T(8,128)(2...) custom-call(s32[1]{0:T(128)} %bitcast.2.refs_0_, bf16[512,512]{1,0:T(8,128)(2,1)} %collective-permute-done.4.refs_1_, ...), custom_call_target="tpu_custom_call" | custom-call | flops 1 | bytes 1 | tf_op jit(solution)/shard_map/feed_back/pallas_call | solution.py:83
  126.1 24.0 %attend_back.4 = (bf16[512,1024]{1,0:T(8,128)(2,1)}, bf16[2,512,1024]{2,1,0:T(8,128)(2,1)}, bf16[2,512,1024]{2,1,0:T(8,128)(2,1)}, bf16[2,512,1024]{2,1,0:T(8,12...) custom-call(s32[1]{0:T(128)} %bitcast.2.refs_0_, ...), custom_call_target="tpu_custom_call" | custom-call | flops 1 | bytes 1 | tf_op jit(solution)/shard_map/attend_back/pallas_call | solution.py:83
  153.6 30.1 %forward.7 = (bf16[512,1024]{1,0:T(8,128)(2,1)}, bf16[2,512,1024]{2,1,0:T(8,128)(2,1)}, bf16[2,512,1024]{2,1,0:T(8,128)(2,1)S(1)}, bf16[2,512,3072]{2,1,0:T(8,12...) custom-call(s32[1]{0:T(128)} %bitcast.2.refs_0_, ...), custom_call_target="tpu_custom_call", output_to_operand_aliasing={{1}: (13, {}), {2}: (14, {}), {3}: (15, {}), {4}: (16, {}),... | custom-call | flops 1 | bytes 1 | tf_op jit(solution)/shard_map/forward/pallas_call | solution.py:83
  183.8 18.0 %feed_back.5 = (bf16[2,512,4096]{2,1,0:T(8,128)(2,1)}, f32[2,512,1024]{2,1,0:T(8,128)}, bf16[2,512,1024]{2,1,0:T(8,128)(2,1)}, bf16[2,512,1024]{2,1,0:T(8,128)(2...) custom-call(s32[1]{0:T(128)} %bitcast.2.refs_0_, ...), custom_call_target="tpu_custom_call", output_to_operand_aliasing={{0}: (9, {}), {1}: (10, {}), {2}: (11, {}), {3}: (12, {}), ... | custom-call | flops 1 | bytes 1 | tf_op jit(solution)/shard_map/feed_back/pallas_call | solution.py:83
  201.9 21.6 %attend_back.5 = (bf16[256,1024]{1,0:T(8,128)(2,1)}, bf16[2,512,1024]{2,1,0:T(8,128)(2,1)}, bf16[2,512,1024]{2,1,0:T(8,128)(2,1)}, bf16[2,512,1024]{2,1,0:T(8,12...) custom-call(s32[1]{0:T(128)} %bitcast.2.refs_0_, ...), custom_call_target="tpu_custom_call", output_to_operand_aliasing={{1}: (12, {}), {2}: (13, {}), {3}: (14, {}), {4}: (15, {}),... | custom-call | flops 1 | bytes 1 | tf_op jit(solution)/shard_map/attend_back/pallas_call | solution.py:83
  225.6 6.8 %project_back.1.refs_14_ = bf16[256,1024]{1,0:T(8,128)(2,1)} custom-call(s32[1]{0:T(128)} %bitcast.2.refs_0_, bf16[2,512,1024]{2,1,0:T(8,128)(2,1)} %get-tuple-element.441.refs_1_.refs_12_, bf16[2,512,1024]{2,1,0:T(8,128)(2,1)} %get-tuple-element.442.refs_2_.refs_13_, bf16[2,512,1024]{2,1,0:T(8,128)(2,1)} %get-tuple-element.443.refs_3_.refs_14_, ...), custom_call_target="tpu_custom_call" | custom-call | flops 99999997952 | bytes 1 | tf_op jit(solution)/shard_map/project_back/pallas_call | solution.py:83
  236.1 11.6 %attend_back.6 = (bf16[512,1024]{1,0:T(8,128)(2,1)}, bf16[2,512,1024]{2,1,0:T(8,128)(2,1)}, bf16[2,512,1024]{2,1,0:T(8,128)(2,1)}, bf16[2,512,1024]{2,1,0:T(8,12...) custom-call(s32[1]{0:T(128)S(6)} %sub.6.refs_0_, ...), custom_call_target="tpu_custom_call", output_to_operand_aliasing={{1}: (12, {}), {2}: (13, {}), {3}: (14, {}), {4}: (15, {}),... | custom-call | flops 1 | bytes 1 | tf_op jit(solution)/shard_map/attend_back/pallas_call | solution.py:83
  247.8 9.3 %conditional.5 = ((bf16[4096,1024]{1,0:T(8,128)(2,1)}, bf16[1024,4096]{1,0:T(8,128)(2,1)}, bf16[1024,1024]{1,0:T(8,128)(2,1)}, bf16[1024,3072]{1,0:T(8,128)(2,1)})) conditional(s32[]{:T(128)} %convert_element_type.25, (s32[1]{0:T(128)}, bf16[2,512,4096]{2,1,0:T(8,128)(2,1)}, bf16[512,1024]{1,0:T(8,128)(2,1)}, bf16[512,512]{1,0:T(8,128)(2,1)}, ...), branch_computations={%region_2.0_spmd, %region_3.0_spmd} | conditional | flops 2 | bytes 4194374 | solution.py:1341
  247.8 9.0 %early_grads.4 = bf16[4096,1024]{1,0:T(8,128)(2,1)} custom-call(s32[1]{0:T(128)} %get-tuple-element.105.refs_0_, bf16[2,512,4096]{2,1,0:T(8,128)(2,1)} %get-tuple-element.106.refs_1_, bf16[512,1024]{1,0:T(8,128)(2,1)} %get-tuple-element.107.refs_2_, bf16[512,512]{1,0:T(8,128)(2,1)} %get-tuple-element.108.refs_3_, ...), custom_call_target="tpu_custom_call" | custom-call | flops 1 | bytes 1 | tf_op jit(solution)/shard_map/cond/branch_0_fun/early_grads/pallas_call | solution.py:83
  257.1 11.5 %weight_grads.3 = (bf16[8,256,384]{2,1,0:T(8,128)(2,1)}, bf16[8,256,256]{2,1,0:T(8,128)(2,1)}, bf16[8,256,384]{2,1,0:T(8,128)(2,1)}, bf16[8,256,384]{2,1,0:T(8,1...) custom-call(s32[1]{0:T(128)} %bitcast.2.refs_0_, s32[1]{0:T(128)} %bitcast.13.refs_1_.refs_0_, ...), custom_call_target="tpu_custom_call" | custom-call | flops 99999997952 | bytes 1 | tf_op jit(solution)/shard_map/weight_grads/pallas_call | solution.py:83
  287.8 9.5 %conditional.6 = ((bf16[1024,4096]{1,0:T(8,128)(2,1)}, bf16[1024,1024]{1,0:T(8,128)(2,1)})) conditional(s32[]{:T(128)} %convert_element_type.25, (s32[1]{0:T(128)}, bf16[2,512,1024]{2,1,0:T(8,128)(2,1)S(1)}, bf16[2,512,4096]{2,1,0:T(8,128)(2,1)}, bf16[2,512,1024]{2,1,0:T(8,128)(2,1)S(1)}, bf16[2,512,1024]{2,1,0:T(8,128)(2,1)}, ...), branch_computations={%region_4.0_spmd, %region_5.0_spmd} | conditional | flops 1 | bytes 9 | solution.py:1350
  287.8 9.4 %early_grads.6 = (bf16[1024,4096]{1,0:T(8,128)(2,1)}, bf16[1024,1024]{1,0:T(8,128)(2,1)}) custom-call(s32[1]{0:T(128)} %get-tuple-element.131.refs_0_, bf16[2,512,1024]{2,1,0:T(8,128)(2,1)S(1)} %get-tuple-element.132.refs_1_, bf16[2,512,4096]{2,1,0:T(8,128)(2,1)} %get-tuple-element.133.refs_2_, bf16[2,512,1024]{2,1,0:T(8,128)(2,1)S(1)} %get-tuple-element.134.refs_3_, ...), custom_call_target="tpu_custom_call" | custom-call | flops 1 | bytes 1 | tf_op jit(solution)/shard_map/cond/branch_0_fun/early_grads/pallas_call | solution.py:83
  304.4 15.5 %weight_grads.4 = (bf16[8,64,2048]{2,1,0:T(8,128)(2,1)}, bf16[8,80,2048]{2,1,0:T(8,128)(2,1)}, bf16[8,64,1024]{2,1,0:T(8,128)(2,1)}, bf16[8,64,2048]{2,1,0:T(8,1...) custom-call(s32[1]{0:T(128)} %bitcast.2.refs_0_, s32[1]{0:T(128)} %bitcast.13.refs_1_.refs_0_, ...), custom_call_target="tpu_custom_call" | custom-call | flops 1 | bytes 1 | tf_op jit(solution)/shard_map/weight_grads/pallas_call | solution.py:83
  345.0 28.0 %conditional.7 = ((bf16[1024,3072]{1,0:T(8,128)(2,1)}, bf16[2,256,1024]{2,1,0:T(8,128)(2,1)})) conditional(s32[]{:T(128)} %convert_element_type.25, (s32[1]{0:T(128)}, bf16[2,512,1024]{2,1,0:T(8,128)(2,1)S(1)}, bf16[1,1024,1024]{2,1,0:T(8,128)(2,1)S(1)}, bf16[2,512,1024]{2,1,0:T(8,128)(2,1)}, bf16[2,1024,1024]{2,1,0:T(8,128)(2,1)}, ...), branch_computations={%region_8.9_spmd, %region_9.10_spmd} | conditional | flops 2 | bytes 4194330 | solution.py:1350
  350.3 11.8 %early_grads.7 = bf16[1024,3072]{1,0:T(8,128)(2,1)} custom-call(s32[1]{0:T(128)} %get-tuple-element.137.refs_0_, bf16[2,512,1024]{2,1,0:T(8,128)(2,1)S(1)} %get-tuple-element.138.refs_1_.refs_7_, bf16[1,1024,1024]{2,1,0:T(8,128)(2,1)S(1)} %get-tuple-element.139.refs_2_, bf16[2,512,1024]{2,1,0:T(8,128)(2,1)} %get-tuple-element.140.refs_3_, ...), custom_call_target="tpu_custom_call" | custom-call | flops 1 | bytes 1 | tf_op jit(solution)/shard_map/cond/branch_0_fun/early_grads/pallas_call | solution.py:83
  366.2 6.5 %compress.3 = bf16[2,256,1024]{2,1,0:T(8,128)(2,1)} custom-call(s32[2]{0:T(128)S(1)} %get-tuple-element.146.refs_0_, bf16[2,256,2048]{2,1,0:T(8,128)(2,1)} %reshape_squeeze.5.refs_1_, bf16[2048,1024]{1,0:T(8,128)(2,1)} %bitcast.68, bf16[1,1024]{1,0:T(2,128)(2,1)S(1)} %get-tuple-element.149.refs_3_, bf16[512,1024]{1,0:T(8,128)(2,1)S(1)} %get-tuple-element.145.refs_9_.refs_4_), custom_call_target="tpu_custom_call" | custom-call | flops 1 | bytes 1 | tf_op jit(solution)/shard_map/cond/branch_0_fun/compress/pallas_call | solution.py:83
  375.9 4.9 halve.20
  385.4 14.0 %weight_grads.5 = (bf16[8,64,1024]{2,1,0:T(8,128)(2,1)}, bf16[8,64,1024]{2,1,0:T(8,128)(2,1)}, bf16[8,64,1024]{2,1,0:T(8,128)(2,1)}, bf16[8,64,1024]{2,1,0:T(8,1...) custom-call(s32[1]{0:T(128)} %bitcast.2.refs_0_, s32[1]{0:T(128)} %bitcast.13.refs_1_.refs_0_, ...), custom_call_target="tpu_custom_call" | custom-call | flops 1 | bytes 1 | tf_op jit(solution)/shard_map/weight_grads/pallas_call | solution.py:83
  400.1 6.8 %collective-permute-done.30.refs_6_ = bf16[2,64,2048]{2,1,0:T(8,128)(2,1)} collective-permute-done((bf16[2,64,2048]{2,1,0:T(8,128)(2,1)}, bf16[2,64,2048]{2,1,0:T(8,128)(2,1)}, u32[]{:S(2)}, u32[]{:S(2)}) %collective-permute-start.30) | collective-permute-done | bytes 524320 | tf_op jit(solution)/shard_map/ppermute | solution.py:1189
  419.8 4.6 halve.22
  424.4 14.2 %collective-permute-done.36.refs_5_ = bf16[1,256,256]{2,1,0:T(8,128)(2,1)S(1)} collective-permute-done((bf16[1,256,256]{2,1,0:T(8,128)(2,1)S(1)}, bf16[1,256,256]{2,1,0:T(8,128)(2,1)S(1)}, u32[]{:S(2)}, u32[]{:S(2)}) %collective-permute-start.36) | collective-permute-done | bytes 131104 | tf_op jit(solution)/shard_map/ppermute | solution.py:1189
  444.8 9.0 %collective-permute-done.32.refs_4_ = bf16[4,64,1024]{2,1,0:T(8,128)(2,1)S(1)} collective-permute-done((bf16[4,64,1024]{2,1,0:T(8,128)(2,1)}, bf16[4,64,1024]{2,1,0:T(8,128)(2,1)S(1)}, u32[]{:S(2)}, u32[]{:S(2)}) %collective-permute-start.32) | collective-permute-done | bytes 524320 | tf_op jit(solution)/shard_map/ppermute | solution.py:1189
  458.2 6.8 %collective-permute-done.38.refs_3_ = bf16[4,64,1024]{2,1,0:T(8,128)(2,1)S(1)} collective-permute-done((bf16[4,64,1024]{2,1,0:T(8,128)(2,1)}, bf16[4,64,1024]{2,1,0:T(8,128)(2,1)S(1)}, u32[]{:S(2)}, u32[]{:S(2)}) %collective-permute-start.38) | collective-permute-done | bytes 524320 | tf_op jit(solution)/shard_map/ppermute | solution.py:1189
  482.5 6.7 %collective-permute-done.43.refs_3_ = bf16[2,64,1024]{2,1,0:T(8,128)(2,1)S(1)} collective-permute-done((bf16[2,64,1024]{2,1,0:T(8,128)(2,1)}, bf16[2,64,1024]{2,1,0:T(8,128)(2,1)S(1)}, u32[]{:S(2)}, u32[]{:S(2)}) %collective-permute-start.43) | collective-permute-done | bytes 262176 | tf_op jit(solution)/shard_map/ppermute | solution.py:1189
  493.5 5.1 %collective-permute-done.45.refs_10_ = bf16[1,64,1024]{2,1,0:T(8,128)(2,1)S(1)} collective-permute-done((bf16[1,64,1024]{2,1,0:T(8,128)(2,1)}, bf16[1,64,1024]{2,1,0:T(8,128)(2,1)S(1)}, u32[]{:S(2)}, u32[]{:S(2)}) %collective-permute-start.45) | collective-permute-done | bytes 131104 | tf_op jit(solution)/shard_map/ppermute | solution.py:1189
  (252 shorter events, 137.7 us)
Async XLA Ops:
  15.3 22.0 %collective-permute-start = (bf16[512,512]{1,0:T(8,128)(2,1)}, bf16[512,512]{1,0:T(8,128)(2,1)}, u32[]{:S(2)}, u32[]{:S(2)}) collective-permute-start(bf16[512,512]{1,0:T(8,128)(2,1)} %slice_bitcast_fusion.3), channel_id=1, source_target_pairs={{1,0},{3,2},{5,4},{7,6},{9,8},{11,10},{13,12},{15,14},{17,16},{19,... | collective-permute-start | bytes 1572872 | tf_op jit(solution)/shard_map/ppermute | solution.py:1193
  26.0 46.4 %collective-permute-start.3 = (bf16[512,1024]{1,0:T(8,128)(2,1)}, bf16[512,1024]{1,0:T(8,128)(2,1)}, u32[]{:S(2)}, u32[]{:S(2)}) collective-permute-start(bf16[512,1024]{1,0:T(8,128)(2,1)} %get-tuple-element.374.refs_5_), channel_id=1, source_target_pairs={{0,1},{2,3},{4,5},{6,7},{8,9},{10,11},{12,13},{14,15},{16,17},{18,... | collective-permute-start | bytes 3145736 | tf_op jit(solution)/shard_map/ppermute | solution.py:1193
  47.9 61.4 %collective-permute-start.4 = (bf16[512,512]{1,0:T(8,128)(2,1)}, bf16[512,512]{1,0:T(8,128)(2,1)}, u32[]{:S(2)}, u32[]{:S(2)}) collective-permute-start(bf16[512,512]{1,0:T(8,128)(2,1)} %get-tuple-element.581), channel_id=1, source_target_pairs={{0,1},{2,3},{4,5},{6,7},{8,9},{10,11},{12,13},{14,15},{16,17},{18,... | collective-permute-start | bytes 1572872 | tf_op jit(solution)/shard_map/ppermute | solution.py:1193
  49.1 104.5 %collective-permute-start.2 = (bf16[512,1024]{1,0:T(8,128)(2,1)}, bf16[512,1024]{1,0:T(8,128)(2,1)}, u32[]{:S(2)}, u32[]{:S(2)}) collective-permute-start(bf16[512,1024]{1,0:T(8,128)(2,1)} %get-tuple-element.388), channel_id=1, source_target_pairs={{0,1},{2,3},{4,5},{6,7},{8,9},{10,11},{12,13},{14,15},{16,17},{18,... | collective-permute-start | bytes 3145736 | tf_op jit(solution)/shard_map/ppermute | solution.py:1193
  150.1 75.5 %collective-permute-start.8 = (bf16[512,1024]{1,0:T(8,128)(2,1)}, bf16[512,1024]{1,0:T(8,128)(2,1)}, u32[]{:S(2)}, u32[]{:S(2)}) collective-permute-start(bf16[512,1024]{1,0:T(8,128)(2,1)} %get-tuple-element.415.refs_24_), channel_id=1, source_target_pairs={{1,0},{3,2},{5,4},{7,6},{9,8},{11,10},{13,12},{15,14},{17,16},{19,... | collective-permute-start | bytes 3145736 | tf_op jit(solution)/shard_map/ppermute | solution.py:1193
  152.3 31.4 %collective-permute-start.6 = (bf16[512,512]{1,0:T(8,128)(2,1)S(1)}, bf16[512,512]{1,0:T(8,128)(2,1)}, u32[]{:S(2)}, u32[]{:S(2)}) collective-permute-start(bf16[512,512]{1,0:T(8,128)(2,1)S(1)} %copy-done.35), channel_id=1, source_target_pairs={{0,1},{2,3},{4,5},{6,7},{8,9},{10,11},{12,13},{14,15},{16,17},{18,... | collective-permute-start | bytes 1572872 | tf_op jit(solution)/shard_map/ppermute | solution.py:1193
  223.5 33.6 %collective-permute-start.7 = (bf16[256,1024]{1,0:T(8,128)(2,1)}, bf16[256,1024]{1,0:T(8,128)(2,1)}, u32[]{:S(2)}, u32[]{:S(2)}) collective-permute-start(bf16[256,1024]{1,0:T(8,128)(2,1)} %get-tuple-element.440.refs_8_), channel_id=1, source_target_pairs={{1,0},{3,2},{5,4},{7,6},{9,8},{11,10},{13,12},{15,14},{17,16},{19,... | collective-permute-start | bytes 1572872 | tf_op jit(solution)/shard_map/ppermute | solution.py:1193
  232.4 24.7 %collective-permute-start.9 = (bf16[256,1024]{1,0:T(8,128)(2,1)}, bf16[256,1024]{1,0:T(8,128)(2,1)}, u32[]{:S(2)}, u32[]{:S(2)}) collective-permute-start(bf16[256,1024]{1,0:T(8,128)(2,1)} %project_back.1.refs_14_), channel_id=1, source_target_pairs={{1,0},{3,2},{5,4},{7,6},{9,8},{11,10},{13,12},{15,14},{17,16},{19,... | collective-permute-start | bytes 1572872 | tf_op jit(solution)/shard_map/ppermute | solution.py:1193
  276.4 21.0 %collective-permute-start.13 = (bf16[4,256,384]{2,1,0:T(8,128)(2,1)}, bf16[4,256,384]{2,1,0:T(8,128)(2,1)S(1)}, u32[]{:S(2)}, u32[]{:S(2)}) collective-permute-start(bf16[4,256,384]{2,1,0:T(8,128)(2,1)} %get-tuple-element.473.refs_5_), channel_id=1, source_target_pairs={{0,4},{2,6},{4,0},{6,2},{8,12},{10,14},{12,8},{14,10},{16,20},{18,... | collective-permute-start | bytes 2359304 | tf_op jit(solution)/shard_map/ppermute | solution.py:1189
  283.5 36.5 %collective-permute-start.17 = (bf16[4,256,256]{2,1,0:T(8,128)(2,1)}, bf16[4,256,256]{2,1,0:T(8,128)(2,1)}, u32[]{:S(2)}, u32[]{:S(2)}) collective-permute-start(bf16[4,256,256]{2,1,0:T(8,128)(2,1)} %get-tuple-element.474.refs_15_), channel_id=1, source_target_pairs={{0,4},{2,6},{4,0},{6,2},{8,12},{10,14},{12,8},{14,10},{16,20},{18,... | collective-permute-start | bytes 1572872 | tf_op jit(solution)/shard_map/ppermute | solution.py:1189
  284.0 40.4 %collective-permute-start.18 = (bf16[4,256,384]{2,1,0:T(8,128)(2,1)}, bf16[4,256,384]{2,1,0:T(8,128)(2,1)}, u32[]{:S(2)}, u32[]{:S(2)}) collective-permute-start(bf16[4,256,384]{2,1,0:T(8,128)(2,1)} %get-tuple-element.498), channel_id=1, source_target_pairs={{0,4},{2,6},{4,0},{6,2},{8,12},{10,14},{12,8},{14,10},{16,20},{18,... | collective-permute-start | bytes 2359304 | tf_op jit(solution)/shard_map/ppermute | solution.py:1189
  300.6 23.9 %collective-permute-start.19 = (bf16[2,256,384]{2,1,0:T(8,128)(2,1)}, bf16[2,256,384]{2,1,0:T(8,128)(2,1)}, u32[]{:S(2)}, u32[]{:S(2)}) collective-permute-start(bf16[2,256,384]{2,1,0:T(8,128)(2,1)} %get-tuple-element.488.refs_11_), channel_id=1, source_target_pairs={{0,8},{2,10},{4,12},{6,14},{8,0},{10,2},{12,4},{14,6},{16,24},{18,... | collective-permute-start | bytes 1179656 | tf_op jit(solution)/shard_map/ppermute | solution.py:1189
  301.1 40.0 %collective-permute-start.5 = (bf16[2,512,512]{2,1,0:T(8,128)(2,1)S(1)}, bf16[2,512,512]{2,1,0:T(8,128)(2,1)}, u32[]{:S(2)}, u32[]{:S(2)}) collective-permute-start(bf16[2,512,512]{2,1,0:T(8,128)(2,1)S(1)} %copy-done.16), channel_id=1, source_target_pairs={{1,0},{3,2},{5,4},{7,6},{9,8},{11,10},{13,12},{15,14},{17,16},{19,... | collective-permute-start | bytes 3145736 | tf_op jit(solution)/shard_map/ppermute | solution.py:1193
  327.2 47.9 %collective-permute-start.22 = (bf16[2,256,256]{2,1,0:T(8,128)(2,1)}, bf16[2,256,256]{2,1,0:T(8,128)(2,1)}, u32[]{:S(2)}, u32[]{:S(2)}) collective-permute-start(bf16[2,256,256]{2,1,0:T(8,128)(2,1)} %get-tuple-element.499.refs_3_), channel_id=1, source_target_pairs={{0,8},{2,10},{4,12},{6,14},{8,0},{10,2},{12,4},{14,6},{16,24},{18,... | collective-permute-start | bytes 786440 | tf_op jit(solution)/shard_map/ppermute | solution.py:1189
  329.6 45.5 %collective-permute-start.23 = (bf16[2,256,384]{2,1,0:T(8,128)(2,1)}, bf16[2,256,384]{2,1,0:T(8,128)(2,1)S(1)}, u32[]{:S(2)}, u32[]{:S(2)}) collective-permute-start(bf16[2,256,384]{2,1,0:T(8,128)(2,1)} %get-tuple-element.518), channel_id=1, source_target_pairs={{0,8},{2,10},{4,12},{6,14},{8,0},{10,2},{12,4},{14,6},{16,24},{18,... | collective-permute-start | bytes 1179656 | tf_op jit(solution)/shard_map/ppermute | solution.py:1189
  334.9 40.1 %collective-permute-start.24 = (bf16[1,256,384]{2,1,0:T(8,128)(2,1)}, bf16[1,256,384]{2,1,0:T(8,128)(2,1)}, u32[]{:S(2)}, u32[]{:S(2)}) collective-permute-start(bf16[1,256,384]{2,1,0:T(8,128)(2,1)} %get-tuple-element.519), channel_id=1, source_target_pairs={{0,16},{2,18},{4,20},{6,22},{8,24},{10,26},{12,28},{14,30},{16,0},... | collective-permute-start | bytes 589832 | tf_op jit(solution)/shard_map/ppermute | solution.py:1189
  335.3 39.8 %collective-permute-start.20 = (bf16[4,80,2048]{2,1,0:T(8,128)(2,1)}, bf16[4,80,2048]{2,1,0:T(8,128)(2,1)}, u32[]{:S(2)}, u32[]{:S(2)}) collective-permute-start(bf16[4,80,2048]{2,1,0:T(8,128)(2,1)} %get-tuple-element.500.refs_5_), channel_id=1, source_target_pairs={{0,4},{2,6},{4,0},{6,2},{8,12},{10,14},{12,8},{14,10},{16,20},{18,... | collective-permute-start | bytes 3932168 | tf_op jit(solution)/shard_map/ppermute | solution.py:1189
  341.1 34.1 %collective-permute-start.21 = (bf16[4,64,2048]{2,1,0:T(8,128)(2,1)}, bf16[4,64,2048]{2,1,0:T(8,128)(2,1)}, u32[]{:S(2)}, u32[]{:S(2)}) collective-permute-start(bf16[4,64,2048]{2,1,0:T(8,128)(2,1)} %get-tuple-element.501.refs_19_), channel_id=1, source_target_pairs={{0,8},{2,10},{4,12},{6,14},{8,0},{10,2},{12,4},{14,6},{16,24},{18,... | collective-permute-start | bytes 3145736 | tf_op jit(solution)/shard_map/ppermute | solution.py:1189
  380.8 27.9 %collective-permute-start.29 = (bf16[2,80,2048]{2,1,0:T(8,128)(2,1)}, bf16[2,80,2048]{2,1,0:T(8,128)(2,1)S(1)}, u32[]{:S(2)}, u32[]{:S(2)}) collective-permute-start(bf16[2,80,2048]{2,1,0:T(8,128)(2,1)} %get-tuple-element.520.refs_12_), channel_id=1, source_target_pairs={{0,8},{2,10},{4,12},{6,14},{8,0},{10,2},{12,4},{14,6},{16,24},{18,... | collective-permute-start | bytes 1966088 | tf_op jit(solution)/shard_map/ppermute | solution.py:1189
  381.5 18.5 %collective-permute-start.28 = (bf16[4,64,1024]{2,1,0:T(8,128)(2,1)S(1)}, bf16[4,64,1024]{2,1,0:T(8,128)(2,1)S(1)}, u32[]{:S(2)}, u32[]{:S(2)}) collective-permute-start(bf16[4,64,1024]{2,1,0:T(8,128)(2,1)S(1)} %copy-done.55), channel_id=1, source_target_pairs={{0,4},{2,6},{4,0},{6,2},{8,12},{10,14},{12,8},{14,10},{16,20},{18,... | collective-permute-start | bytes 1572872 | tf_op jit(solution)/shard_map/ppermute | solution.py:1189
  382.8 24.1 %collective-permute-start.30 = (bf16[2,64,2048]{2,1,0:T(8,128)(2,1)}, bf16[2,64,2048]{2,1,0:T(8,128)(2,1)}, u32[]{:S(2)}, u32[]{:S(2)}) collective-permute-start(bf16[2,64,2048]{2,1,0:T(8,128)(2,1)} %get-tuple-element.531), channel_id=1, source_target_pairs={{0,16},{2,18},{4,20},{6,22},{8,24},{10,26},{12,28},{14,30},{16,0},... | collective-permute-start | bytes 1572872 | tf_op jit(solution)/shard_map/ppermute | solution.py:1189
  399.4 16.0 %collective-permute-start.25 = (bf16[8,64,1024]{2,1,0:T(8,128)(2,1)}, bf16[8,64,1024]{2,1,0:T(8,128)(2,1)S(1)}, u32[]{:S(2)}, u32[]{:S(2)}) collective-permute-start(bf16[8,64,1024]{2,1,0:T(8,128)(2,1)} %get-tuple-element.524.refs_7_), channel_id=1, source_target_pairs={{0,2},{2,0},{4,6},{6,4},{8,10},{10,8},{12,14},{14,12},{16,18},{18,... | collective-permute-start | bytes 3145736 | tf_op jit(solution)/shard_map/ppermute | solution.py:1189
  399.5 17.1 %collective-permute-start.26 = (bf16[8,64,1024]{2,1,0:T(8,128)(2,1)}, bf16[8,64,1024]{2,1,0:T(8,128)(2,1)S(1)}, u32[]{:S(2)}, u32[]{:S(2)}) collective-permute-start(bf16[8,64,1024]{2,1,0:T(8,128)(2,1)} %get-tuple-element.525), channel_id=1, source_target_pairs={{0,2},{2,0},{4,6},{6,4},{8,10},{10,8},{12,14},{14,12},{16,18},{18,... | collective-permute-start | bytes 3145736 | tf_op jit(solution)/shard_map/ppermute | solution.py:1189
  400.0 18.4 %collective-permute-start.27 = (bf16[8,64,1024]{2,1,0:T(8,128)(2,1)}, bf16[8,64,1024]{2,1,0:T(8,128)(2,1)S(1)}, u32[]{:S(2)}, u32[]{:S(2)}) collective-permute-start(bf16[8,64,1024]{2,1,0:T(8,128)(2,1)} %get-tuple-element.526), channel_id=1, source_target_pairs={{0,2},{2,0},{4,6},{6,4},{8,10},{10,8},{12,14},{14,12},{16,18},{18,... | collective-permute-start | bytes 3145736 | tf_op jit(solution)/shard_map/ppermute | solution.py:1189
  412.4 28.8 %collective-permute-start.35 = (bf16[1,64,2048]{2,1,0:T(8,128)(2,1)}, bf16[1,64,2048]{2,1,0:T(8,128)(2,1)S(1)}, u32[]{:S(2)}, u32[]{:S(2)}) collective-permute-start(bf16[1,64,2048]{2,1,0:T(8,128)(2,1)} %get-tuple-element.543), channel_id=1, source_target_pairs={{0,4},{2,6},{4,0},{6,2},{8,12},{10,14},{12,8},{14,10},{16,20},{18,... | collective-permute-start | bytes 786440 | tf_op jit(solution)/shard_map/ppermute | solution.py:1189
  413.6 25.9 %collective-permute-start.37 = (bf16[1,256,384]{2,1,0:T(8,128)(2,1)S(1)}, bf16[1,256,384]{2,1,0:T(8,128)(2,1)S(1)}, u32[]{:S(2)}, u32[]{:S(2)}) collective-permute-start(bf16[1,256,384]{2,1,0:T(8,128)(2,1)S(1)} %copy-done.59), channel_id=1, source_target_pairs={{0,16},{2,18},{4,20},{6,22},{8,24},{10,26},{12,28},{14,30},{16,0},... | collective-permute-start | bytes 589832 | tf_op jit(solution)/shard_map/ppermute | solution.py:1189
  415.4 23.2 %collective-permute-start.36 = (bf16[1,256,256]{2,1,0:T(8,128)(2,1)S(1)}, bf16[1,256,256]{2,1,0:T(8,128)(2,1)S(1)}, u32[]{:S(2)}, u32[]{:S(2)}) collective-permute-start(bf16[1,256,256]{2,1,0:T(8,128)(2,1)S(1)} %copy-done.61), channel_id=1, source_target_pairs={{0,16},{2,18},{4,20},{6,22},{8,24},{10,26},{12,28},{14,30},{16,0},... | collective-permute-start | bytes 393224 | tf_op jit(solution)/shard_map/ppermute | solution.py:1189
  416.6 28.1 %collective-permute-start.33 = (bf16[1,80,2048]{2,1,0:T(8,128)(2,1)}, bf16[1,80,2048]{2,1,0:T(8,128)(2,1)S(1)}, u32[]{:S(2)}, u32[]{:S(2)}) collective-permute-start(bf16[1,80,2048]{2,1,0:T(8,128)(2,1)} %get-tuple-element.539), channel_id=1, source_target_pairs={{0,16},{2,18},{4,20},{6,22},{8,24},{10,26},{12,28},{14,30},{16,0},... | collective-permute-start | bytes 983048 | tf_op jit(solution)/shard_map/ppermute | solution.py:1189
  418.4 26.3 %collective-permute-start.34 = (bf16[2,64,1024]{2,1,0:T(8,128)(2,1)}, bf16[2,64,1024]{2,1,0:T(8,128)(2,1)S(1)}, u32[]{:S(2)}, u32[]{:S(2)}) collective-permute-start(bf16[2,64,1024]{2,1,0:T(8,128)(2,1)} %get-tuple-element.532.refs_7_), channel_id=1, source_target_pairs={{0,8},{2,10},{4,12},{6,14},{8,0},{10,2},{12,4},{14,6},{16,24},{18,... | collective-permute-start | bytes 786440 | tf_op jit(solution)/shard_map/ppermute | solution.py:1189
  439.5 34.2 %collective-permute-start.31 = (bf16[2,512,512]{2,1,0:T(8,128)(2,1)S(1)}, bf16[2,512,512]{2,1,0:T(8,128)(2,1)S(1)}, u32[]{:S(2)}, u32[]{:S(2)}) collective-permute-start(bf16[2,512,512]{2,1,0:T(8,128)(2,1)S(1)} %copy-done.21), channel_id=1, source_target_pairs={{0,1},{2,3},{4,5},{6,7},{8,9},{10,11},{12,13},{14,15},{16,17},{18,... | collective-permute-start | bytes 3145736 | tf_op jit(solution)/shard_map/ppermute | solution.py:1193
  441.2 23.8 %collective-permute-start.38 = (bf16[4,64,1024]{2,1,0:T(8,128)(2,1)}, bf16[4,64,1024]{2,1,0:T(8,128)(2,1)S(1)}, u32[]{:S(2)}, u32[]{:S(2)}) collective-permute-start(bf16[4,64,1024]{2,1,0:T(8,128)(2,1)} %get-tuple-element.549), channel_id=1, source_target_pairs={{0,4},{2,6},{4,0},{6,2},{8,12},{10,14},{12,8},{14,10},{16,20},{18,... | collective-permute-start | bytes 1572872 | tf_op jit(solution)/shard_map/ppermute | solution.py:1189
  457.3 19.5 %collective-permute-start.40 = (bf16[4,64,1024]{2,1,0:T(8,128)(2,1)}, bf16[4,64,1024]{2,1,0:T(8,128)(2,1)}, u32[]{:S(2)}, u32[]{:S(2)}) collective-permute-start(bf16[4,64,1024]{2,1,0:T(8,128)(2,1)} %get-tuple-element.560), channel_id=1, source_target_pairs={{0,4},{2,6},{4,0},{6,2},{8,12},{10,14},{12,8},{14,10},{16,20},{18,... | collective-permute-start | bytes 1572872 | tf_op jit(solution)/shard_map/ppermute | solution.py:1189
  (80 other events, 543.9 us)
